TPU v7x, 256 devices: a whole 4x4x8 slice. The times are simulated.
256 devices in a mesh: dp: 4 (over y_lo, core), seq: 32 (over z, x), tensor: 2 (over y_hi).
Axes of the slice: x: 4, y: 4 (y_hi: 2, y_lo: 2; y = y_hi * 2 + y_lo), z: 8, core: 2. Of those that a mesh axis runs over, the one named last changes fastest.
Arguments:
- lengths: int32 [4], P('dp'), may hold values from 3072 to 12288, as said below
- query_act: bfloat16 [4, 12288, 1024], P('dp', 'seq', 'tensor'), may hold values from -6 to 6
- key_act: bfloat16 [4, 12288, 1024], P('dp', 'seq', 'tensor'), may hold values from -6 to 6
- value_act: bfloat16 [4, 12288, 1024], P('dp', 'seq', 'tensor'), may hold values from -6 to 6
- conv_input: bfloat16 [4, 12288, 1024], P('dp', 'seq'), may hold values from -6 to 6
- conv_result: bfloat16 [4, 12288, 1024], P('dp', 'seq', 'tensor'), may hold values from -6 to 6
- out_grad: bfloat16 [4, 12288, 1024], P('dp', 'seq'), may hold values from -6 to 6
- out_weight: bfloat16 [1024, 1024], P('tensor'), may hold values from -0.1875 to 0.1875
- glu_weight: bfloat16 [2, 1024, 1024], P(None, None, 'tensor'), may hold values from -0.1875 to 0.1875
- conv_taps: bfloat16 [31, 1024], P(None, 'tensor'), may hold values from -1 to 1
- proj_weight: bfloat16 [1024, 1024], P('tensor'), may hold values from -0.1875 to 0.1875
Outputs:
- input_grad: bfloat16 [4, 12288, 1024], P('dp', 'seq')
- query_grad: bfloat16 [4, 12288, 1024], P('dp', 'seq', 'tensor')
- key_grad: bfloat16 [4, 12288, 1024], P('dp', 'seq', 'tensor')
- value_grad: bfloat16 [4, 12288, 1024], P('dp', 'seq', 'tensor')
- out_weight_grad: bfloat16 [1024, 1024], P('tensor', ('dp', 'seq'))
- glu_weight_grad: bfloat16 [2, 1024, 1024], P(None, ('dp', 'seq'), 'tensor')
- proj_weight_grad: bfloat16 [1024, 1024], P('tensor', ('dp', 'seq'))
Inputs may be any that keep to these rules, and one draw needn't show every extreme that they name: `lengths`: every length is at least 3072, and in every draw one recording has all 12288 frames valid.
All inputs are finite; a program needn't handle non-finite values.
Results may differ from a plain program's by a relative error of at most 0.013.
Values may be sent and summed in bfloat16 or wider, within the bound.
No kernel may reach another device: no remote copies, remote signals or barrier semaphores. Data moves between devices by JAX's collectives and lax.ppermute only.
A program may use at most 128 MiB of HBM per device.

v0:
```python
import jax
import jax.numpy as jnp
from jax import lax
from jax.sharding import PartitionSpec as P

HEAD_DIM = 64
WIN = 256


NEG_FILL = -1e30


def extended(shard, sides, width):
    for axis, dim in sides:
        peers, length = (lax.axis_size(axis), shard.shape[dim])
        up = [(i, (i + 1) % peers) for i in range(peers - 1)]
        down = [(j, i) for i, j in up]
        last = lax.slice_in_dim(shard, length - width, length, axis=dim)
        leading = lax.slice_in_dim(shard, 0, width, axis=dim)
        before = lax.ppermute(last, axis, up)
        after = lax.ppermute(leading, axis, down)
        shard = jnp.concatenate([before, shard, after], axis=dim)
    return shard


def from_behind(value, axis, steps):
    count = lax.axis_size(axis)
    leading, last = (max(0, -steps), min(count, count - steps))
    return lax.ppermute(value, axis, [(source, source + steps) for source in range(leading, last)])


def silu_slope(pre_act):
    logistic = jax.nn.sigmoid(pre_act)
    return logistic * (1.0 + pre_act * (1.0 - logistic))


def tap_sum(padded, conv_taps, frames):
    kernel = conv_taps.shape[0]
    summed = jnp.zeros((frames, padded.shape[1]), jnp.float32)
    for offset in range(kernel):
        start_row = kernel - 1 - offset
        summed = summed + conv_taps[offset].astype(jnp.float32) * padded[
            start_row : start_row + frames
        ].astype(jnp.float32)
    return summed


def head_grads(operands, q_pos, k_pos, length, query_mask):
    q_head, k_head, v_head, d_head = operands
    score_scale = q_head.shape[1] ** (-0.5)
    allowed = (
        (jnp.abs(q_pos[:, None] - k_pos[None, :]) <= WIN)
        & (k_pos[None, :] >= 0)
        & (k_pos[None, :] < length)
    )
    scores = jnp.dot(q_head, k_head.T, preferred_element_type=jnp.float32) * score_scale
    scores = jnp.where(allowed, scores, NEG_FILL)
    row_top = jnp.max(scores, axis=1, keepdims=True)
    exponent = jnp.exp(scores - row_top)
    attn_prob = exponent / jnp.sum(exponent, axis=1, keepdims=True)
    prob_low = attn_prob.astype(jnp.bfloat16)
    attended = jnp.dot(prob_low, v_head, preferred_element_type=jnp.float32) * query_mask[:, None]
    grad_prob = jnp.dot(d_head, v_head.T, preferred_element_type=jnp.float32)
    row_delta = jnp.sum(attn_prob * grad_prob, axis=1, keepdims=True)
    grad_score = (attn_prob * (grad_prob - row_delta) * score_scale).astype(jnp.bfloat16)
    grad_query = jnp.dot(grad_score, k_head, preferred_element_type=jnp.float32).astype(
        jnp.bfloat16
    )
    grad_key = jnp.dot(grad_score.T, q_head, preferred_element_type=jnp.float32)
    grad_value = jnp.dot(prob_low.T, d_head, preferred_element_type=jnp.float32)
    return (grad_query, grad_key, grad_value, attended.astype(jnp.bfloat16))


def attend(q_rows, kv_rows, d_rows, q_pos, k_pos, length):
    frames, head_cols = q_rows.shape
    key_span = kv_rows.shape[0]
    heads = head_cols // HEAD_DIM
    query_mask = (q_pos < length).astype(jnp.float32)

    def split_heads(values, rows):
        return values.reshape(rows, heads, HEAD_DIM).transpose(1, 0, 2)

    def one_head(operands):
        return head_grads(operands, q_pos, k_pos, length, query_mask)

    results = lax.map(
        one_head,
        (
            split_heads(q_rows, frames),
            split_heads(kv_rows[:, :head_cols], key_span),
            split_heads(kv_rows[:, head_cols:], key_span),
            split_heads(d_rows, frames),
        ),
    )

    def join_heads(values):
        return values.transpose(1, 0, 2).reshape(values.shape[1], head_cols)

    grad_query, grad_key, grad_value, attended = [join_heads(stacked) for stacked in results]
    return (grad_query, jnp.concatenate([grad_key, grad_value], axis=1), attended)


def reduce_weights(terms):
    return lax.psum_scatter(terms, ("dp", "seq"), scatter_dimension=1, tiled=True)


def unpack_conv(summed_rows, local_cols):
    glu_part = (
        summed_rows[: 2 * local_cols]
        .reshape(2, local_cols, summed_rows.shape[1])
        .transpose(0, 2, 1)
    )
    return (glu_part, summed_rows[2 * local_cols :])


def local(
    lengths,
    query_act,
    key_act,
    value_act,
    conv_input,
    conv_result,
    out_grad,
    out_weight,
    glu_weight,
    conv_taps,
    proj_weight,
):
    length = lengths[0]
    q_rows = query_act[0]
    frames, head_cols = q_rows.shape
    first_frame = lax.axis_index("seq") * frames
    positions = first_frame + jnp.arange(frames, dtype=jnp.int32)
    frame_mask = (positions < length).astype(jnp.float32)
    kv_ext = extended(jnp.concatenate([key_act[0], value_act[0]], axis=1), (("seq", 0),), WIN)
    resid_rows = conv_input[0]
    out_rows = out_grad[0]
    pre_float = conv_result[0].astype(jnp.float32)
    activated = jax.nn.silu(pre_float).astype(jnp.bfloat16)
    grad_act = jnp.dot(out_rows, proj_weight.T, preferred_element_type=jnp.float32)
    grad_pre = (grad_act * silu_slope(pre_float)).astype(jnp.bfloat16)
    half_width = (conv_taps.shape[0] - 1) // 2
    padded = extended(grad_pre, (("seq", 0),), half_width)
    grad_conv = tap_sum(padded, conv_taps, frames) * frame_mask[:, None]
    value_half = jnp.dot(resid_rows, glu_weight[0], preferred_element_type=jnp.float32)
    gate_half = jnp.dot(resid_rows, glu_weight[1], preferred_element_type=jnp.float32)
    logistic = jax.nn.sigmoid(gate_half)
    grad_glu = jnp.stack(
        [grad_conv * logistic, grad_conv * value_half * logistic * (1.0 - logistic)]
    ).astype(jnp.bfloat16)
    local_cols = grad_glu.shape[2]
    partial_grad = lax.dot_general(
        grad_glu, glu_weight, (((0, 2), (0, 2)), ((), ())), preferred_element_type=jnp.float32
    )
    glu_rows = jnp.einsum(
        "fd,hfc->hcd", resid_rows, grad_glu, preferred_element_type=jnp.float32
    ).reshape(2 * local_cols, resid_rows.shape[1])
    proj_term = jnp.dot(activated.T, out_rows, preferred_element_type=jnp.float32)
    grad_resid = out_rows.astype(jnp.float32) + lax.psum(partial_grad, "tensor")
    resid_low = grad_resid.astype(jnp.bfloat16)
    grad_attn = (
        jnp.dot(resid_low, out_weight.T, preferred_element_type=jnp.float32) * frame_mask[:, None]
    ).astype(jnp.bfloat16)
    key_span = kv_ext.shape[0]
    k_pos = first_frame - WIN + jnp.arange(key_span, dtype=jnp.int32)
    operands = (q_rows, kv_ext, grad_attn)
    grad_query, grad_kv, attended = attend(
        operands[0], operands[1], operands[2], positions, k_pos, length
    )
    summed = grad_kv[WIN : WIN + frames]
    tail_rows = frames - WIN
    for offset, edge_rows in ((-1, grad_kv[:WIN]), (1, grad_kv[WIN + frames :])):
        arrived = from_behind(edge_rows.astype(jnp.bfloat16), "seq", offset).astype(edge_rows.dtype)
        if offset < 0:
            summed = summed + jnp.pad(arrived, ((tail_rows, 0), (0, 0)))
        else:
            summed = summed + jnp.pad(arrived, ((0, tail_rows), (0, 0)))
    out_term = jnp.dot(attended.T, resid_low, preferred_element_type=jnp.float32)
    joined = reduce_weights(jnp.concatenate([out_term, glu_rows, proj_term], axis=0))
    out_sum = joined[:head_cols]
    glu_sum, proj_sum = unpack_conv(joined[head_cols:], local_cols)
    return (
        resid_low[None],
        grad_query[None],
        summed[:, :head_cols].astype(jnp.bfloat16)[None],
        summed[:, head_cols:].astype(jnp.bfloat16)[None],
        out_sum.astype(jnp.bfloat16),
        glu_sum.astype(jnp.bfloat16),
        proj_sum.astype(jnp.bfloat16),
    )


def solution(mesh):
    in_specs = (
        P("dp"),
        P("dp", "seq", "tensor"),
        P("dp", "seq", "tensor"),
        P("dp", "seq", "tensor"),
        P("dp", "seq", None),
        P("dp", "seq", "tensor"),
        P("dp", "seq", None),
        P("tensor", None),
        P(None, None, "tensor"),
        P(None, "tensor"),
        P("tensor", None),
    )
    out_specs = (
        P("dp", "seq", None),
        P("dp", "seq", "tensor"),
        P("dp", "seq", "tensor"),
        P("dp", "seq", "tensor"),
        P("tensor", ("dp", "seq")),
        P(None, ("dp", "seq"), "tensor"),
        P("tensor", ("dp", "seq")),
    )
    return jax.shard_map(local, mesh=mesh, in_specs=in_specs, out_specs=out_specs, check_vma=False)
```

profile of v0, /device:TPU:32, one launch (start us, length us, event | category | flops | bytes accessed | tf_op | source)
XLA Modules:
  0.0 798.3 jit_solution(5807780133396398045)
XLA Ops:
  8.4 2.0 fusion.58
  10.4 4.2 collective-permute-start
  14.6 1.9 collective-permute-start.1
  17.3 2.1 fusion.56
  19.4 3.0 collective-permute-done.1
  22.3 6.0 fusion.85
  29.8 2.3 convolution_bitcast_fusion.2
  34.7 1.9 collective-permute-start.2
  36.6 6.2 collective-permute-start.3
  42.8 3.1 fusion.80
  46.0 1.9 copy.40
  47.9 2.1 fusion.84
  49.9 2.3 copy.48
  52.2 4.6 fusion.76
  59.6 38.7 %all-reduce.4.cloned.1.call-done = f32[384,1024]{1,0:T(8,128)} async-done(((f32[384,1024]{1,0:T(8,128)}), f32[384,1024]{1,0:T(8,128)}) %all-reduce.4.cloned.1.call-update) | async-done | bytes 1572880 | tf_op jit(solution)/shard_map/psum | solution.py:159
  98.3 1.9 add_convert_fusion
  102.5 1.9 copy.43
  104.4 94.9 %while.18 = (s32[]{:T(128)}, bf16[8,384,64]{1,2,0:T(8,128)(2,1)}, f32[8,896,64]{1,2,0:T(8,128)}, f32[8,896,64]{1,2,0:T(8,128)S(1)}, bf16[8,384,64]{1,2,0:T(8,128...) while((s32[]{:T(128)}, bf16[8,384,64]{1,2,0:T(8,128)(2,1)}, ...), condition=%wide.region_5.6_spmd.clone.clone, body=%wide.region_1.5_spmd.clone.clone.sunk | while | flops 273264512 | bytes 14332573 | solution.py:86
  111.4 1.9 fusion.161
  123.2 1.9 fusion.161
  158.8 1.9 fusion.161
  170.7 1.9 fusion.161
  182.6 1.9 fusion.161
  199.4 2.0 fusion.125
  201.4 5.3 pad_maximum_fusion
  206.7 9.3 %copy.55 = f32[2048,1024]{0,1:T(8,128)} copy(f32[2048,1024]{1,0:T(8,128)} %pad_maximum_fusion) | data formatting | bytes 16777216
  218.6 4.5 collective-permute-start.4
  223.1 1.9 collective-permute-start.5
  225.0 1.9 copy.50
  226.9 9.7 %collective-permute-done.4 = bf16[256,1024]{0,1:T(8,128)(2,1)} collective-permute-done((bf16[256,1024]{0,1:T(8,128)(2,1)}, bf16[256,1024]{0,1:T(8,128)(2,1)}, u32[]{:S(2)}, u32[]{:S(2)}) %collective-permute-start.4) | collective-permute-done | bytes 524320 | tf_op jit(solution)/shard_map/ppermute | solution.py:29
  236.6 6.9 collective-permute-done.5
  247.1 541.1 %reduce-scatter.4.cloned.1.call-done = f32[8,2048]{1,0:T(8,128)} async-done(((f32[1024,2048]{1,0:T(8,128)}), f32[8,2048]{1,0:T(8,128)}) %reduce-scatter.4.cloned.1.call-update) | async-done | bytes 65552
  (157 shorter events, 104.8 us)
Async XLA Ops:
  7.2 1.2 copy-start
  7.2 9.4 %copy-start.14 = (bf16[31,512]{1,0:T(8,128)(2,1)S(1)}, bf16[31,512]{1,0:T(8,128)(2,1)}, u32[]{:S(2)}) copy-start(bf16[31,512]{1,0:T(8,128)(2,1)} %param.22) | copy-start | bytes 95236
  7.2 10.1 %copy-start.4 = (bf16[1,384,1024]{2,1,0:T(8,128)(2,1)S(1)}, bf16[1,384,1024]{2,1,0:T(8,128)(2,1)}, u32[]{:S(2)}) copy-start(bf16[1,384,1024]{2,1,0:T(8,128)(2,1)} %param.17) | copy-start | bytes 2359300
  7.2 91.1 %all-reduce.4.cloned.1.call-start = ((), (), s32[]{:S(2)}) async-start(), calls=%async_computation.1 | async-start | bytes 3145728 | tf_op jit(solution)/shard_map/psum | solution.py:159
  10.4 9.0 %collective-permute-start = (bf16[15,512]{1,0:T(8,128)(2,1)S(1)}, bf16[15,512]{1,0:T(8,128)(2,1)S(1)}, u32[]{:S(2)}, u32[]{:S(2)}) collective-permute-start(bf16[15,512]{1,0:T(8,128)(2,1)S(1)} %get-tuple-element.236), channel_id=1, source_target_pairs={{2,0},{4,2},{6,4},{8,6},{10,8},{12,10},{14,12},{16,14},{18,16},{20... | collective-permute-start | bytes 46088 | tf_op jit(solution)/shard_map/ppermute | solution.py:21
  14.6 7.7 collective-permute-start.1
  17.3 11.1 %copy-start.10 = (bf16[2,1024,512]{2,1,0:T(8,128)(2,1)S(1)}, bf16[2,1024,512]{2,1,0:T(8,128)(2,1)}, u32[]{:S(2)}) copy-start(bf16[2,1024,512]{2,1,0:T(8,128)(2,1)} %param.21) | copy-start | bytes 6291460
  19.3 9.1 %copy-start.5 = (bf16[1,384,1024]{2,1,0:T(8,128)(2,1)S(1)}, bf16[1,384,1024]{2,1,0:T(8,128)(2,1)}, u32[]{:S(2)}) copy-start(bf16[1,384,1024]{2,1,0:T(8,128)(2,1)} %param.17) | copy-start | bytes 2359300
  28.4 0.8 copy-start.7
  29.0 0.8 copy-start.8
  32.1 1.0 copy-start.12
  32.1 1.2 copy-start.13
  32.1 10.7 %copy-start.9 = (bf16[1,384,1024]{2,1,0:T(8,128)(2,1)S(1)}, bf16[1,384,1024]{2,1,0:T(8,128)(2,1)}, u32[]{:S(2)}) copy-start(bf16[1,384,1024]{2,1,0:T(8,128)(2,1)} %param.19) | copy-start | bytes 2359300
  32.1 756.1 %reduce-scatter.4.cloned.1.call-start = ((), (), s32[]{:S(2)}) async-start(), calls=%async_computation.2 | async-start | bytes 8454144
  33.5 12.4 %copy-start.1 = (bf16[1,384,512]{1,2,0:T(8,128)(2,1)}, bf16[1,384,512]{1,2,0:T(8,128)(2,1)S(1)}, u32[]{:S(2)}) copy-start(bf16[1,384,512]{1,2,0:T(8,128)(2,1)S(1)} %copy.42) | copy-start | bytes 1179652
  34.7 22.2 %collective-permute-start.2 = (bf16[256,1024]{0,1:T(8,128)(2,1)}, bf16[256,1024]{0,1:T(8,128)(2,1)}, u32[]{:S(2)}, u32[]{:S(2)}) collective-permute-start(bf16[256,1024]{0,1:T(8,128)(2,1)} %get-tuple-element.232), channel_id=1, source_target_pairs={{0,2},{2,4},{4,6},{6,8},{8,10},{10,12},{12,14},{14,16},{16,18},{18... | collective-permute-start | bytes 1572872 | tf_op jit(solution)/shard_map/ppermute | solution.py:20
  36.6 20.3 %collective-permute-start.3 = (bf16[256,1024]{0,1:T(8,128)(2,1)}, bf16[256,1024]{0,1:T(8,128)(2,1)}, u32[]{:S(2)}, u32[]{:S(2)}) collective-permute-start(bf16[256,1024]{0,1:T(8,128)(2,1)} %get-tuple-element.233), channel_id=1, source_target_pairs={{2,0},{4,2},{6,4},{8,6},{10,8},{12,10},{14,12},{16,14},{18,16},{20... | collective-permute-start | bytes 1572872 | tf_op jit(solution)/shard_map/ppermute | solution.py:21
  52.2 4.6 copy-start.2
  98.3 2.8 copy-start.15
  100.3 0.9 copy-start.3
  101.2 3.3 copy-start.11
  199.4 2.0 copy-start.6
  218.6 18.1 %collective-permute-start.4 = (bf16[256,1024]{0,1:T(8,128)(2,1)}, bf16[256,1024]{0,1:T(8,128)(2,1)}, u32[]{:S(2)}, u32[]{:S(2)}) collective-permute-start(bf16[256,1024]{0,1:T(8,128)(2,1)} %get-tuple-element.226), channel_id=1, source_target_pairs={{2,0},{4,2},{6,4},{8,6},{10,8},{12,10},{14,12},{16,14},{18,16},{20... | collective-permute-start | bytes 1572872 | tf_op jit(solution)/shard_map/ppermute | solution.py:29
  223.1 20.5 %collective-permute-start.5 = (bf16[256,1024]{0,1:T(8,128)(2,1)S(1)}, bf16[256,1024]{0,1:T(8,128)(2,1)}, u32[]{:S(2)}, u32[]{:S(2)}) collective-permute-start(bf16[256,1024]{0,1:T(8,128)(2,1)S(1)} %get-tuple-element.227), channel_id=1, source_target_pairs={{0,2},{2,4},{4,6},{6,8},{8,10},{10,12},{12,14},{14,16},{16,18},{18... | collective-permute-start | bytes 1572872 | tf_op jit(solution)/shard_map/ppermute | solution.py:29
Sparse Core Ops, SparseCore 0:
  32.2 66.0 all-reduce.3
  216.1 572.0 reduce-scatter.3
where the time goes:
time: 807 us; the launch traced here: 798 us
  waiting for transfers between devices  599 us (74%)
  matrix products  95.2 us (12%)
  other arithmetic  38.7 us (5%)
  local copies, waits for them, and re-layouts  28.9 us (4%)
  starting transfers between devices  20.7 us (3%)
  between operations  15 us (2%)
    unnamed x3, waiting for transfers between devices  541 us
    psum x1, waiting for transfers between devices, local(): grad_resid = out_rows.astype(jnp.float32) + lax.psum(partial_grad, 'tensor')  38.7 us
    unnamed x42, local copies, waits for them, and re-layouts  21.6 us
    ppermute x2, waiting for transfers between devices, from_behind(): lax.ppermute(value, axis, [(source, source + steps) for source in range(l...  16.6 us
  transfers between devices with their start and end apart: 8, of which 5 were waited for; matrix products, arithmetic and copies ran while one was open for 4% of the time, Pallas kernels for 0%

commit v1 on v0

--- a/solution.py
+++ b/solution.py
@@ -100,17 +100,29 @@
     return (grad_query, jnp.concatenate([grad_key, grad_value], axis=1), attended)
 
 
+def swapped(value, axis, stride):
+    count = lax.axis_size(axis)
+    return lax.ppermute(value, axis, [(i, i ^ stride) for i in range(count)])
+
+
+def halved(value, bit, axis, stride):
+    half = value.shape[0] // 2
+    mine = lax.dynamic_slice_in_dim(value, bit * half, half, axis=0)
+    other = lax.dynamic_slice_in_dim(value, (1 - bit) * half, half, axis=0)
+    arrived = swapped(other.astype(jnp.bfloat16), axis, stride)
+    return (mine.astype(jnp.float32) + arrived.astype(jnp.float32)).astype(jnp.bfloat16)
+
+
 def reduce_weights(terms):
-    return lax.psum_scatter(terms, ("dp", "seq"), scatter_dimension=1, tiled=True)
-
-
-def unpack_conv(summed_rows, local_cols):
-    glu_part = (
-        summed_rows[: 2 * local_cols]
-        .reshape(2, local_cols, summed_rows.shape[1])
-        .transpose(0, 2, 1)
-    )
-    return (glu_part, summed_rows[2 * local_cols :])
+    place = lax.axis_index("dp")
+    core, y_lo = (place % 2, place // 2)
+    rows, cols = terms.shape
+    by_core = terms.reshape(2, 2, rows // 4, cols).transpose(1, 0, 2, 3)
+    on_chip = halved(by_core, core, "dp", 1)[0]
+    on_pair = halved(on_chip, y_lo, "dp", 2)[0]
+    peers = lax.axis_size("seq")
+    arrived = lax.all_to_all(on_pair.reshape(peers, rows // 4 // peers, cols), "seq", 0, 0)
+    return jnp.sum(arrived.astype(jnp.float32), axis=0)
 
 
 def local(
@@ -153,10 +165,13 @@
         grad_glu, glu_weight, (((0, 2), (0, 2)), ((), ())), preferred_element_type=jnp.float32
     )
     glu_rows = jnp.einsum(
-        "fd,hfc->hcd", resid_rows, grad_glu, preferred_element_type=jnp.float32
-    ).reshape(2 * local_cols, resid_rows.shape[1])
-    proj_term = jnp.dot(activated.T, out_rows, preferred_element_type=jnp.float32)
-    grad_resid = out_rows.astype(jnp.float32) + lax.psum(partial_grad, "tensor")
+        "fd,hfc->dhc", resid_rows, grad_glu, preferred_element_type=jnp.float32
+    ).reshape(resid_rows.shape[1], 2 * local_cols)
+    proj_term = jnp.dot(out_rows.T, activated, preferred_element_type=jnp.float32)
+    own_grad = partial_grad.astype(jnp.bfloat16)
+    other_grad = swapped(own_grad, "tensor", 1)
+    channel_sum = own_grad.astype(jnp.float32) + other_grad.astype(jnp.float32)
+    grad_resid = out_rows.astype(jnp.float32) + channel_sum
     resid_low = grad_resid.astype(jnp.bfloat16)
     grad_attn = (
         jnp.dot(resid_low, out_weight.T, preferred_element_type=jnp.float32) * frame_mask[:, None]
@@ -175,10 +190,11 @@
             summed = summed + jnp.pad(arrived, ((tail_rows, 0), (0, 0)))
         else:
             summed = summed + jnp.pad(arrived, ((0, tail_rows), (0, 0)))
-    out_term = jnp.dot(attended.T, resid_low, preferred_element_type=jnp.float32)
-    joined = reduce_weights(jnp.concatenate([out_term, glu_rows, proj_term], axis=0))
-    out_sum = joined[:head_cols]
-    glu_sum, proj_sum = unpack_conv(joined[head_cols:], local_cols)
+    out_term = jnp.dot(resid_low.T, attended, preferred_element_type=jnp.float32)
+    joined = reduce_weights(jnp.concatenate([out_term, glu_rows, proj_term], axis=1))
+    out_sum = joined[:, :head_cols].T
+    glu_sum = joined[:, head_cols : 3 * head_cols].reshape(-1, 2, local_cols).transpose(1, 0, 2)
+    proj_sum = joined[:, 3 * head_cols :].T
     return (
         resid_low[None],
         grad_query[None],

time: 807 us -> 251 us (0.31)
  waiting for transfers between devices: 599 us -> 53.5 us
  matrix products: 95.2 us -> 69.3 us
  starting transfers between devices: 20.7 us -> 37.3 us
  between operations: 15 us -> 1.85 us
  other arithmetic: 38.7 us -> 51.3 us
    unnamed x3 -> x0, waiting for transfers between devices: 541 us -> none
    psum x1 -> x0, waiting for transfers between devices: 38.7 us -> none  [local(): grad_resid = out_rows.astype(jnp.float32) + lax.psum(partial_grad, 'tensor')]
    ppermute x0 -> x3, waiting for transfers between devices: none -> 28.9 us  [swapped(): return lax.ppermute(value, axis, [(i, i ^ stride) for i in range(count)])]
    concatenate x0 -> x4, local copies, waits for them, and re-layouts: none -> 19.8 us  [local(): jnp.concatenate([out_term, glu_rows, proj_term], axis=1)]
    all_to_all x0 -> x1, starting transfers between devices: none -> 11.1 us  [reduce_weights(): lax.all_to_all(on_pair.reshape(peers, rows // 4 // peers, cols), 'seq', 0...]
    unnamed x42 -> x50, local copies, waits for them, and re-layouts: 21.6 us -> 11 us
    another operation x1, other arithmetic: 6.04 us -> 16.4 us  [local(): jnp.stack([grad_conv * logistic, grad_conv * value_half * logistic * (1.0...]
  transfers between devices with their start and end apart: 8 -> 10, of which waited for: 5 -> 3; matrix products, arithmetic and copies ran while one was open for 4% -> 23% of each run, Pallas kernels for 0% -> 0%
where the time goes in v1:
time: 251 us; the launch traced here: 249 us
  matrix products  69.3 us (28%)
  waiting for transfers between devices  53.5 us (21%)
  other arithmetic  51.3 us (20%)
  starting transfers between devices  37.3 us (15%)
  local copies, waits for them, and re-layouts  35.1 us (14%)
    ppermute x3, waiting for transfers between devices, swapped(): return lax.ppermute(value, axis, [(i, i ^ stride) for i in range(count)])  28.9 us
    ppermute x2, waiting for transfers between devices, from_behind(): lax.ppermute(value, axis, [(source, source + steps) for source in range(l...  24.6 us
    concatenate x4, local copies, waits for them, and re-layouts, local(): jnp.concatenate([out_term, glu_rows, proj_term], axis=1)  19.8 us
    dot_general x8, matrix products, head_grads(): grad_value = jnp.dot(prob_low.T, d_head, preferred_element_type=jnp.float32)  16.7 us
    another operation x1, other arithmetic, local(): jnp.stack([grad_conv * logistic, grad_conv * value_half * logistic * (1.0...  16.4 us
    dot_general x8, matrix products, head_grads(): grad_prob = jnp.dot(d_head, v_head.T, preferred_element_type=jnp.float32)  11.3 us
    all_to_all x1, starting transfers between devices, reduce_weights(): lax.all_to_all(on_pair.reshape(peers, rows // 4 // peers, cols), 'seq', 0...  11.1 us
    unnamed x50, local copies, waits for them, and re-layouts  11 us
  transfers between devices with their start and end apart: 10, of which 3 were waited for; matrix products, arithmetic and copies ran while one was open for 23% of the time, Pallas kernels for 0%

profile of v1, /device:TPU:32, one launch (start us, length us, event | category | flops | bytes accessed | tf_op | source)
XLA Modules:
  0.0 248.8 jit_solution(15412719863046815107)
XLA Ops:
  3.9 3.5 %collective-permute-start.1 = (bf16[15,512]{1,0:T(8,128)(2,1)S(1)}, bf16[15,512]{1,0:T(8,128)(2,1)S(1)}, u32[]{:S(2)}, u32[]{:S(2)}) collective-permute-start(bf16[15,512]{1,0:T(8,128)(2,1)S(1)} %get-tuple-element.209), channel_id=1, source_target_pairs={{0,2},{2,4},{4,6},{6,8},{8,10},{10,12},{12,14},{14,16},{16,18},{18... | collective-permute-start | bytes 46088 | tf_op jit(solution)/shard_map/ppermute | solution.py:20
  7.4 4.6 %collective-permute-start = (bf16[15,512]{1,0:T(8,128)(2,1)S(1)}, bf16[15,512]{1,0:T(8,128)(2,1)S(1)}, u32[]{:S(2)}, u32[]{:S(2)}) collective-permute-start(bf16[15,512]{1,0:T(8,128)(2,1)S(1)} %get-tuple-element.208), channel_id=1, source_target_pairs={{2,0},{4,2},{6,4},{8,6},{10,8},{12,10},{14,12},{16,14},{18,16},{20... | collective-permute-start | bytes 46088 | tf_op jit(solution)/shard_map/ppermute | solution.py:21
  13.5 2.1 collective-permute-start.4
  15.6 3.7 %collective-permute-start.3 = (bf16[256,1024]{0,1:T(8,128)(2,1)}, bf16[256,1024]{0,1:T(8,128)(2,1)}, u32[]{:S(2)}, u32[]{:S(2)}) collective-permute-start(bf16[256,1024]{0,1:T(8,128)(2,1)} %get-tuple-element.206), channel_id=1, source_target_pairs={{0,2},{2,4},{4,6},{6,8},{8,10},{10,12},{12,14},{14,16},{16,18},{18... | collective-permute-start | bytes 1572872 | tf_op jit(solution)/shard_map/ppermute | solution.py:20
  19.5 2.1 convolution_bitcast_fusion.3
  22.3 2.8 %fusion.59 = f32[384,512]{1,0:T(8,128)} fusion(bf16[2,1024,512]{2,1,0:T(8,128)(2,1)} %param.21, bf16[1,384,1024]{2,1,0:T(8,128)(2,1)S(1)} %copy-done.7), kind=kOutput, calls=%fused_computation.110 | convolution fusion | flops 403243008 | bytes 2621440 | tf_op jit(solution)/shard_map/dot_general | solution.py:158
  25.4 3.0 %concatenate.58 = f32[2,2,256,512]{2,1,0,3:T(2,128)S(1)} reshape(f32[1024,512]{0,1:T(8,128)} %convolution_bitcast_fusion.3) | data formatting | bytes 4194304 | tf_op jit(solution)/shard_map/concatenate | solution.py:194
  28.4 2.8 %copy.39 = f32[2,2,256,512]{3,2,0,1:T(8,128)} copy(f32[2,2,256,512]{2,1,0,3:T(2,128)S(1)} %concatenate.58) | data formatting | bytes 4194304 | tf_op jit(solution)/shard_map/concatenate | solution.py:194
  31.3 16.4 %fusion.88 = (bf16[1,384,512]{2,1,0:T(8,128)(2,1)S(1)}, f32[384,512]{1,0:T(8,128)S(1)}) fusion(f32[384,512]{1,0:T(8,128)} %fusion.59, f32[384]{0:T(512)S(1)} %fusion.120, bf16[384,512]{1,0:T(8,128)(2,1)} %copy-done.16, bf16[15,512]{1,0:T(8,128)(2,1)S(1)} %collective-permute-done.1, f32[512]{0:T(512)S(1)} %bitcast.262, f32[512]{0:T(512)S(1)} %bitcast.263, ...), kind=kLoop, calls=%fused_computation.149 | loop fusion | flops 36372480 | bytes 2455040 | tf_op jit(solution)/shard_map/stack | solution.py:160
  50.7 3.5 %collective-permute-start.2 = (bf16[384,1024]{1,0:T(8,128)(2,1)S(1)}, bf16[384,1024]{1,0:T(8,128)(2,1)}, u32[]{:S(2)}, u32[]{:S(2)}) collective-permute-start(bf16[384,1024]{1,0:T(8,128)(2,1)S(1)} %bitcast_convert_fusion), channel_id=1, source_target_pairs={{0,1},{1,0},{2,3},{3,2},{4,5},{5,4},{6,7},{7,6},{8,9},{9,8},{10,11... | collective-permute-start | bytes 2359304 | tf_op jit(solution)/shard_map/ppermute | solution.py:105
  54.2 3.3 %convolution_bitcast_fusion.2 = f32[1024,2,512]{0,2,1:T(8,128)} fusion(bf16[1,384,1024]{2,1,0:T(8,128)(2,1)S(1)} %copy-done.8, bf16[1,384,512]{2,1,0:T(8,128)(2,1)S(1)} %fusion.63, bf16[1,384,512]{2,1,0:T(8,128)(2,1)S(1)} %get-tuple-element.192), kind=kOutput, calls=%fused_computation.90 | convolution fusion | flops 805699584 | bytes 5767168 | tf_op jit(solution)/shard_map/fd,hfc->dhc/dot_general | solution.py:167
  57.4 6.7 %concatenate.57 = f32[2,2,256,1024]{2,1,0,3:T(2,128)} reshape(f32[1024,2,512]{0,2,1:T(8,128)} %convolution_bitcast_fusion.2) | data formatting | bytes 8388608 | tf_op jit(solution)/shard_map/concatenate | solution.py:194
  64.1 7.3 %copy.38 = f32[2,2,256,1024]{3,2,0,1:T(8,128)} copy(f32[2,2,256,1024]{2,1,0,3:T(2,128)} %concatenate.57) | data formatting | bytes 8388608 | tf_op jit(solution)/shard_map/concatenate | solution.py:194
  79.1 72.1 %while.18 = (s32[]{:T(128)}, bf16[8,384,64]{1,2,0:T(8,128)(2,1)}, f32[8,896,64]{1,2,0:T(8,128)}, f32[8,896,64]{1,2,0:T(8,128)}, bf16[8,384,64]{1,2,0:T(8,128)(2,...) while((s32[]{:T(128)}, bf16[8,384,64]{1,2,0:T(8,128)(2,1)}, ...), condition=%wide.region_4.5_spmd.clone.clone, body=%wide.region_0.4_spmd.clone.clone.sunk | while | flops 273264512 | bytes 21673940 | solution.py:86
  84.8 2.1 fusion.163
  93.8 2.1 fusion.163
  102.8 2.1 fusion.163
  111.8 2.1 fusion.163
  120.8 2.1 fusion.163
  129.8 2.1 fusion.163
  138.9 2.1 fusion.163
  147.9 2.1 fusion.163
  153.2 2.6 %pad_maximum_fusion = f32[2,2,256,2048]{3,2,0,1:T(8,128)S(1)} fusion(f32[2,2,256,512]{3,2,0,1:T(8,128)S(1)} %copy-done.3, f32[2,2,256,1024]{3,2,0,1:T(8,128)} %copy.38, f32[2,2,256,512]{3,2,0,1:T(8,128)S(1)} %fusion.85), kind=kLoop, calls=%fused_computation.54 | loop fusion | flops 4194304 | bytes 16777216 | tf_op jit(solution)/shard_map/concatenate | solution.py:194
  155.7 3.3 %copy-done.2 = f32[2,2,256,2048]{3,2,0,1:T(8,128)} copy-done((f32[2,2,256,2048]{3,2,0,1:T(8,128)}, f32[2,2,256,2048]{3,2,0,1:T(8,128)S(1)}, u32[]{:S(2)}) %copy-start.2) | copy-done | bytes 8388632
  159.4 4.2 %collective-permute-done.7 = bf16[1,2,256,2048]{3,2,1,0:T(8,128)(2,1)} collective-permute-done((bf16[1,2,256,2048]{3,2,1,0:T(8,128)(2,1)S(1)}, bf16[1,2,256,2048]{3,2,1,0:T(8,128)(2,1)}, u32[]{:S(2)}, u32[]{:S(2)}) %collective-permute-start.7) | collective-permute-done | bytes 2097184 | tf_op jit(solution)/shard_map/ppermute | solution.py:105
  163.7 3.5 %fusion.47 = bf16[1,2,256,2048]{3,2,1,0:T(8,128)(2,1)S(1)} fusion(bf16[1,2,256,2048]{3,2,1,0:T(8,128)(2,1)} %collective-permute-done.7, f32[2,2,256,2048]{3,2,0,1:T(8,128)} %copy-done.2, s32[]{:T(128)S(6)} %select_n.28), kind=kLoop, calls=%fused_computation.59 | loop fusion | flops 3145728 | bytes 8388612 | tf_op jit(solution)/shard_map/convert_element_type | solution.py:113
  168.0 24.6 %collective-permute-done.8 = bf16[1,256,2048]{2,1,0:T(8,128)(2,1)} collective-permute-done((bf16[1,256,2048]{2,1,0:T(8,128)(2,1)S(1)}, bf16[1,256,2048]{2,1,0:T(8,128)(2,1)}, u32[]{:S(2)}, u32[]{:S(2)}) %collective-permute-start.8) | collective-permute-done | bytes 1048608 | tf_op jit(solution)/shard_map/ppermute | solution.py:105
  192.7 2.6 %fusion.64 = bf16[32,8,2048]{2,1,0:T(8,128)(2,1)} fusion(bf16[1,256,2048]{2,1,0:T(8,128)(2,1)} %collective-permute-done.8, bf16[1,2,256,2048]{3,2,1,0:T(8,128)(2,1)S(1)} %fusion.47, s32[]{:T(128)S(6)} %select_n.31), kind=kLoop, calls=%fused_computation.118 | loop fusion | flops 2097152 | bytes 3145732 | tf_op jit(solution)/shard_map/reshape;squeeze | solution.py:124
  195.3 11.1 %all-to-all-start = ((bf16[32,8,2048]{2,1,0:T(8,128)(2,1)}), bf16[32,8,2048]{2,1,0:T(8,128)(2,1)}, u32[]{:S(2)}, u32[]{:S(2)}) async-start(bf16[32,8,2048]{2,1,0:T(8,128)(2,1)} %fusion.64), calls=%async_computation | async-start | bytes 2097152 | tf_op jit(solution)/shard_map/all_to_all | solution.py:124
  208.2 3.4 %collective-permute-start.6 = (bf16[256,1024]{0,1:T(8,128)(2,1)S(1)}, bf16[256,1024]{0,1:T(8,128)(2,1)S(1)}, u32[]{:S(2)}, u32[]{:S(2)}) collective-permute-start(bf16[256,1024]{0,1:T(8,128)(2,1)S(1)} %get-tuple-element.201), channel_id=1, source_target_pairs={{0,2},{2,4},{4,6},{6,8},{8,10},{10,12},{12,14},{14,16},{16,18},{18... | collective-permute-start | bytes 1572872 | tf_op jit(solution)/shard_map/ppermute | solution.py:29
  211.5 4.6 %collective-permute-start.5 = (bf16[256,1024]{0,1:T(8,128)(2,1)S(1)}, bf16[256,1024]{0,1:T(8,128)(2,1)}, u32[]{:S(2)}, u32[]{:S(2)}) collective-permute-start(bf16[256,1024]{0,1:T(8,128)(2,1)S(1)} %get-tuple-element.200), channel_id=1, source_target_pairs={{2,0},{4,2},{6,4},{8,6},{10,8},{12,10},{14,12},{16,14},{18,16},{20... | collective-permute-start | bytes 1572872 | tf_op jit(solution)/shard_map/ppermute | solution.py:29
  218.1 24.6 %collective-permute-done.6 = bf16[256,1024]{0,1:T(8,128)(2,1)S(1)} collective-permute-done((bf16[256,1024]{0,1:T(8,128)(2,1)S(1)}, bf16[256,1024]{0,1:T(8,128)(2,1)S(1)}, u32[]{:S(2)}, u32[]{:S(2)}) %collective-permute-start.6) | collective-permute-done | bytes 524320 | tf_op jit(solution)/shard_map/ppermute | solution.py:29
  (206 shorter events, 83.5 us)
Async XLA Ops:
  0.6 11.4 %copy-start.18 = (bf16[1,384,512]{2,1,0:T(8,128)(2,1)S(1)}, bf16[1,384,512]{2,1,0:T(8,128)(2,1)}, u32[]{:S(2)}) copy-start(bf16[1,384,512]{2,1,0:T(8,128)(2,1)} %param.15) | copy-start | bytes 1179652
  0.7 11.6 %copy-start.19 = (bf16[1,384,512]{2,1,0:T(8,128)(2,1)S(1)}, bf16[1,384,512]{2,1,0:T(8,128)(2,1)}, u32[]{:S(2)}) copy-start(bf16[1,384,512]{2,1,0:T(8,128)(2,1)} %param.16) | copy-start | bytes 1179652
  3.8 3.6 %copy-start.16 = (bf16[384,512]{1,0:T(8,128)(2,1)}, bf16[384,512]{1,0:T(8,128)(2,1)S(1)}, u32[]{:S(2)}) copy-start(bf16[384,512]{1,0:T(8,128)(2,1)S(1)} %fusion.61) | copy-start | bytes 1179652
  3.8 15.5 %copy-start.21 = (bf16[31,512]{1,0:T(8,128)(2,1)S(1)}, bf16[31,512]{1,0:T(8,128)(2,1)}, u32[]{:S(2)}) copy-start(bf16[31,512]{1,0:T(8,128)(2,1)} %param.22) | copy-start | bytes 95236
  3.9 15.6 %copy-start.11 = (bf16[1,384,1024]{2,1,0:T(8,128)(2,1)S(1)}, bf16[1,384,1024]{2,1,0:T(8,128)(2,1)}, u32[]{:S(2)}) copy-start(bf16[1,384,1024]{2,1,0:T(8,128)(2,1)} %param.19) | copy-start | bytes 2359300
  3.9 15.6 %copy-start.23 = (bf16[1,384,512]{2,1,0:T(8,128)(2,1)S(1)}, bf16[1,384,512]{2,1,0:T(8,128)(2,1)}, u32[]{:S(2)}) copy-start(bf16[1,384,512]{2,1,0:T(8,128)(2,1)} %param.18) | copy-start | bytes 1179652
  3.9 27.4 %collective-permute-start.1 = (bf16[15,512]{1,0:T(8,128)(2,1)S(1)}, bf16[15,512]{1,0:T(8,128)(2,1)S(1)}, u32[]{:S(2)}, u32[]{:S(2)}) collective-permute-start(bf16[15,512]{1,0:T(8,128)(2,1)S(1)} %get-tuple-element.209), channel_id=1, source_target_pairs={{0,2},{2,4},{4,6},{6,8},{8,10},{10,12},{12,14},{14,16},{16,18},{18... | collective-permute-start | bytes 46088 | tf_op jit(solution)/shard_map/ppermute | solution.py:20
  7.4 23.8 %collective-permute-start = (bf16[15,512]{1,0:T(8,128)(2,1)S(1)}, bf16[15,512]{1,0:T(8,128)(2,1)S(1)}, u32[]{:S(2)}, u32[]{:S(2)}) collective-permute-start(bf16[15,512]{1,0:T(8,128)(2,1)S(1)} %get-tuple-element.208), channel_id=1, source_target_pairs={{2,0},{4,2},{6,4},{8,6},{10,8},{12,10},{14,12},{16,14},{18,16},{20... | collective-permute-start | bytes 46088 | tf_op jit(solution)/shard_map/ppermute | solution.py:21
  13.5 57.9 %collective-permute-start.4 = (bf16[256,1024]{0,1:T(8,128)(2,1)}, bf16[256,1024]{0,1:T(8,128)(2,1)}, u32[]{:S(2)}, u32[]{:S(2)}) collective-permute-start(bf16[256,1024]{0,1:T(8,128)(2,1)} %get-tuple-element.207), channel_id=1, source_target_pairs={{2,0},{4,2},{6,4},{8,6},{10,8},{12,10},{14,12},{16,14},{18,16},{20... | collective-permute-start | bytes 1572872 | tf_op jit(solution)/shard_map/ppermute | solution.py:21
  15.6 55.8 %collective-permute-start.3 = (bf16[256,1024]{0,1:T(8,128)(2,1)}, bf16[256,1024]{0,1:T(8,128)(2,1)}, u32[]{:S(2)}, u32[]{:S(2)}) collective-permute-start(bf16[256,1024]{0,1:T(8,128)(2,1)} %get-tuple-element.206), channel_id=1, source_target_pairs={{0,2},{2,4},{4,6},{6,8},{8,10},{10,12},{12,14},{14,16},{16,18},{18... | collective-permute-start | bytes 1572872 | tf_op jit(solution)/shard_map/ppermute | solution.py:20
  19.5 2.8 %copy-start.7 = (bf16[1,384,1024]{2,1,0:T(8,128)(2,1)S(1)}, bf16[1,384,1024]{2,1,0:T(8,128)(2,1)}, u32[]{:S(2)}) copy-start(bf16[1,384,1024]{2,1,0:T(8,128)(2,1)} %param.17) | copy-start | bytes 2359300
  22.3 2.9 %copy-start.20 = (bf16[1,384,512]{2,1,0:T(8,128)(2,1)S(1)}, bf16[1,384,512]{2,1,0:T(8,128)(2,1)}, u32[]{:S(2)}) copy-start(bf16[1,384,512]{2,1,0:T(8,128)(2,1)} %param.14) | copy-start | bytes 1179652
  31.2 16.4 %copy-start.6 = (f32[384,512]{1,0:T(8,128)S(1)}, f32[384,512]{1,0:T(8,128)}, u32[]{:S(2)}) copy-start(f32[384,512]{1,0:T(8,128)} %fusion.59) | copy-start | bytes 2359300
  31.2 16.4 %copy-start.8 = (bf16[1,384,1024]{2,1,0:T(8,128)(2,1)S(1)}, bf16[1,384,1024]{2,1,0:T(8,128)(2,1)}, u32[]{:S(2)}) copy-start(bf16[1,384,1024]{2,1,0:T(8,128)(2,1)} %param.17) | copy-start | bytes 2359300
  50.7 6.7 %copy-start.13 = (bf16[384,1024]{1,0:T(8,128)(2,1)}, bf16[384,1024]{1,0:T(8,128)(2,1)S(1)}, u32[]{:S(2)}) copy-start(bf16[384,1024]{1,0:T(8,128)(2,1)S(1)} %bitcast_convert_fusion) | copy-start | bytes 2359300
  50.7 22.3 %collective-permute-start.2 = (bf16[384,1024]{1,0:T(8,128)(2,1)S(1)}, bf16[384,1024]{1,0:T(8,128)(2,1)}, u32[]{:S(2)}, u32[]{:S(2)}) collective-permute-start(bf16[384,1024]{1,0:T(8,128)(2,1)S(1)} %bitcast_convert_fusion), channel_id=1, source_target_pairs={{0,1},{1,0},{2,3},{3,2},{4,5},{5,4},{6,7},{7,6},{8,9},{9,8},{10,11... | collective-permute-start | bytes 2359304 | tf_op jit(solution)/shard_map/ppermute | solution.py:105
  73.0 2.8 %copy-start.22 = (bf16[512,1024]{1,0:T(8,128)(2,1)S(1)}, bf16[512,1024]{1,0:T(8,128)(2,1)}, u32[]{:S(2)}) copy-start(bf16[512,1024]{1,0:T(8,128)(2,1)} %param.20) | copy-start | bytes 3145732
  75.8 75.4 %copy-start.5 = (bf16[384,1024]{1,0:T(8,128)(2,1)}, bf16[384,1024]{1,0:T(8,128)(2,1)S(1)}, u32[]{:S(2)}) copy-start(bf16[384,1024]{1,0:T(8,128)(2,1)S(1)} %add_convert_fusion) | copy-start | bytes 2359300
  75.8 3.3 %copy-start.17 = (bf16[8,384,64]{1,2,0:T(8,128)(2,1)S(1)}, bf16[8,384,64]{1,2,0:T(8,128)(2,1)}, u32[]{:S(2)}) copy-start(bf16[8,384,64]{1,2,0:T(8,128)(2,1)} %custom-call.3) | copy-start | bytes 1179652
  84.8 2.8 %copy-start.10 = (bf16[8,896,64]{1,2,0:T(8,128)(2,1)S(1)}, bf16[8,896,64]{1,2,0:T(8,128)(2,1)}, u32[]{:S(2)}) copy-start(bf16[8,896,64]{1,2,0:T(8,128)(2,1)} %copy-done.9) | copy-start | bytes 2752516 | tf_op jit(solution)/shard_map/while
  93.8 2.8 %copy-start.10 = (bf16[8,896,64]{1,2,0:T(8,128)(2,1)S(1)}, bf16[8,896,64]{1,2,0:T(8,128)(2,1)}, u32[]{:S(2)}) copy-start(bf16[8,896,64]{1,2,0:T(8,128)(2,1)} %copy-done.9) | copy-start | bytes 2752516 | tf_op jit(solution)/shard_map/while
  102.8 2.8 %copy-start.10 = (bf16[8,896,64]{1,2,0:T(8,128)(2,1)S(1)}, bf16[8,896,64]{1,2,0:T(8,128)(2,1)}, u32[]{:S(2)}) copy-start(bf16[8,896,64]{1,2,0:T(8,128)(2,1)} %copy-done.9) | copy-start | bytes 2752516 | tf_op jit(solution)/shard_map/while
  120.8 2.7 %copy-start.10 = (bf16[8,896,64]{1,2,0:T(8,128)(2,1)S(1)}, bf16[8,896,64]{1,2,0:T(8,128)(2,1)}, u32[]{:S(2)}) copy-start(bf16[8,896,64]{1,2,0:T(8,128)(2,1)} %copy-done.9) | copy-start | bytes 2752516 | tf_op jit(solution)/shard_map/while
  129.8 2.8 %copy-start.10 = (bf16[8,896,64]{1,2,0:T(8,128)(2,1)S(1)}, bf16[8,896,64]{1,2,0:T(8,128)(2,1)}, u32[]{:S(2)}) copy-start(bf16[8,896,64]{1,2,0:T(8,128)(2,1)} %copy-done.9) | copy-start | bytes 2752516 | tf_op jit(solution)/shard_map/while
  155.7 3.3 %copy-start.2 = (f32[2,2,256,2048]{3,2,0,1:T(8,128)}, f32[2,2,256,2048]{3,2,0,1:T(8,128)S(1)}, u32[]{:S(2)}) copy-start(f32[2,2,256,2048]{3,2,0,1:T(8,128)S(1)} %pad_maximum_fusion) | copy-start | bytes 25165828
  159.3 4.4 %collective-permute-start.7 = (bf16[1,2,256,2048]{3,2,1,0:T(8,128)(2,1)S(1)}, bf16[1,2,256,2048]{3,2,1,0:T(8,128)(2,1)}, u32[]{:S(2)}, u32[]{:S(2)}) collective-permute-start(bf16[1,2,256,2048]{3,2,1,0:T(8,128)(2,1)S(1)} %fusion.49), channel_id=1, source_target_pairs={{0,64},{64,0},{128,192},{192,128},{1,65},{65,1},{129,193},{193,129... | collective-permute-start | bytes 6291464 | tf_op jit(solution)/shard_map/ppermute | solution.py:105
  167.3 25.4 %collective-permute-start.8 = (bf16[1,256,2048]{2,1,0:T(8,128)(2,1)S(1)}, bf16[1,256,2048]{2,1,0:T(8,128)(2,1)}, u32[]{:S(2)}, u32[]{:S(2)}) collective-permute-start(bf16[1,256,2048]{2,1,0:T(8,128)(2,1)S(1)} %dynamic-slice_bitcast_fusion), channel_id=1, source_target_pairs={{0,128},{64,192},{128,0},{192,64},{1,129},{65,193},{129,1},{193,65... | collective-permute-start | bytes 3145736 | tf_op jit(solution)/shard_map/ppermute | solution.py:105
  195.3 11.1 %copy-start.4 = (f32[8,896,64]{1,2,0:T(8,128)S(1)}, f32[8,896,64]{1,2,0:T(8,128)}, u32[]{:S(2)}) copy-start(f32[8,896,64]{1,2,0:T(8,128)} %get-tuple-element.78) | copy-start | bytes 5505028
  195.3 50.9 %all-to-all-start = ((bf16[32,8,2048]{2,1,0:T(8,128)(2,1)}), bf16[32,8,2048]{2,1,0:T(8,128)(2,1)}, u32[]{:S(2)}, u32[]{:S(2)}) async-start(bf16[32,8,2048]{2,1,0:T(8,128)(2,1)} %fusion.64), calls=%async_computation | async-start | bytes 2097152 | tf_op jit(solution)/shard_map/all_to_all | solution.py:124
  208.2 34.5 %collective-permute-start.6 = (bf16[256,1024]{0,1:T(8,128)(2,1)S(1)}, bf16[256,1024]{0,1:T(8,128)(2,1)S(1)}, u32[]{:S(2)}, u32[]{:S(2)}) collective-permute-start(bf16[256,1024]{0,1:T(8,128)(2,1)S(1)} %get-tuple-element.201), channel_id=1, source_target_pairs={{0,2},{2,4},{4,6},{6,8},{8,10},{10,12},{12,14},{14,16},{16,18},{18... | collective-permute-start | bytes 1572872 | tf_op jit(solution)/shard_map/ppermute | solution.py:29
  211.5 31.1 %collective-permute-start.5 = (bf16[256,1024]{0,1:T(8,128)(2,1)S(1)}, bf16[256,1024]{0,1:T(8,128)(2,1)}, u32[]{:S(2)}, u32[]{:S(2)}) collective-permute-start(bf16[256,1024]{0,1:T(8,128)(2,1)S(1)} %get-tuple-element.200), channel_id=1, source_target_pairs={{2,0},{4,2},{6,4},{8,6},{10,8},{12,10},{14,12},{16,14},{18,16},{20... | collective-permute-start | bytes 1572872 | tf_op jit(solution)/shard_map/ppermute | solution.py:29
  242.6 6.1 %copy-start.1 = (bf16[512,1024]{1,0:T(8,128)(2,1)S(1)}, bf16[512,1024]{1,0:T(8,128)(2,1)}, u32[]{:S(2)}) copy-start(bf16[512,1024]{1,0:T(8,128)(2,1)} %param.23) | copy-start | bytes 3145732
  (16 other events, 30.7 us)

commit v2 on v0

v2 whole, which is shorter than its diff:
```python
import functools

import jax
import jax.numpy as jnp
from jax import lax
from jax.experimental import pallas as pl
from jax.experimental.pallas import tpu as pltpu
from jax.sharding import PartitionSpec as P

HEAD_DIM = 64
WIN = 256


NEG_FILL = -1e30
FULL, LOW = jnp.float32, jnp.bfloat16
TAPS = 31
EDGE = 16
STRIP = 32
VMEM = pl.BlockSpec(memory_space=pltpu.VMEM)
SMEM = pl.BlockSpec(memory_space=pltpu.SMEM)


def shape(dims, kind=LOW):
    return jax.ShapeDtypeStruct(dims, kind)


def call(kernel, name, operands, in_specs, out_shape, out_specs=None, scratch=(), flops=0, moved=0, limit=24, **more):
    return pl.pallas_call(
        kernel,
        in_specs=in_specs,
        out_specs=[VMEM] * len(out_shape) if out_specs is None else out_specs,
        out_shape=out_shape,
        scratch_shapes=list(scratch),
        compiler_params=pltpu.CompilerParams(vmem_limit_bytes=limit * 2**20),
        cost_estimate=pl.CostEstimate(flops=flops, bytes_accessed=moved, transcendentals=0),
        name=name,
        **more,
    )(*operands)


def dot_nt(left, right):
    return lax.dot_general(left, right, (((1,), (1,)), ((), ())), preferred_element_type=FULL)


def dot_tn(left, right):
    return lax.dot_general(left, right, (((0,), (0,)), ((), ())), preferred_element_type=FULL)


def round_ring(value, steps):
    count = lax.axis_size("seq")
    return lax.ppermute(value, "seq", [(i, (i + steps) % count) for i in range(count)])


def swapped(value, axis, stride):
    count = lax.axis_size(axis)
    return lax.ppermute(value, axis, [(i, i ^ stride) for i in range(count)])


def pack_kernel(k_ref, v_ref, grad_ref, pre_ref, up_ref, down_ref):
    frames, cols = k_ref.shape
    for out_ref, start, edge in ((up_ref, frames - WIN, frames - EDGE), (down_ref, 0, 0)):
        out_ref[:WIN, :cols] = k_ref[start : start + WIN]
        out_ref[:WIN, cols:] = v_ref[start : start + WIN]
        out_ref[WIN : WIN + EDGE] = grad_ref[edge : edge + EDGE]
        out_ref[WIN + EDGE :, :cols] = pre_ref[edge : edge + EDGE]
        out_ref[WIN + EDGE :, cols:] = pre_ref[edge : edge + EDGE]


def pack(k_rows, v_rows, out_rows, pre_rows):
    dims = (WIN + 2 * EDGE, 2 * k_rows.shape[1])
    return call(pack_kernel, "pack", (k_rows, v_rows, out_rows, pre_rows), [VMEM] * 4, [shape(dims)] * 2, moved=2**21)


def pre_grad(out_rows, pre_rows, proj):
    pre = pre_rows.astype(FULL)
    logistic = jax.nn.sigmoid(pre)
    slope = logistic * (1.0 + pre * (1.0 - logistic))
    return (dot_nt(out_rows, proj) * slope).astype(LOW), (pre * logistic).astype(LOW)


def conv_strip(rows, taps):
    count = rows.shape[0] - 2 * EDGE
    total = jnp.zeros((count, rows.shape[1]), FULL)
    for shift in range(8):
        moved = rows[shift : shift + count + 24]
        for coarse in range(4):
            step = 8 * coarse + shift
            if step >= 1:
                total = total + taps[TAPS - step : TAPS - step + 1] * moved[8 * coarse : 8 * coarse + count]
    return total


def glu_grads(grad_conv, logistic, value):
    first = grad_conv * logistic
    return first.astype(LOW), (first * value * (1.0 - logistic)).astype(LOW)


def front_kernel(
    place, out_ref, pre_ref, proj_ref, input_ref, glu_w_ref, taps_ref,
    mid_ref, glu_ref, act_ref, rim_ref, rim_gate_ref, rim_value_ref,
    padded, taps, gates, values,
):
    frames, cols = pre_ref.shape
    first, length = place[0], place[1]
    inner = frames - EDGE
    taps[:TAPS] = taps_ref[...].astype(FULL)
    for part in range(0, cols, 256):
        span = slice(part, part + 256)
        grad_pre, activated = pre_grad(out_ref[...], pre_ref[:, span], proj_ref[span])
        act_ref[:, span] = activated
        padded[:, span] = grad_pre.astype(FULL)
        rim_ref[: 2 * EDGE, span] = grad_pre[: 2 * EDGE]
        rim_ref[2 * EDGE :, span] = grad_pre[frames - 2 * EDGE :]
        values[:, span] = jnp.dot(input_ref[...], glu_w_ref[0, :, span], preferred_element_type=FULL)
        gate_half = jnp.dot(input_ref[...], glu_w_ref[1, :, span], preferred_element_type=FULL)
        gates[:, span] = jax.nn.sigmoid(gate_half)
    for whole, rim in ((gates, rim_gate_ref), (values, rim_value_ref)):
        rim[:EDGE] = whole[:EDGE]
        rim[EDGE:] = whole[inner:]

    def strip(i, carry):
        at = pl.multiple_of(i * STRIP, STRIP)
        rows = pl.ds(pl.multiple_of(at + EDGE, EDGE), STRIP)
        frame = lax.broadcasted_iota(jnp.int32, (STRIP, 128), 0) + (first + EDGE + at)
        valid = frame < length
        for part in range(0, cols, 128):
            span = slice(part, part + 128)
            grad_conv = conv_strip(padded[pl.ds(at, STRIP + 2 * EDGE), span], taps[:, span])
            grad_conv = jnp.where(valid, grad_conv, 0.0)
            low = glu_grads(grad_conv, gates[rows, span], values[rows, span])
            glu_ref[rows, span] = low[0]
            glu_ref[rows, cols + part : cols + part + 128] = low[1]
        return carry

    lax.fori_loop(0, (frames - 2 * EDGE) // STRIP, strip, 0)
    for part in range(0, mid_ref.shape[1], 256):
        span = slice(part, part + 256)
        mid_ref[:, span] = (
            dot_nt(glu_ref[EDGE:inner, :cols], glu_w_ref[0, span])
            + dot_nt(glu_ref[EDGE:inner, cols:], glu_w_ref[1, span])
        ).astype(LOW)


def front(place, out_rows, pre_rows, proj, input_rows, glu_weight, taps):
    frames, cols = pre_rows.shape
    wide = input_rows.shape[1]
    return call(
        front_kernel, "front",
        (place, out_rows, pre_rows, proj, input_rows, glu_weight, taps),
        [SMEM] + [VMEM] * 6,
        [
            shape((frames - 2 * EDGE, wide)), shape((frames, 2 * cols)), shape((frames, cols)),
            shape((4 * EDGE, cols)), shape((2 * EDGE, cols), FULL), shape((2 * EDGE, cols), FULL),
        ],
        scratch=[
            pltpu.VMEM((frames, cols), FULL), pltpu.VMEM((32, cols), FULL),
            pltpu.VMEM((frames, cols), FULL), pltpu.VMEM((frames, cols), FULL),
        ],
        flops=10 * frames * cols * wide, moved=6 * 2**20,
    )


def rim_kernel(
    place, before_ref, after_ref, rim_ref, gate_ref, value_ref, proj_ref, glu_w_ref, taps_ref, glu_in_ref,
    part_ref, glu_ref,
):
    del glu_in_ref
    frames = glu_ref.shape[0]
    cols = rim_ref.shape[1]
    first, length, total = place[0], place[1], place[2]
    out_rows = jnp.concatenate([before_ref[:EDGE], after_ref[:EDGE]], axis=0)
    pre_rows = jnp.concatenate([before_ref[EDGE:, :cols], after_ref[EDGE:, :cols]], axis=0)
    arrived = pre_grad(out_rows, pre_rows, proj_ref[...])[0].astype(FULL)
    above = jnp.where(first > 0, arrived[:EDGE], 0.0)
    below = jnp.where(first + frames < total, arrived[EDGE:], 0.0)
    own = rim_ref[...].astype(FULL)
    taps = taps_ref[...].astype(FULL)
    pieces = []
    for rows, start, place_of in (
        (jnp.concatenate([above, own[: 2 * EDGE]], axis=0), 0, slice(0, EDGE)),
        (jnp.concatenate([own[2 * EDGE :], below], axis=0), frames - EDGE, slice(EDGE, 2 * EDGE)),
    ):
        lows = []
        for part in range(0, cols, 128):
            span = slice(part, part + 128)
            frame = lax.broadcasted_iota(jnp.int32, (EDGE, 128), 0) + (first + start)
            grad_conv = jnp.where(frame < length, conv_strip(rows[:, span], taps[:, span]), 0.0)
            lows.append(glu_grads(grad_conv, gate_ref[place_of, span], value_ref[place_of, span]))
        low = jnp.concatenate([pair[0] for pair in lows] + [pair[1] for pair in lows], axis=1)
        glu_ref[start : start + EDGE] = low
        pieces.append(low)
    low = jnp.concatenate(pieces, axis=0)
    part_ref[...] = (dot_nt(low[:, :cols], glu_w_ref[0]) + dot_nt(low[:, cols:], glu_w_ref[1])).astype(LOW)


def rim(place, before, after, rim_rows, gate, value, proj, glu_weight, taps, glu_low):
    edge = pl.BlockSpec((2 * EDGE, before.shape[1]), lambda i: (WIN // (2 * EDGE), 0))
    whole = lambda array: pl.BlockSpec(array.shape, lambda i: (0,) * array.ndim)
    wide = glu_weight.shape[1]
    return call(
        rim_kernel, "rim",
        (place, before, after, rim_rows, gate, value, proj, glu_weight, taps, glu_low),
        [SMEM, edge, edge, whole(rim_rows), whole(gate), whole(value), VMEM, VMEM, whole(taps), VMEM],
        [shape((2 * EDGE, wide)), shape(glu_low.shape)],
        out_specs=[pl.BlockSpec((2 * EDGE, wide), lambda i: (0, 0)), VMEM],
        grid=(1,), input_output_aliases={9: 1},
        flops=2 * 32 * 1024 * 1536, moved=4 * 2**20,
    )


def terms_kernel(keeps, place, input_ref, glu_ref, out_ref, act_ref, *refs):
    sum_ref = refs[-1]
    core = place[3]
    wide = 2 * act_ref.shape[1]
    rows = sum_ref.shape[1]
    for half in range(2):
        block = 2 * half + (core if keeps else 1 - core)
        span = pl.ds(pl.multiple_of(block * rows, rows), rows)
        for source, low, start in ((input_ref, glu_ref, 0), (out_ref, act_ref, wide)):
            left = source[:, span]
            for part in range(0, low.shape[1], 256):
                term = dot_tn(left, low[:, part : part + 256])
                at = slice(start + part, start + part + 256)
                if keeps:
                    term = term + refs[0][half, :, at].astype(FULL)
                sum_ref[half, :, at] = term.astype(LOW)


def terms(place, input_rows, glu_low, out_rows, activated, arrived=None):
    wide = input_rows.shape[1]
    dims = (2, wide // 4, glu_low.shape[1] + activated.shape[1])
    operands = (place, input_rows, glu_low, out_rows, activated) + (() if arrived is None else (arrived,))
    return call(
        functools.partial(terms_kernel, arrived is not None), "terms",
        operands, [SMEM] + [VMEM] * (len(operands) - 1), [shape(dims)],
        flops=2 * input_rows.shape[0] * dims[0] * dims[1] * dims[2], moved=5 * 2**20,
    )[0]


def resid_kernel(
    place, out_ref, mid_ref, far_mid_ref, part_ref, far_part_ref, weight_ref, attended_ref,
    resid_ref, grad_ref, send_ref, keep_ref,
):
    frames = out_ref.shape[0]
    first, length, core = place[0], place[1], place[3]
    inner = frames - EDGE

    def total(rows, own, far):
        resid_ref[rows] = (out_ref[rows].astype(FULL) + (own.astype(FULL) + far.astype(FULL))).astype(LOW)

    total(slice(0, EDGE), part_ref[:EDGE], far_part_ref[:EDGE])
    total(slice(EDGE, inner), mid_ref[...], far_mid_ref[...])
    total(slice(inner, frames), part_ref[EDGE:], far_part_ref[EDGE:])
    rows = send_ref.shape[1]
    for out, flip in ((send_ref, 1), (keep_ref, 0)):
        for half in range(2):
            block = 2 * half + (1 - core if flip else core)
            span = pl.ds(pl.multiple_of(block * rows, rows), rows)
            out[half] = dot_tn(resid_ref[:, span], attended_ref[...]).astype(LOW)
    frame = lax.broadcasted_iota(jnp.int32, grad_ref.shape, 0) + first
    grad = dot_nt(resid_ref[...], weight_ref[...])
    grad_ref[...] = jnp.where(frame < length, grad, 0.0).astype(LOW)


def resid(place, out_rows, mid, far_mid, part, far_part, weight, attended):
    frames, wide = out_rows.shape
    cols = attended.shape[1]
    return call(
        resid_kernel, "resid",
        (place, out_rows, mid, far_mid, part, far_part, weight, attended),
        [SMEM] + [VMEM] * 7,
        [shape((frames, wide)), shape((frames, cols))] + [shape((2, wide // 4, cols))] * 2,
        flops=4 * frames * wide * cols, moved=6 * 2**20,
    )


def halves_kernel(place, own_ref, arrived_ref, send_ref, keep_ref):
    y_lo = place[4]
    for out, at in ((send_ref, 1 - y_lo), (keep_ref, y_lo)):
        out[...] = (own_ref[at].astype(FULL) + arrived_ref[at].astype(FULL)).astype(LOW)


def halves(place, own, arrived):
    return call(
        halves_kernel, "halves", (place, own, arrived), [SMEM, VMEM, VMEM], [shape(own.shape[1:])] * 2,
        moved=6 * own.size,
    )


BLOCK = 128
SPAN = BLOCK + 2 * WIN
SCALE = HEAD_DIM**-0.5
PAIR = 2 * HEAD_DIM


def side_by_side(rows):
    lane = lax.broadcasted_iota(jnp.int32, rows.shape, 1)
    zero = jnp.zeros_like(rows)
    return jnp.concatenate(
        [jnp.where(lane < HEAD_DIM, rows, zero), jnp.where(lane < HEAD_DIM, zero, rows)], axis=0
    )


def own_columns(columns):
    return jnp.concatenate([columns[:HEAD_DIM, :BLOCK], columns[HEAD_DIM:, BLOCK:]], axis=0)


def gather_rows(whole, before_ref, own_ref, after_ref, edge_span, span):
    frames = own_ref.shape[0]
    whole[:WIN] = before_ref[:WIN, edge_span]
    whole[WIN : WIN + frames] = own_ref[:, span]
    whole[WIN + frames :] = after_ref[:WIN, edge_span]


def spans(pair, cols):
    own = pl.ds(pl.multiple_of(pair * PAIR, PAIR), PAIR)
    far = pl.ds(pl.multiple_of(pair * PAIR + cols, PAIR), PAIR)
    return own, far


def attend_kernel(place, q_ref, k_ref, v_ref, before_ref, after_ref, prob_ref, out_ref, fill, keys, values):
    first, length = place[0], place[1]
    frames, cols = q_ref.shape
    for block in range(frames // BLOCK):
        key = lax.broadcasted_iota(jnp.int32, (SPAN, BLOCK), 0)
        offset = key - lax.broadcasted_iota(jnp.int32, (SPAN, BLOCK), 1)
        frame = key + (first - WIN + block * BLOCK)
        allowed = (offset >= 0) & (offset <= 2 * WIN) & (frame >= 0) & (frame < length)
        fill[block] = jnp.where(allowed, 0.0, NEG_FILL)

    def one_pair(pair, carry):
        own, far = spans(pair, cols)
        gather_rows(keys, before_ref, k_ref, after_ref, own, own)
        gather_rows(values, before_ref, v_ref, after_ref, far, own)
        for block in range(frames // BLOCK):
            rows = slice(block * BLOCK, (block + 1) * BLOCK)
            span = slice(block * BLOCK, block * BLOCK + SPAN)
            queries = side_by_side(q_ref[rows, own] * SCALE)
            scores = dot_nt(keys[span], queries) + jnp.concatenate([fill[block], fill[block]], axis=1)
            exponent = jnp.exp(scores - jnp.max(scores, axis=0, keepdims=True))
            prob = exponent * (1.0 / jnp.sum(exponent, axis=0, keepdims=True))
            prob_low = prob.astype(LOW)
            prob_ref[pair, block] = prob_low
            summed = own_columns(dot_tn(values[span], prob_low))
            frame = lax.broadcasted_iota(jnp.int32, (1, BLOCK), 1) + (first + block * BLOCK)
            out_ref[rows, own] = jnp.where(frame < length, summed, 0.0).T.astype(LOW)
        return carry

    lax.fori_loop(0, cols // PAIR, one_pair, 0)


def attend_grad_kernel(
    q_ref, k_ref, v_ref, before_ref, after_ref, prob_ref, out_ref, grad_ref,
    dq_ref, dk_ref, dv_ref, to_before_ref, to_after_ref, keys, values, key_sum, value_sum,
):
    frames, cols = q_ref.shape

    def one_pair(pair, carry):
        own, far = spans(pair, cols)
        gather_rows(keys, before_ref, k_ref, after_ref, own, own)
        gather_rows(values, before_ref, v_ref, after_ref, far, own)
        key_sum[...] = jnp.zeros_like(key_sum)
        value_sum[...] = jnp.zeros_like(value_sum)
        for block in range(frames // BLOCK):
            rows = slice(block * BLOCK, (block + 1) * BLOCK)
            span = slice(block * BLOCK, block * BLOCK + SPAN)
            queries = side_by_side(q_ref[rows, own] * SCALE)
            grad_rows = grad_ref[rows, own]
            grads = side_by_side(grad_rows)
            product = (grad_rows.astype(FULL) * out_ref[rows, own].astype(FULL)).T
            row_delta = jnp.concatenate(
                [
                    jnp.sum(product[:HEAD_DIM], axis=0, keepdims=True),
                    jnp.sum(product[HEAD_DIM:], axis=0, keepdims=True),
                ],
                axis=1,
            )
            prob_low = prob_ref[pair, block]
            grad_prob = dot_nt(values[span], grads)
            grad_score = (prob_low.astype(FULL) * (grad_prob - row_delta)).astype(LOW)
            value_sum[span] += jnp.dot(prob_low, grads, preferred_element_type=FULL)
            key_sum[span] += jnp.dot(grad_score, queries, preferred_element_type=FULL)
            dq_ref[rows, own] = (own_columns(dot_tn(keys[span], grad_score)).T * SCALE).astype(LOW)
        for total, inner, outer in ((key_sum, dk_ref, own), (value_sum, dv_ref, far)):
            to_before_ref[:, outer] = total[:WIN].astype(LOW)
            inner[:, own] = total[WIN : WIN + frames]
            to_after_ref[:, outer] = total[WIN + frames :].astype(LOW)
        return carry

    lax.fori_loop(0, cols // PAIR, one_pair, 0)


def attend(place, q_rows, k_rows, v_rows, before, after):
    frames, cols = q_rows.shape
    pairs, blocks = cols // PAIR, frames // BLOCK
    return call(
        attend_kernel, "attend", (place, q_rows, k_rows, v_rows, before, after), [SMEM] + [VMEM] * 5,
        [shape((pairs, blocks, SPAN, 2 * BLOCK)), shape((frames, cols))],
        scratch=[pltpu.VMEM((blocks, SPAN, BLOCK), FULL)] + [pltpu.VMEM((frames + 2 * WIN, PAIR), LOW)] * 2,
        flops=8 * frames * SPAN * cols, moved=6 * 2**20,
    )


def attend_grad(q_rows, k_rows, v_rows, before, after, prob, attended, grad_attn):
    frames, cols = q_rows.shape
    return call(
        attend_grad_kernel, "attend_grad",
        (q_rows, k_rows, v_rows, before, after, prob, attended, grad_attn), [VMEM] * 8,
        [shape((frames, cols))] + [shape((frames, cols), FULL)] * 2 + [shape((WIN, 2 * cols))] * 2,
        scratch=[pltpu.VMEM((frames + 2 * WIN, PAIR), LOW)] * 2 + [pltpu.VMEM((frames + 2 * WIN, PAIR), FULL)] * 2,
        flops=16 * frames * SPAN * cols, moved=9 * 2**20,
    )


def local(
    lengths,
    query_act,
    key_act,
    value_act,
    conv_input,
    conv_result,
    out_grad,
    out_weight,
    glu_weight,
    conv_taps,
    proj_weight,
):
    q_rows, k_rows, v_rows = (query_act[0], key_act[0], value_act[0])
    input_rows, pre_rows, out_rows = (conv_input[0], conv_result[0], out_grad[0])
    frames, cols = q_rows.shape
    peers = lax.axis_size("seq")
    index = lax.axis_index("dp")
    first = lax.axis_index("seq") * frames
    place = jnp.stack([first, lengths[0], peers * frames, index % 2, index // 2]).astype(jnp.int32)

    up, down = pack(k_rows, v_rows, out_rows, pre_rows)
    before, after = (round_ring(up, 1), round_ring(down, -1))
    mid, glu_low, activated, rim_rows, rim_gate, rim_value = front(
        place, out_rows, pre_rows, proj_weight, input_rows, glu_weight, conv_taps
    )
    far_mid = swapped(mid, "tensor", 1)
    part, glu_low = rim(
        place, before, after, rim_rows, rim_gate, rim_value, proj_weight, glu_weight, conv_taps, glu_low
    )
    far_part = swapped(part, "tensor", 1)
    given = swapped(terms(place, input_rows, glu_low, out_rows, activated), "dp", 1)
    prob, attended = attend(place, q_rows, k_rows, v_rows, before, after)
    on_chip = terms(place, input_rows, glu_low, out_rows, activated, given)
    resid_low, grad_attn, out_send, out_keep = resid(
        place, out_rows, mid, far_mid, part, far_part, out_weight, attended
    )
    out_given = swapped(out_send, "dp", 1)
    on_chip_out = halves(place, out_keep, out_given)
    on_chip_rest = halves(place, on_chip, jnp.zeros_like(on_chip))
    pair_out = on_chip_out[1].astype(FULL) + swapped(on_chip_out[0], "dp", 2).astype(FULL)
    pair_rest = on_chip_rest[1].astype(FULL) + swapped(on_chip_rest[0], "dp", 2).astype(FULL)
    grad_query, grad_key, grad_value, to_before, to_after = attend_grad(
        q_rows, k_rows, v_rows, before, after, prob, attended, grad_attn
    )
    from_after, from_before = (round_ring(to_before, -1), round_ring(to_after, 1))

    def with_arrived(own, span):
        below = jnp.pad(from_before[:, span].astype(FULL), ((0, frames - WIN), (0, 0)))
        above = jnp.pad(from_after[:, span].astype(FULL), ((frames - WIN, 0), (0, 0)))
        return (own + below + above).astype(LOW)

    joined = jnp.concatenate([pair_out, pair_rest], axis=1).astype(LOW)
    arrived = lax.all_to_all(joined.reshape(peers, -1, joined.shape[1]), "seq", 0, 0)
    summed = jnp.sum(arrived.astype(FULL), axis=0)
    glu_sum = summed[:, cols : 3 * cols].reshape(-1, 2, cols).transpose(1, 0, 2)
    return (
        resid_low[None],
        grad_query[None],
        with_arrived(grad_key, slice(0, cols))[None],
        with_arrived(grad_value, slice(cols, 2 * cols))[None],
        summed[:, :cols].T.astype(LOW),
        glu_sum.astype(LOW),
        summed[:, 3 * cols :].T.astype(LOW),
    )


def solution(mesh):
    in_specs = (
        P("dp"),
        P("dp", "seq", "tensor"),
        P("dp", "seq", "tensor"),
        P("dp", "seq", "tensor"),
        P("dp", "seq", None),
        P("dp", "seq", "tensor"),
        P("dp", "seq", None),
        P("tensor", None),
        P(None, None, "tensor"),
        P(None, "tensor"),
        P("tensor", None),
    )
    out_specs = (
        P("dp", "seq", None),
        P("dp", "seq", "tensor"),
        P("dp", "seq", "tensor"),
        P("dp", "seq", "tensor"),
        P("tensor", ("dp", "seq")),
        P(None, ("dp", "seq"), "tensor"),
        P("tensor", ("dp", "seq")),
    )
    return jax.shard_map(local, mesh=mesh, in_specs=in_specs, out_specs=out_specs, check_vma=False)
```

time: 807 us -> 137 us (0.17)
  the two profiles are of different devices: /device:TPU:32 before, /device:TPU:1 now
where the time goes in v2:
time: 137 us
  waiting for transfers between devices  56.9 us (42%)
  Pallas kernels  31.8 us (23%)
  starting transfers between devices  28.4 us (21%)
  local copies, waits for them, and re-layouts  14.2 us (10%)
  other arithmetic  3.96 us (3%)
  between operations  1.5 us (1%)
    pallas_call x10, Pallas kernels, call(): pl.pallas_call(kernel, in_specs=in_specs, out_specs=[VMEM] * len(out_shap...  31.8 us
    ppermute x6, waiting for transfers between devices, swapped(): return lax.ppermute(value, axis, [(i, i ^ stride) for i in range(count)])  29.5 us
    ppermute x4, waiting for transfers between devices, round_ring(): lax.ppermute(value, 'seq', [(i, (i + steps) % count) for i in range(count)])  27.4 us
    ppermute x4, starting transfers between devices, round_ring(): lax.ppermute(value, 'seq', [(i, (i + steps) % count) for i in range(count)])  13.4 us
    unnamed x42, local copies, waits for them, and re-layouts  12.7 us
    all_to_all x1, starting transfers between devices, local(): lax.all_to_all(joined.reshape(peers, -1, joined.shape[1]), 'seq', 0, 0)  8.23 us
    ppermute x6, starting transfers between devices, swapped(): return lax.ppermute(value, axis, [(i, i ^ stride) for i in range(count)])  6.81 us
  transfers between devices with their start and end apart: 11, of which 4 were waited for; matrix products, arithmetic and copies ran while one was open for 1% of the time, Pallas kernels for 20%

profile of v2, /device:TPU:1, one launch (start us, length us, event | category | flops | bytes accessed | tf_op | source)
XLA Modules:
  0.0 136.7 jit_solution(4681141126842397277)
XLA Ops:
  0.6 1.1 copy-done
  1.8 1.0 copy-done.7
  2.8 1.0 copy-done.9
  3.8 1.0 copy-done.11
  4.8 1.1 pack.1
  5.9 2.0 %collective-permute-start.1 = (bf16[288,1024]{1,0:T(8,128)(2,1)}, bf16[288,1024]{1,0:T(8,128)(2,1)S(1)}, u32[]{:S(2)}, u32[]{:S(2)}) collective-permute-start(bf16[288,1024]{1,0:T(8,128)(2,1)} %get-tuple-element.33), channel_id=1, source_target_pairs={{0,2},{2,4},{4,6},{6,8},{8,10},{10,12},{12,14},{14,16},{16,18},{18... | collective-permute-start | bytes 1769480 | tf_op jit(solution)/shard_map/ppermute | solution.py:51
  7.9 6.6 %collective-permute-start.2 = (bf16[288,1024]{1,0:T(8,128)(2,1)}, bf16[288,1024]{1,0:T(8,128)(2,1)S(1)}, u32[]{:S(2)}, u32[]{:S(2)}) collective-permute-start(bf16[288,1024]{1,0:T(8,128)(2,1)} %get-tuple-element.34), channel_id=1, source_target_pairs={{0,62},{2,0},{4,2},{6,4},{8,6},{10,8},{12,10},{14,12},{16,14},{18,... | collective-permute-start | bytes 1769480 | tf_op jit(solution)/shard_map/ppermute | solution.py:51
  15.2 1.6 %copy-done.3 = bf16[2,1024,512]{2,1,0:T(8,128)(2,1)S(1)} copy-done((bf16[2,1024,512]{2,1,0:T(8,128)(2,1)S(1)}, bf16[2,1024,512]{2,1,0:T(8,128)(2,1)}, u32[]{:S(2)}) %copy-start.3) | copy-done | bytes 2097176
  16.8 1.2 copy-done.5
  18.1 6.9 %front.1 = (bf16[352,1024]{1,0:T(8,128)(2,1)S(1)}, bf16[384,1024]{1,0:T(8,128)(2,1)S(1)}, bf16[384,512]{1,0:T(8,128)(2,1)S(1)}, bf16[64,512]{1,0:T(8,128)(2,1)S(...) custom-call(s32[5]{0:T(128)S(1)} %stack.15.place, bf16[384,1024]{1,0:T(8,128)(2,1)S(1)} %bitcast.27, ...), custom_call_target="tpu_custom_call" | custom-call | flops 2013265920 | bytes 6291456 | tf_op jit(solution)/shard_map/front/pallas_call | solution.py:28
  24.9 2.8 %collective-permute-done.1.before_ref = bf16[288,1024]{1,0:T(8,128)(2,1)S(1)} collective-permute-done((bf16[288,1024]{1,0:T(8,128)(2,1)}, bf16[288,1024]{1,0:T(8,128)(2,1)S(1)}, u32[]{:S(2)}, u32[]{:S(2)}) %collective-permute-start.1) | collective-permute-done | bytes 589856 | tf_op jit(solution)/shard_map/ppermute | solution.py:51
  27.7 1.8 %rim.1 = (bf16[32,1024]{1,0:T(8,128)(2,1)S(1)}, bf16[384,1024]{1,0:T(8,128)(2,1)S(1)}) custom-call(s32[5]{0:T(128)S(1)} %stack.15.place, bf16[288,1024]{1,0:T(8,128)(2,1)S(1)} %collective-permute-done.1.before_ref, bf16[288,1024]{1,0:T(8,128)(2,1)S(1)} %collective-permute-done.2.after_ref, ...), custom_call_target="tpu_custom_call", output_to_operand_aliasing={{1}: (9, {})} | custom-call | flops 100663296 | bytes 4194304 | tf_op jit(solution)/shard_map/rim/pallas_call | solution.py:28
  29.6 1.6 %terms.2 = bf16[2,256,1536]{2,1,0:T(8,128)(2,1)S(1)} custom-call(s32[5]{0:T(128)S(1)} %stack.15.place, bf16[384,1024]{1,0:T(8,128)(2,1)S(1)} %bitcast.32, bf16[384,1024]{1,0:T(8,128)(2,1)S(1)} %get-tuple-element.53.glu_ref, bf16[384,1024]{1,0:T(8,128)(2,1)S(1)} %bitcast.28, bf16[384,512]{1,0:T(8,128)(2,1)S(1)} %get-tuple-element.54.act_ref), custom_call_target="tpu_custom_call" | custom-call | flops 603979776 | bytes 5242880 | tf_op jit(solution)/shard_map/terms/pallas_call | solution.py:28
  31.2 1.3 collective-permute-start.8
  32.5 2.9 %collective-permute-start = (bf16[352,1024]{1,0:T(8,128)(2,1)S(1)}, bf16[352,1024]{1,0:T(8,128)(2,1)S(1)}, u32[]{:S(2)}, u32[]{:S(2)}) collective-permute-start(bf16[352,1024]{1,0:T(8,128)(2,1)S(1)} %get-tuple-element.32.mid_ref), channel_id=1, source_target_pairs={{0,1},{1,0},{2,3},{3,2},{4,5},{5,4},{6,7},{7,6},{8,9},{9,8},{10,11... | collective-permute-start | bytes 2162696 | tf_op jit(solution)/shard_map/ppermute | solution.py:56
  35.5 8.8 %attend.1 = (bf16[4,3,640,256]{3,2,1,0:T(8,128)(2,1)S(1)}, bf16[384,512]{1,0:T(8,128)(2,1)S(1)}) custom-call(s32[5]{0:T(128)S(1)} %stack.15.place, bf16[384,512]{1,0:T(8,128)(2,1)S(1)} %bitcast.42, bf16[384,512]{1,0:T(8,128)(2,1)S(1)} %bitcast.37, bf16[384,512]{1,0:T(8,128)(2,1)S(1)} %bitcast.40, bf16[288,1024]{1,0:T(8,128)(2,1)S(1)} %collective-permute-done.1.before_ref, ...), custom_call_target="tpu_custom_call" | custom-call | flops 1006632960 | bytes 6291456 | tf_op jit(solution)/shard_map/attend/pallas_call | solution.py:28
  44.3 1.9 %copy-done.19 = bf16[4,3,640,256]{3,2,1,0:T(8,128)(2,1)} copy-done((bf16[4,3,640,256]{3,2,1,0:T(8,128)(2,1)}, bf16[4,3,640,256]{3,2,1,0:T(8,128)(2,1)S(1)}, u32[]{:S(2)}) %copy-start.19) | copy-done | bytes 3932184
  46.1 7.0 %collective-permute-done.3.far_part_ref = bf16[32,1024]{1,0:T(8,128)(2,1)S(1)} collective-permute-done((bf16[32,1024]{1,0:T(8,128)(2,1)S(1)}, bf16[32,1024]{1,0:T(8,128)(2,1)S(1)}, u32[]{:S(2)}, u32[]{:S(2)}) %collective-permute-start.3) | collective-permute-done | bytes 65568 | tf_op jit(solution)/shard_map/ppermute | solution.py:56
  53.1 2.5 %resid.1 = (bf16[384,1024]{1,0:T(8,128)(2,1)}, bf16[384,512]{1,0:T(8,128)(2,1)S(1)}, bf16[2,256,512]{2,1,0:T(8,128)(2,1)S(1)}, bf16[2,256,512]{2,1,0:T(8,128)(2,1)S(1)}) custom-call(s32[5]{0:T(128)S(1)} %stack.15.place, bf16[384,1024]{1,0:T(8,128)(2,1)S(1)} %bitcast.29, bf16[352,1024]{1,0:T(8,128)(2,1)S(1)} %get-tuple-element.32.mid_ref, ...), custom_call_target="tpu_custom_call" | custom-call | flops 805306368 | bytes 6291456 | tf_op jit(solution)/shard_map/resid/pallas_call | solution.py:28
  57.2 1.6 %terms.3.own_ref = bf16[2,256,1536]{2,1,0:T(8,128)(2,1)S(1)} custom-call(s32[5]{0:T(128)S(1)} %stack.15.place, bf16[384,1024]{1,0:T(8,128)(2,1)S(1)} %bitcast.33, bf16[384,1024]{1,0:T(8,128)(2,1)S(1)} %get-tuple-element.53.glu_ref, bf16[384,1024]{1,0:T(8,128)(2,1)S(1)} %bitcast.30, bf16[384,512]{1,0:T(8,128)(2,1)S(1)} %get-tuple-element.54.act_ref, ...), custom_call_target="tpu_custom_call" | custom-call | flops 603979776 | bytes 5242880 | tf_op jit(solution)/shard_map/terms/pallas_call | solution.py:28
  59.8 1.4 %collective-permute-start.9 = (bf16[256,1536]{1,0:T(8,128)(2,1)S(1)}, bf16[256,1536]{1,0:T(8,128)(2,1)S(1)}, u32[]{:S(2)}, u32[]{:S(2)}) collective-permute-start(bf16[256,1536]{1,0:T(8,128)(2,1)S(1)} %get-tuple-element.56), channel_id=1, source_target_pairs={{0,128},{64,192},{128,0},{192,64},{1,129},{65,193},{129,1},{193,65... | collective-permute-start | bytes 2359304 | tf_op jit(solution)/shard_map/ppermute | solution.py:56
  62.1 22.6 %collective-permute-done.7 = bf16[256,512]{1,0:T(8,128)(2,1)S(1)} collective-permute-done((bf16[256,512]{1,0:T(8,128)(2,1)S(1)}, bf16[256,512]{1,0:T(8,128)(2,1)S(1)}, u32[]{:S(2)}, u32[]{:S(2)}) %collective-permute-start.7) | collective-permute-done | bytes 262176 | tf_op jit(solution)/shard_map/ppermute | solution.py:56
  84.9 1.1 pad_maximum_fusion
  86.1 8.2 %all-to-all-start = ((bf16[32,8,2048]{2,1,0:T(8,128)(2,1)}), bf16[32,8,2048]{2,1,0:T(8,128)(2,1)}, u32[]{:S(2)}, u32[]{:S(2)}) async-start(bf16[32,8,2048]{2,1,0:T(8,128)(2,1)} %pad_maximum_fusion), calls=%async_computation | async-start | bytes 2097152 | tf_op jit(solution)/shard_map/all_to_all | solution.py:468
  94.3 1.0 copy-done.18
  95.3 2.1 %copy-done.20 = bf16[4,3,640,256]{3,2,1,0:T(8,128)(2,1)S(1)} copy-done((bf16[4,3,640,256]{3,2,1,0:T(8,128)(2,1)S(1)}, bf16[4,3,640,256]{3,2,1,0:T(8,128)(2,1)}, u32[]{:S(2)}) %copy-start.20) | copy-done | bytes 3932184
  97.4 6.1 %attend_grad.1 = (bf16[384,512]{1,0:T(8,128)(2,1)}, f32[384,512]{1,0:T(8,128)S(1)}, f32[384,512]{1,0:T(8,128)S(1)}, bf16[256,1024]{1,0:T(8,128)(2,1)S(1)}, bf16[256,1024]{1,0:T(8,128)(2,1)S(1)}) custom-call(bf16[384,512]{1,0:T(8,128)(2,1)S(1)} %bitcast.43, bf16[384,512]{1,0:T(8,128)(2,1)S(1)} %bitcast.38, bf16[384,512]{1,0:T(8,128)(2,1)S(1)} %bitcast.41, ...), custom_call_target="tpu_custom_call" | custom-call | flops 2013265920 | bytes 9437184 | tf_op jit(solution)/shard_map/attend_grad/pallas_call | solution.py:28
  103.5 1.2 collective-permute-start.4
  104.6 3.6 %collective-permute-start.5 = (bf16[256,1024]{1,0:T(8,128)(2,1)S(1)}, bf16[256,1024]{1,0:T(8,128)(2,1)S(1)}, u32[]{:S(2)}, u32[]{:S(2)}) collective-permute-start(bf16[256,1024]{1,0:T(8,128)(2,1)S(1)} %get-tuple-element.47), channel_id=1, source_target_pairs={{0,62},{2,0},{4,2},{6,4},{8,6},{10,8},{12,10},{14,12},{16,14},{18,... | collective-permute-start | bytes 1572872 | tf_op jit(solution)/shard_map/ppermute | solution.py:51
  108.3 24.6 %collective-permute-done.4 = bf16[256,1024]{1,0:T(8,128)(2,1)S(1)} collective-permute-done((bf16[256,1024]{1,0:T(8,128)(2,1)S(1)}, bf16[256,1024]{1,0:T(8,128)(2,1)S(1)}, u32[]{:S(2)}, u32[]{:S(2)}) %collective-permute-start.4) | collective-permute-done | bytes 524320 | tf_op jit(solution)/shard_map/ppermute | solution.py:51
  132.9 1.2 fusion.1
  134.1 1.4 %reduce = bf16[8,2048]{1,0:T(8,128)(2,1)S(1)} reduce(bf16[32,8,2048]{2,1,0:T(8,128)(2,1)} %all-to-all-done, bf16[]{:T(256)} %constant.45.clone.1), dimensions={0}, to_apply=%region_0.1.clone | reduce | flops 507904 | bytes 1081346 | tf_op jit(solution)/shard_map/reduce_sum | solution.py:469
  (53 shorter events, 5.3 us)
Async XLA Ops:
  0.6 1.1 copy-start
  1.8 1.0 copy-start.7
  2.8 1.0 copy-start.9
  3.8 1.0 copy-start.11
  4.8 10.5 %copy-start.1 = (bf16[1,384,1024]{2,1,0:T(8,128)(2,1)S(1)}, bf16[1,384,1024]{2,1,0:T(8,128)(2,1)}, u32[]{:S(2)}) copy-start(bf16[1,384,1024]{2,1,0:T(8,128)(2,1)} %param.17) | copy-start | bytes 2359300
  4.8 10.5 %copy-start.2 = (bf16[1,384,1024]{2,1,0:T(8,128)(2,1)S(1)}, bf16[1,384,1024]{2,1,0:T(8,128)(2,1)}, u32[]{:S(2)}) copy-start(bf16[1,384,1024]{2,1,0:T(8,128)(2,1)} %param.15) | copy-start | bytes 2359300
  4.8 10.5 %copy-start.8 = (bf16[1,384,512]{2,1,0:T(8,128)(2,1)S(1)}, bf16[1,384,512]{2,1,0:T(8,128)(2,1)}, u32[]{:S(2)}) copy-start(bf16[1,384,512]{2,1,0:T(8,128)(2,1)} %param.16) | copy-start | bytes 1179652
  4.8 10.5 %copy-start.14 = (bf16[31,512]{1,0:T(8,128)(2,1)S(1)}, bf16[31,512]{1,0:T(8,128)(2,1)}, u32[]{:S(2)}) copy-start(bf16[31,512]{1,0:T(8,128)(2,1)} %taps_ref.3) | copy-start | bytes 95236
  5.9 21.9 %collective-permute-start.1 = (bf16[288,1024]{1,0:T(8,128)(2,1)}, bf16[288,1024]{1,0:T(8,128)(2,1)S(1)}, u32[]{:S(2)}, u32[]{:S(2)}) collective-permute-start(bf16[288,1024]{1,0:T(8,128)(2,1)} %get-tuple-element.33), channel_id=1, source_target_pairs={{0,2},{2,4},{4,6},{6,8},{8,10},{10,12},{12,14},{14,16},{16,18},{18... | collective-permute-start | bytes 1769480 | tf_op jit(solution)/shard_map/ppermute | solution.py:51
  7.9 19.8 %collective-permute-start.2 = (bf16[288,1024]{1,0:T(8,128)(2,1)}, bf16[288,1024]{1,0:T(8,128)(2,1)S(1)}, u32[]{:S(2)}, u32[]{:S(2)}) collective-permute-start(bf16[288,1024]{1,0:T(8,128)(2,1)} %get-tuple-element.34), channel_id=1, source_target_pairs={{0,62},{2,0},{4,2},{6,4},{8,6},{10,8},{12,10},{14,12},{16,14},{18,... | collective-permute-start | bytes 1769480 | tf_op jit(solution)/shard_map/ppermute | solution.py:51
  15.2 1.6 %copy-start.3 = (bf16[2,1024,512]{2,1,0:T(8,128)(2,1)S(1)}, bf16[2,1024,512]{2,1,0:T(8,128)(2,1)}, u32[]{:S(2)}) copy-start(bf16[2,1024,512]{2,1,0:T(8,128)(2,1)} %glu_w_ref.3) | copy-start | bytes 6291460
  16.8 1.2 copy-start.5
  18.0 9.7 %copy-start.4 = (bf16[2,1024,512]{2,1,0:T(8,128)(2,1)S(1)}, bf16[2,1024,512]{2,1,0:T(8,128)(2,1)}, u32[]{:S(2)}) copy-start(bf16[2,1024,512]{2,1,0:T(8,128)(2,1)} %glu_w_ref.3) | copy-start | bytes 6291460
  29.6 5.9 %copy-start.10 = (bf16[1,384,512]{2,1,0:T(8,128)(2,1)S(1)}, bf16[1,384,512]{2,1,0:T(8,128)(2,1)}, u32[]{:S(2)}) copy-start(bf16[1,384,512]{2,1,0:T(8,128)(2,1)} %param.13) | copy-start | bytes 1179652
  29.6 5.9 %copy-start.12 = (bf16[1,384,512]{2,1,0:T(8,128)(2,1)S(1)}, bf16[1,384,512]{2,1,0:T(8,128)(2,1)}, u32[]{:S(2)}) copy-start(bf16[1,384,512]{2,1,0:T(8,128)(2,1)} %param.14) | copy-start | bytes 1179652
  29.6 5.9 %copy-start.15 = (bf16[1,384,512]{2,1,0:T(8,128)(2,1)S(1)}, bf16[1,384,512]{2,1,0:T(8,128)(2,1)}, u32[]{:S(2)}) copy-start(bf16[1,384,512]{2,1,0:T(8,128)(2,1)} %param.12) | copy-start | bytes 1179652
  31.2 26.0 %collective-permute-start.8 = (bf16[2,256,1536]{2,1,0:T(8,128)(2,1)S(1)}, bf16[2,256,1536]{2,1,0:T(8,128)(2,1)S(1)}, u32[]{:S(2)}, u32[]{:S(2)}) collective-permute-start(bf16[2,256,1536]{2,1,0:T(8,128)(2,1)S(1)} %terms.2), channel_id=1, source_target_pairs={{0,64},{64,0},{128,192},{192,128},{1,65},{65,1},{129,193},{193,129... | collective-permute-start | bytes 4718600 | tf_op jit(solution)/shard_map/ppermute | solution.py:56
  32.5 20.6 %collective-permute-start = (bf16[352,1024]{1,0:T(8,128)(2,1)S(1)}, bf16[352,1024]{1,0:T(8,128)(2,1)S(1)}, u32[]{:S(2)}, u32[]{:S(2)}) collective-permute-start(bf16[352,1024]{1,0:T(8,128)(2,1)S(1)} %get-tuple-element.32.mid_ref), channel_id=1, source_target_pairs={{0,1},{1,0},{2,3},{3,2},{4,5},{5,4},{6,7},{7,6},{8,9},{9,8},{10,11... | collective-permute-start | bytes 2162696 | tf_op jit(solution)/shard_map/ppermute | solution.py:56
  35.4 17.7 %collective-permute-start.3 = (bf16[32,1024]{1,0:T(8,128)(2,1)S(1)}, bf16[32,1024]{1,0:T(8,128)(2,1)S(1)}, u32[]{:S(2)}, u32[]{:S(2)}) collective-permute-start(bf16[32,1024]{1,0:T(8,128)(2,1)S(1)} %get-tuple-element.39.part_ref), channel_id=1, source_target_pairs={{0,1},{1,0},{2,3},{3,2},{4,5},{5,4},{6,7},{7,6},{8,9},{9,8},{10,11... | collective-permute-start | bytes 196616 | tf_op jit(solution)/shard_map/ppermute | solution.py:56
  35.5 17.6 %copy-start.6 = (bf16[512,1024]{1,0:T(8,128)(2,1)S(1)}, bf16[512,1024]{1,0:T(8,128)(2,1)}, u32[]{:S(2)}) copy-start(bf16[512,1024]{1,0:T(8,128)(2,1)} %weight_ref.1) | copy-start | bytes 3145732
  44.3 1.9 %copy-start.19 = (bf16[4,3,640,256]{3,2,1,0:T(8,128)(2,1)}, bf16[4,3,640,256]{3,2,1,0:T(8,128)(2,1)S(1)}, u32[]{:S(2)}) copy-start(bf16[4,3,640,256]{3,2,1,0:T(8,128)(2,1)S(1)} %get-tuple-element.42.prob_ref) | copy-start | bytes 11796484
  55.6 0.7 copy-start.17
  56.3 4.9 %collective-permute-start.6 = (bf16[2,256,512]{2,1,0:T(8,128)(2,1)S(1)}, bf16[2,256,512]{2,1,0:T(8,128)(2,1)S(1)}, u32[]{:S(2)}, u32[]{:S(2)}) collective-permute-start(bf16[2,256,512]{2,1,0:T(8,128)(2,1)S(1)} %get-tuple-element.50), channel_id=1, source_target_pairs={{0,64},{64,0},{128,192},{192,128},{1,65},{65,1},{129,193},{193,129... | collective-permute-start | bytes 1572872 | tf_op jit(solution)/shard_map/ppermute | solution.py:56
  59.8 24.9 %collective-permute-start.9 = (bf16[256,1536]{1,0:T(8,128)(2,1)S(1)}, bf16[256,1536]{1,0:T(8,128)(2,1)S(1)}, u32[]{:S(2)}, u32[]{:S(2)}) collective-permute-start(bf16[256,1536]{1,0:T(8,128)(2,1)S(1)} %get-tuple-element.56), channel_id=1, source_target_pairs={{0,128},{64,192},{128,0},{192,64},{1,129},{65,193},{129,1},{193,65... | collective-permute-start | bytes 2359304 | tf_op jit(solution)/shard_map/ppermute | solution.py:56
  61.9 22.8 %collective-permute-start.7 = (bf16[256,512]{1,0:T(8,128)(2,1)S(1)}, bf16[256,512]{1,0:T(8,128)(2,1)S(1)}, u32[]{:S(2)}, u32[]{:S(2)}) collective-permute-start(bf16[256,512]{1,0:T(8,128)(2,1)S(1)} %get-tuple-element.52), channel_id=1, source_target_pairs={{0,128},{64,192},{128,0},{192,64},{1,129},{65,193},{129,1},{193,65... | collective-permute-start | bytes 786440 | tf_op jit(solution)/shard_map/ppermute | solution.py:56
  86.1 8.2 %copy-start.13 = (bf16[1,384,512]{2,1,0:T(8,128)(2,1)S(1)}, bf16[1,384,512]{2,1,0:T(8,128)(2,1)}, u32[]{:S(2)}) copy-start(bf16[1,384,512]{2,1,0:T(8,128)(2,1)} %param.14) | copy-start | bytes 1179652
  86.1 8.3 %copy-start.16 = (bf16[1,384,512]{2,1,0:T(8,128)(2,1)S(1)}, bf16[1,384,512]{2,1,0:T(8,128)(2,1)}, u32[]{:S(2)}) copy-start(bf16[1,384,512]{2,1,0:T(8,128)(2,1)} %param.12) | copy-start | bytes 1179652
  86.1 48.1 %all-to-all-start = ((bf16[32,8,2048]{2,1,0:T(8,128)(2,1)}), bf16[32,8,2048]{2,1,0:T(8,128)(2,1)}, u32[]{:S(2)}, u32[]{:S(2)}) async-start(bf16[32,8,2048]{2,1,0:T(8,128)(2,1)} %pad_maximum_fusion), calls=%async_computation | async-start | bytes 2097152 | tf_op jit(solution)/shard_map/all_to_all | solution.py:468
  94.3 1.0 copy-start.18
  95.3 2.1 %copy-start.20 = (bf16[4,3,640,256]{3,2,1,0:T(8,128)(2,1)S(1)}, bf16[4,3,640,256]{3,2,1,0:T(8,128)(2,1)}, u32[]{:S(2)}) copy-start(bf16[4,3,640,256]{3,2,1,0:T(8,128)(2,1)} %copy-done.19) | copy-start | bytes 11796484
  103.5 29.3 %collective-permute-start.4 = (bf16[256,1024]{1,0:T(8,128)(2,1)S(1)}, bf16[256,1024]{1,0:T(8,128)(2,1)S(1)}, u32[]{:S(2)}, u32[]{:S(2)}) collective-permute-start(bf16[256,1024]{1,0:T(8,128)(2,1)S(1)} %get-tuple-element.46), channel_id=1, source_target_pairs={{0,2},{2,4},{4,6},{6,8},{8,10},{10,12},{12,14},{14,16},{16,18},{18... | collective-permute-start | bytes 1572872 | tf_op jit(solution)/shard_map/ppermute | solution.py:51
  104.6 28.2 %collective-permute-start.5 = (bf16[256,1024]{1,0:T(8,128)(2,1)S(1)}, bf16[256,1024]{1,0:T(8,128)(2,1)S(1)}, u32[]{:S(2)}, u32[]{:S(2)}) collective-permute-start(bf16[256,1024]{1,0:T(8,128)(2,1)S(1)} %get-tuple-element.47), channel_id=1, source_target_pairs={{0,62},{2,0},{4,2},{6,4},{8,6},{10,8},{12,10},{14,12},{16,14},{18,... | collective-permute-start | bytes 1572872 | tf_op jit(solution)/shard_map/ppermute | solution.py:51

commit v3 on v2

v3 whole, which is shorter than its diff:
```python
import functools

import jax
import jax.numpy as jnp
from jax import lax
from jax.experimental import pallas as pl
from jax.experimental.pallas import tpu as pltpu
from jax.sharding import PartitionSpec as P

HEAD_DIM = 64
WIN = 256


NEG_FILL = -1e30
FULL, LOW = jnp.float32, jnp.bfloat16
TAPS = 31
EDGE = 16
STRIP = 32
VMEM = pl.BlockSpec(memory_space=pltpu.VMEM)
SMEM = pl.BlockSpec(memory_space=pltpu.SMEM)
HBM = pl.BlockSpec(memory_space=pltpu.HBM)


def shape(dims, kind=LOW):
    return jax.ShapeDtypeStruct(dims, kind)


def call(kernel, name, operands, in_specs, out_shape, out_specs=None, scratch=(), micros=1, limit=24, **more):
    return pl.pallas_call(
        kernel,
        in_specs=in_specs,
        out_specs=[VMEM] * len(out_shape) if out_specs is None else out_specs,
        out_shape=out_shape,
        scratch_shapes=list(scratch),
        compiler_params=pltpu.CompilerParams(vmem_limit_bytes=limit * 2**20),
        cost_estimate=pl.CostEstimate(flops=int(micros * 9e8), bytes_accessed=1, transcendentals=0),
        name=name,
        **more,
    )(*operands)


def whole(array):
    return pl.BlockSpec(array.shape, lambda i: (0,) * array.ndim)


def dot_nt(left, right):
    return lax.dot_general(left, right, (((1,), (1,)), ((), ())), preferred_element_type=FULL)


def dot_tn(left, right):
    return lax.dot_general(left, right, (((0,), (0,)), ((), ())), preferred_element_type=FULL)


def round_ring(value, steps):
    count = lax.axis_size("seq")
    return lax.ppermute(value, "seq", [(i, (i + steps) % count) for i in range(count)])


def swapped(value, axis, stride):
    count = lax.axis_size(axis)
    return lax.ppermute(value, axis, [(i, i ^ stride) for i in range(count)])


def pack_kernel(k_ref, v_ref, grad_ref, pre_ref, up_ref, down_ref, sems):
    frames, cols = k_ref.shape
    copies = []
    for out_ref, start, edge in ((up_ref, frames - WIN, frames - EDGE), (down_ref, 0, 0)):
        for source, rows, count, first, span in (
            (k_ref, 0, WIN, start, slice(0, cols)),
            (v_ref, 0, WIN, start, slice(cols, 2 * cols)),
            (grad_ref, WIN, EDGE, edge, slice(0, 2 * cols)),
            (pre_ref, WIN + EDGE, EDGE, edge, slice(0, cols)),
        ):
            copies.append(
                pltpu.make_async_copy(
                    source.at[pl.ds(first, count)], out_ref.at[pl.ds(rows, count), span], sems.at[len(copies)]
                )
            )
    for copy in copies:
        copy.start()
    for out_ref in (up_ref, down_ref):
        out_ref[WIN + EDGE :, cols:] = jnp.zeros((EDGE, cols), LOW)
    for copy in copies:
        copy.wait()


def pack(k_rows, v_rows, out_rows, pre_rows):
    dims = (WIN + 2 * EDGE, 2 * k_rows.shape[1])
    return call(
        pack_kernel, "pack", (k_rows, v_rows, out_rows, pre_rows), [HBM] * 4, [shape(dims)] * 2,
        scratch=[pltpu.SemaphoreType.DMA((8,))], limit=58,
    )


def pre_grad(out_rows, pre_rows, proj):
    pre = pre_rows.astype(FULL)
    logistic = jax.nn.sigmoid(pre)
    slope = logistic * (1.0 + pre * (1.0 - logistic))
    return (dot_nt(out_rows, proj) * slope).astype(LOW), (pre * logistic).astype(LOW)


def conv_strip(rows, taps):
    count = rows.shape[0] - 2 * EDGE
    total = jnp.zeros((count, rows.shape[1]), FULL)
    for shift in range(8):
        moved = rows[shift : shift + count + 24]
        for coarse in range(4):
            step = 8 * coarse + shift
            if step >= 1:
                total = total + taps[TAPS - step : TAPS - step + 1] * moved[8 * coarse : 8 * coarse + count]
    return total


def glu_grads(grad_conv, logistic, value):
    first = grad_conv * logistic
    return first.astype(LOW), (first * value * (1.0 - logistic)).astype(LOW)


def front_kernel(
    place, out_ref, pre_ref, proj_ref, input_ref, glu_w_ref, taps_ref,
    mid_ref, glu_ref, act_ref, rim_ref, rim_gate_ref, rim_value_ref,
    padded, taps, gates, values,
):
    frames, cols = pre_ref.shape
    first, length = place[0], place[1]
    inner = frames - EDGE
    taps[:TAPS] = taps_ref[...].astype(FULL)
    for part in range(0, cols, 256):
        span = slice(part, part + 256)
        grad_pre, activated = pre_grad(out_ref[...], pre_ref[:, span], proj_ref[span])
        act_ref[:, span] = activated
        padded[:, span] = grad_pre.astype(FULL)
        rim_ref[: 2 * EDGE, span] = grad_pre[: 2 * EDGE]
        rim_ref[2 * EDGE :, span] = grad_pre[frames - 2 * EDGE :]
        values[:, span] = jnp.dot(input_ref[...], glu_w_ref[0, :, span], preferred_element_type=FULL)
        gate_half = jnp.dot(input_ref[...], glu_w_ref[1, :, span], preferred_element_type=FULL)
        gates[:, span] = jax.nn.sigmoid(gate_half)
    for whole, rim in ((gates, rim_gate_ref), (values, rim_value_ref)):
        rim[:EDGE] = whole[:EDGE]
        rim[EDGE:] = whole[inner:]

    def strip(i, carry):
        at = pl.multiple_of(i * STRIP, STRIP)
        rows = pl.ds(pl.multiple_of(at + EDGE, EDGE), STRIP)
        frame = lax.broadcasted_iota(jnp.int32, (STRIP, 128), 0) + (first + EDGE + at)
        valid = frame < length
        for part in range(0, cols, 128):
            span = slice(part, part + 128)
            grad_conv = conv_strip(padded[pl.ds(at, STRIP + 2 * EDGE), span], taps[:, span])
            grad_conv = jnp.where(valid, grad_conv, 0.0)
            low = glu_grads(grad_conv, gates[rows, span], values[rows, span])
            glu_ref[rows, span] = low[0]
            glu_ref[rows, cols + part : cols + part + 128] = low[1]
        return carry

    lax.fori_loop(0, (frames - 2 * EDGE) // STRIP, strip, 0)
    for part in range(0, mid_ref.shape[1], 256):
        span = slice(part, part + 256)
        mid_ref[:, span] = (
            dot_nt(glu_ref[EDGE:inner, :cols], glu_w_ref[0, span])
            + dot_nt(glu_ref[EDGE:inner, cols:], glu_w_ref[1, span])
        ).astype(LOW)


def front(place, out_rows, pre_rows, proj, input_rows, glu_weight, taps):
    frames, cols = pre_rows.shape
    wide = input_rows.shape[1]
    return call(
        front_kernel, "front",
        (place, out_rows, pre_rows, proj, input_rows, glu_weight, taps),
        [SMEM] + [VMEM] * 6,
        [
            shape((frames - 2 * EDGE, wide)), shape((frames, 2 * cols)), shape((frames, cols)),
            shape((4 * EDGE, cols)), shape((2 * EDGE, cols), FULL), shape((2 * EDGE, cols), FULL),
        ],
        scratch=[
            pltpu.VMEM((frames, cols), FULL), pltpu.VMEM((32, cols), FULL),
            pltpu.VMEM((frames, cols), FULL), pltpu.VMEM((frames, cols), FULL),
        ],
        micros=7,
    )


def rim_kernel(
    place, before_ref, after_ref, rim_ref, gate_ref, value_ref, proj_ref, glu_w_ref, taps_ref, glu_in_ref,
    part_ref, glu_ref,
):
    frames = glu_ref.shape[0]
    cols = rim_ref.shape[1]
    first, length, total = place[0], place[1], place[2]
    glu_ref[EDGE : frames - EDGE] = glu_in_ref[EDGE : frames - EDGE]
    out_rows = jnp.concatenate([before_ref[:EDGE], after_ref[:EDGE]], axis=0)
    pre_rows = jnp.concatenate([before_ref[EDGE:, :cols], after_ref[EDGE:, :cols]], axis=0)
    arrived = pre_grad(out_rows, pre_rows, proj_ref[...])[0].astype(FULL)
    above = jnp.where(first > 0, arrived[:EDGE], 0.0)
    below = jnp.where(first + frames < total, arrived[EDGE:], 0.0)
    own = rim_ref[...].astype(FULL)
    taps = taps_ref[...].astype(FULL)
    pieces = []
    for rows, start, place_of in (
        (jnp.concatenate([above, own[: 2 * EDGE]], axis=0), 0, slice(0, EDGE)),
        (jnp.concatenate([own[2 * EDGE :], below], axis=0), frames - EDGE, slice(EDGE, 2 * EDGE)),
    ):
        lows = []
        for part in range(0, cols, 128):
            span = slice(part, part + 128)
            frame = lax.broadcasted_iota(jnp.int32, (EDGE, 128), 0) + (first + start)
            grad_conv = jnp.where(frame < length, conv_strip(rows[:, span], taps[:, span]), 0.0)
            lows.append(glu_grads(grad_conv, gate_ref[place_of, span], value_ref[place_of, span]))
        low = jnp.concatenate([pair[0] for pair in lows] + [pair[1] for pair in lows], axis=1)
        glu_ref[start : start + EDGE] = low
        pieces.append(low)
    low = jnp.concatenate(pieces, axis=0)
    part_ref[...] = (dot_nt(low[:, :cols], glu_w_ref[0]) + dot_nt(low[:, cols:], glu_w_ref[1])).astype(LOW)


def rim(place, before, after, rim_rows, gate, value, proj, glu_weight, taps, glu_low):
    edge = pl.BlockSpec((2 * EDGE, before.shape[1]), lambda i: (WIN // (2 * EDGE), 0))
    wide = glu_weight.shape[1]
    return call(
        rim_kernel, "rim",
        (place, before, after, rim_rows, gate, value, proj, glu_weight, taps, glu_low),
        [SMEM, edge, edge, whole(rim_rows), whole(gate), whole(value), VMEM, VMEM, whole(taps), VMEM],
        [shape((2 * EDGE, wide)), shape(glu_low.shape)],
        out_specs=[pl.BlockSpec((2 * EDGE, wide), lambda i: (0, 0)), VMEM],
        grid=(1,), micros=0.1,
    )


def terms_kernel(keeps, place, input_ref, glu_ref, out_ref, act_ref, *refs):
    core = place[3]
    cols = act_ref.shape[1]
    rows = input_ref.shape[1] // 4
    peers = 4
    sources = ((input_ref, glu_ref, 0), (input_ref, glu_ref, cols), (out_ref, act_ref, 0))
    for half in range(2):
        block = 2 * half + (core if keeps else 1 - core)
        span = pl.ds(pl.multiple_of(block * rows, rows), rows)
        for which, (source, low, start) in enumerate(sources):
            left = source[:, span]
            for part in range(0, cols, 256):
                term = dot_tn(left, low[:, start + part : start + part + 256])
                at = slice(part, part + 256)
                if not keeps:
                    refs[which][half, :, at] = term.astype(LOW)
                    continue
                term = term + refs[which][half, :, at].astype(FULL)
                at = slice(cols * which + part, cols * which + part + 256)
                for peer, moved in enumerate(by_peer(term, peers)):
                    refs[3][half, peer, :, at] = moved.astype(LOW)


def terms(place, input_rows, glu_low, out_rows, activated, arrived=()):
    wide, cols = input_rows.shape[1], activated.shape[1]
    out_shape = [shape((2, 4, wide // 16, 3 * cols))] if arrived else [shape((2, wide // 4, cols))] * 3
    operands = (place, input_rows, glu_low, out_rows, activated) + tuple(arrived)
    return call(
        functools.partial(terms_kernel, bool(arrived)), "terms",
        operands, [SMEM] + [VMEM] * (len(operands) - 1), out_shape, micros=0.1,
    )


def resid_kernel(
    place, out_ref, mid_ref, far_mid_ref, part_ref, far_part_ref, weight_ref, attended_ref,
    resid_ref, grad_ref, send_ref, keep_ref,
):
    frames = out_ref.shape[0]
    first, length, core = place[0], place[1], place[3]
    inner = frames - EDGE

    def total(rows, own, far):
        resid_ref[rows] = (out_ref[rows].astype(FULL) + (own.astype(FULL) + far.astype(FULL))).astype(LOW)

    total(slice(0, EDGE), part_ref[:EDGE], far_part_ref[:EDGE])
    total(slice(EDGE, inner), mid_ref[...], far_mid_ref[...])
    total(slice(inner, frames), part_ref[EDGE:], far_part_ref[EDGE:])
    rows = send_ref.shape[1]
    for out, flip in ((send_ref, 1), (keep_ref, 0)):
        for half in range(2):
            block = 2 * half + (1 - core if flip else core)
            span = pl.ds(pl.multiple_of(block * rows, rows), rows)
            out[half] = dot_tn(resid_ref[:, span], attended_ref[...]).astype(LOW)
    frame = lax.broadcasted_iota(jnp.int32, grad_ref.shape, 0) + first
    grad = dot_nt(resid_ref[...], weight_ref[...])
    grad_ref[...] = jnp.where(frame < length, grad, 0.0).astype(LOW)


def resid(place, out_rows, mid, far_mid, part, far_part, weight, attended):
    frames, wide = out_rows.shape
    cols = attended.shape[1]
    return call(
        resid_kernel, "resid",
        (place, out_rows, mid, far_mid, part, far_part, weight, attended),
        [SMEM] + [whole(a) for a in (out_rows, mid, far_mid, part, far_part, weight, attended)],
        [shape((frames, wide)), shape((frames, cols))] + [shape((2, wide // 4, cols))] * 2,
        out_specs=[whole(a) for a in (out_rows, attended)]
        + [pl.BlockSpec((2, wide // 4, cols), lambda i: (0, 0, 0))] * 2,
        grid=(1,), micros=60, limit=58,
    )


def by_peer(rows, peers):
    groups = rows.reshape(rows.shape[0] // (8 * peers), peers, 8, rows.shape[1])
    return [groups[:, peer].reshape(-1, rows.shape[1]) for peer in range(peers)]


def add_kernel(own_ref, arrived_ref, sum_ref):
    for half in range(2):
        total = own_ref[half].astype(FULL) + arrived_ref[half].astype(FULL)
        for peer, rows in enumerate(by_peer(total, sum_ref.shape[1])):
            sum_ref[half, peer] = rows.astype(LOW)


def add(own, arrived, peers):
    halves, rows, cols = own.shape
    return call(add_kernel, "add", (own, arrived), [VMEM, VMEM], [shape((halves, peers, rows // peers, cols))])[0]


def plane_kernel(*refs):
    *sources, sum_ref = refs
    at = 0
    for parts_ref in sources:
        for start in range(0, parts_ref.shape[2], 512):
            span = slice(start, start + 512)
            total = parts_ref[0, :, span].astype(FULL)
            for i in range(1, parts_ref.shape[0]):
                total = total + parts_ref[i, :, span].astype(FULL)
            sum_ref[:, at : at + 512] = total.astype(LOW)
            at += 512


def plane_sum(*parts):
    dims = (parts[0].shape[1], sum(part.shape[2] for part in parts))
    return call(plane_kernel, "plane_sum", parts, [VMEM] * len(parts), [shape(dims)])[0]


def line_kernel(parts_ref, out_ref, glu_ref, proj_ref):
    total = parts_ref[0].astype(FULL)
    for i in range(1, parts_ref.shape[0]):
        total = total + parts_ref[i].astype(FULL)
    cols = out_ref.shape[1]
    glu_ref[0] = total[:, :cols].astype(LOW)
    glu_ref[1] = total[:, cols : 2 * cols].astype(LOW)
    proj_ref[...] = total[:, 2 * cols : 3 * cols].astype(LOW)
    out_ref[...] = total[:, 3 * cols :].astype(LOW)


def line_sum(parts):
    rows, cols = parts.shape[1], parts.shape[2] // 4
    return call(
        line_kernel, "line_sum", (parts,), [VMEM], [shape((rows, cols)), shape((2, rows, cols)), shape((rows, cols))]
    )


def exchanged(parts, groups):
    return lax.all_to_all(parts, ("dp", "seq"), 0, 0, axis_index_groups=groups)


BLOCK = 128
SPAN = BLOCK + 2 * WIN
SCALE = HEAD_DIM**-0.5
PAIR = 2 * HEAD_DIM


def side_by_side(rows):
    lane = lax.broadcasted_iota(jnp.int32, rows.shape, 1)
    zero = jnp.zeros_like(rows)
    return jnp.concatenate(
        [jnp.where(lane < HEAD_DIM, rows, zero), jnp.where(lane < HEAD_DIM, zero, rows)], axis=0
    )


def own_columns(columns):
    return jnp.concatenate([columns[:HEAD_DIM, :BLOCK], columns[HEAD_DIM:, BLOCK:]], axis=0)


def gather_rows(whole, before_ref, own_ref, after_ref):
    frames = own_ref.shape[0]
    whole[:WIN] = before_ref[...]
    whole[WIN : WIN + frames] = own_ref[...]
    whole[WIN + frames :] = after_ref[...]


def pair_specs(frames, pairs):
    own = pl.BlockSpec((frames, PAIR), lambda i: (0, i))
    far_key = pl.BlockSpec((WIN, PAIR), lambda i: (0, i))
    far_value = pl.BlockSpec((WIN, PAIR), lambda i: (0, i + pairs))
    return own, far_key, far_value


def attend_kernel(
    place, q_ref, k_ref, v_ref, kb_ref, vb_ref, ka_ref, va_ref, prob_ref, out_ref, fill, keys, values
):
    first, length = place[0], place[1]
    frames = q_ref.shape[0]

    @pl.when(pl.program_id(0) == 0)
    def _():
        for block in range(frames // BLOCK):
            key = lax.broadcasted_iota(jnp.int32, (SPAN, BLOCK), 0)
            offset = key - lax.broadcasted_iota(jnp.int32, (SPAN, BLOCK), 1)
            frame = key + (first - WIN + block * BLOCK)
            allowed = (offset >= 0) & (offset <= 2 * WIN) & (frame >= 0) & (frame < length)
            fill[block] = jnp.where(allowed, 0.0, NEG_FILL)

    gather_rows(keys, kb_ref, k_ref, ka_ref)
    gather_rows(values, vb_ref, v_ref, va_ref)
    for block in range(frames // BLOCK):
        rows = slice(block * BLOCK, (block + 1) * BLOCK)
        span = slice(block * BLOCK, block * BLOCK + SPAN)
        queries = side_by_side(q_ref[rows] * SCALE)
        scores = dot_nt(keys[span], queries) + jnp.concatenate([fill[block], fill[block]], axis=1)
        exponent = jnp.exp(scores - jnp.max(scores, axis=0, keepdims=True))
        prob = exponent * (1.0 / jnp.sum(exponent, axis=0, keepdims=True))
        prob_low = prob.astype(LOW)
        prob_ref[0, block] = prob_low
        summed = own_columns(dot_tn(values[span], prob_low))
        frame = lax.broadcasted_iota(jnp.int32, (1, BLOCK), 1) + (first + block * BLOCK)
        out_ref[rows] = jnp.where(frame < length, summed, 0.0).T.astype(LOW)


def attend_grad_kernel(
    q_ref, k_ref, v_ref, kb_ref, vb_ref, ka_ref, va_ref, prob_ref, out_ref, grad_ref,
    dq_ref, dk_ref, dv_ref, to_before_ref, to_after_ref, keys, values, key_sum, value_sum,
):
    frames = q_ref.shape[0]
    gather_rows(keys, kb_ref, k_ref, ka_ref)
    gather_rows(values, vb_ref, v_ref, va_ref)
    key_sum[...] = jnp.zeros_like(key_sum)
    value_sum[...] = jnp.zeros_like(value_sum)
    for block in range(frames // BLOCK):
        rows = slice(block * BLOCK, (block + 1) * BLOCK)
        span = slice(block * BLOCK, block * BLOCK + SPAN)
        queries = side_by_side(q_ref[rows] * SCALE)
        grad_rows = grad_ref[rows]
        grads = side_by_side(grad_rows)
        product = (grad_rows.astype(FULL) * out_ref[rows].astype(FULL)).T
        row_delta = jnp.concatenate(
            [
                jnp.sum(product[:HEAD_DIM], axis=0, keepdims=True),
                jnp.sum(product[HEAD_DIM:], axis=0, keepdims=True),
            ],
            axis=1,
        )
        prob_low = prob_ref[0, block]
        grad_prob = dot_nt(values[span], grads)
        grad_score = (prob_low.astype(FULL) * (grad_prob - row_delta)).astype(LOW)
        value_sum[span] += jnp.dot(prob_low, grads, preferred_element_type=FULL)
        key_sum[span] += jnp.dot(grad_score, queries, preferred_element_type=FULL)
        dq_ref[rows] = (own_columns(dot_tn(keys[span], grad_score)).T * SCALE).astype(LOW)
    for total, inner, lane in ((key_sum, dk_ref, 0), (value_sum, dv_ref, PAIR)):
        to_before_ref[:, lane : lane + PAIR] = total[:WIN].astype(LOW)
        inner[...] = total[WIN : WIN + frames]
        to_after_ref[:, lane : lane + PAIR] = total[WIN + frames :].astype(LOW)


def attend(place, q_rows, k_rows, v_rows, before, after):
    frames, cols = q_rows.shape
    pairs, blocks = cols // PAIR, frames // BLOCK
    own, far_key, far_value = pair_specs(frames, pairs)
    return call(
        attend_kernel, "attend", (place, q_rows, k_rows, v_rows, before, before, after, after),
        [SMEM, own, own, own, far_key, far_value, far_key, far_value],
        [shape((pairs, blocks, SPAN, 2 * BLOCK)), shape((frames, cols))],
        out_specs=[pl.BlockSpec((1, blocks, SPAN, 2 * BLOCK), lambda i: (i, 0, 0, 0)), own],
        scratch=[pltpu.VMEM((blocks, SPAN, BLOCK), FULL)] + [pltpu.VMEM((frames + 2 * WIN, PAIR), LOW)] * 2,
        grid=(pairs,), micros=0.5, limit=58,
    )


def attend_grad(q_rows, k_rows, v_rows, before, after, prob, attended, grad_attn):
    frames, cols = q_rows.shape
    pairs, blocks = cols // PAIR, frames // BLOCK
    own, far_key, far_value = pair_specs(frames, pairs)
    far = pl.BlockSpec((WIN, 2 * PAIR), lambda i: (0, i))
    return call(
        attend_grad_kernel, "attend_grad",
        (q_rows, k_rows, v_rows, before, before, after, after, prob, attended, grad_attn),
        [own, own, own, far_key, far_value, far_key, far_value]
        + [pl.BlockSpec((1, blocks, SPAN, 2 * BLOCK), lambda i: (i, 0, 0, 0)), own, own],
        [shape((frames, cols))] + [shape((frames, cols), FULL)] * 2 + [shape((WIN, 2 * cols))] * 2,
        out_specs=[own, own, own, far, far],
        scratch=[pltpu.VMEM((frames + 2 * WIN, PAIR), LOW)] * 2 + [pltpu.VMEM((frames + 2 * WIN, PAIR), FULL)] * 2,
        grid=(pairs,), micros=50, limit=58,
    )


def finish_kernel(dk_ref, dv_ref, from_before_ref, from_after_ref, key_ref, value_ref):
    frames, cols = dk_ref.shape
    shared = frames - WIN
    for own, out, lane in ((dk_ref, key_ref, 0), (dv_ref, value_ref, PAIR)):
        for start in range(0, cols, PAIR):
            span = slice(start, start + PAIR)
            far_span = slice(2 * start + lane, 2 * start + lane + PAIR)
            above = own[:WIN, span] + from_before_ref[:, far_span].astype(FULL)
            far = from_after_ref[:, far_span].astype(FULL)
            out[:shared, span] = above[:shared].astype(LOW)
            out[shared:WIN, span] = (above[shared:] + far[: WIN - shared]).astype(LOW)
            out[WIN:, span] = (own[WIN:, span] + far[WIN - shared :]).astype(LOW)


def finish(grad_key, grad_value, from_before, from_after):
    own = pl.BlockSpec(grad_key.shape, lambda i: (0, 0))
    far = pl.BlockSpec(from_before.shape, lambda i: (0, 0))
    return call(
        finish_kernel, "finish", (grad_key, grad_value, from_before, from_after), [own, own, far, far],
        [shape(grad_key.shape)] * 2, out_specs=[own, own], grid=(1,), micros=2, limit=58,
    )


def local(
    lengths,
    query_act,
    key_act,
    value_act,
    conv_input,
    conv_result,
    out_grad,
    out_weight,
    glu_weight,
    conv_taps,
    proj_weight,
):
    q_rows, k_rows, v_rows = (query_act[0], key_act[0], value_act[0])
    input_rows, pre_rows, out_rows = (conv_input[0], conv_result[0], out_grad[0])
    frames, cols = q_rows.shape
    peers = lax.axis_size("seq")
    index = lax.axis_index("dp")
    first = lax.axis_index("seq") * frames
    place = jnp.stack([first, lengths[0], peers * frames, index % 2, index // 2]).astype(jnp.int32)

    up, down = pack(k_rows, v_rows, out_rows, pre_rows)
    before, after = (round_ring(up, 1), round_ring(down, -1))
    mid, glu_low, activated, rim_rows, rim_gate, rim_value = front(
        place, out_rows, pre_rows, proj_weight, input_rows, glu_weight, conv_taps
    )
    far_mid = swapped(mid, "tensor", 1)
    part, glu_low = rim(
        place, before, after, rim_rows, rim_gate, rim_value, proj_weight, glu_weight, conv_taps, glu_low
    )
    far_part = swapped(part, "tensor", 1)
    given = [swapped(term, "dp", 1) for term in terms(place, input_rows, glu_low, out_rows, activated)]
    on_chip = terms(place, input_rows, glu_low, out_rows, activated, given)[0]
    q_late, on_chip = lax.optimization_barrier((q_rows, on_chip))
    prob, attended = attend(place, q_late, k_rows, v_rows, before, after)
    resid_low, grad_attn, out_send, out_keep = resid(
        place, out_rows, mid, far_mid, part, far_part, out_weight, attended
    )
    xs, zs, pairs, cores = (4, peers // 4, range(2), range(2))
    by_plane = [
        [(2 * y + core) * peers + z * xs + x for y in pairs for x in range(xs)]
        for core in cores for z in range(zs)
    ]
    by_line = [[d * peers + z * xs + x for z in range(zs)] for d in range(4) for x in range(xs)]
    rest = exchanged(on_chip.reshape((2 * xs,) + on_chip.shape[2:]), by_plane)
    on_chip_out = add(out_keep, swapped(out_send, "dp", 1), xs)
    on_chip_out, rest = lax.optimization_barrier((on_chip_out, rest))
    outs = exchanged(on_chip_out.reshape((2 * xs,) + on_chip_out.shape[2:]), by_plane)
    plane = plane_sum(rest, outs)
    out_sum, glu_sum, proj_sum = line_sum(exchanged(plane.reshape(zs, -1, plane.shape[1]), by_line))
    grad_query, grad_key, grad_value, to_before, to_after = attend_grad(
        q_rows, k_rows, v_rows, before, after, prob, attended, grad_attn
    )
    from_after, from_before = (round_ring(to_before, -1), round_ring(to_after, 1))

    key_grad, value_grad = finish(grad_key, grad_value, from_before, from_after)
    return (
        resid_low[None],
        grad_query[None],
        key_grad[None],
        value_grad[None],
        out_sum.T,
        glu_sum,
        proj_sum.T,
    )


def solution(mesh):
    in_specs = (
        P("dp"),
        P("dp", "seq", "tensor"),
        P("dp", "seq", "tensor"),
        P("dp", "seq", "tensor"),
        P("dp", "seq", None),
        P("dp", "seq", "tensor"),
        P("dp", "seq", None),
        P("tensor", None),
        P(None, None, "tensor"),
        P(None, "tensor"),
        P("tensor", None),
    )
    out_specs = (
        P("dp", "seq", None),
        P("dp", "seq", "tensor"),
        P("dp", "seq", "tensor"),
        P("dp", "seq", "tensor"),
        P("tensor", ("dp", "seq")),
        P(None, ("dp", "seq"), "tensor"),
        P("tensor", ("dp", "seq")),
    )
    return jax.shard_map(local, mesh=mesh, in_specs=in_specs, out_specs=out_specs, check_vma=False)
```

time: 137 us -> 101 us (0.74)
  the two profiles are of different devices: /device:TPU:1 before, /device:TPU:32 now
where the time goes in v3:
time: 101 us; the launch traced here: 100 us
  Pallas kernels  44 us (44%)
  starting transfers between devices  34 us (34%)
  waiting for transfers between devices  14.9 us (15%)
  local copies, waits for them, and re-layouts  5.86 us (6%)
  between operations  1.43 us (1%)
    pallas_call x12, Pallas kernels, call(): pl.pallas_call(kernel, in_specs=in_specs, out_specs=[VMEM] * len(out_shap...  44 us
    all_to_all x3, starting transfers between devices, exchanged(): return lax.all_to_all(parts, ('dp', 'seq'), 0, 0, axis_index_groups=groups)  17.1 us
    ppermute x4, starting transfers between devices, round_ring(): lax.ppermute(value, 'seq', [(i, (i + steps) % count) for i in range(count)])  11.3 us
    all_to_all x3, waiting for transfers between devices, exchanged(): return lax.all_to_all(parts, ('dp', 'seq'), 0, 0, axis_index_groups=groups)  7.49 us
    unnamed x28, local copies, waits for them, and re-layouts  5.77 us
    ppermute x6, starting transfers between devices, swapped(): return lax.ppermute(value, axis, [(i, i ^ stride) for i in range(count)])  5.67 us
    ppermute x4, waiting for transfers between devices, round_ring(): lax.ppermute(value, 'seq', [(i, (i + steps) % count) for i in range(count)])  4.15 us
    ppermute x6, waiting for transfers between devices, swapped(): return lax.ppermute(value, axis, [(i, i ^ stride) for i in range(count)])  3.22 us
  transfers between devices with their start and end apart: 13, of which 7 were waited for; matrix products, arithmetic and copies ran while one was open for 0% of the time, Pallas kernels for 41%

profile of v3, /device:TPU:32, one launch (start us, length us, event | category | flops | bytes accessed | tf_op | source)
XLA Modules:
  0.0 100.1 jit_solution(17315197438011894523)
XLA Ops:
  0.7 2.4 %pack.1 = (bf16[288,1024]{1,0:T(8,128)(2,1)}, bf16[288,1024]{1,0:T(8,128)(2,1)}) custom-call(bf16[384,512]{1,0:T(8,128)(2,1)} %bitcast.28, bf16[384,512]{1,0:T(8,128)(2,1)} %bitcast.31, bf16[384,1024]{1,0:T(8,128)(2,1)} %bitcast.21, bf16[384,512]{1,0:T(8,128)(2,1)} %bitcast.26), custom_call_target="tpu_custom_call" | custom-call | flops 900000000 | bytes 1 | tf_op jit(solution)/shard_map/pack/pallas_call | solution.py:29
  3.1 1.6 %collective-permute-start.1 = (bf16[288,1024]{1,0:T(8,128)(2,1)}, bf16[288,1024]{1,0:T(8,128)(2,1)S(1)}, u32[]{:S(2)}, u32[]{:S(2)}) collective-permute-start(bf16[288,1024]{1,0:T(8,128)(2,1)} %get-tuple-element.41), channel_id=1, source_target_pairs={{0,2},{2,4},{4,6},{6,8},{8,10},{10,12},{12,14},{14,16},{16,18},{18... | collective-permute-start | bytes 1769480 | tf_op jit(solution)/shard_map/ppermute | solution.py:56
  4.6 2.6 %collective-permute-start.2 = (bf16[288,1024]{1,0:T(8,128)(2,1)}, bf16[288,1024]{1,0:T(8,128)(2,1)S(1)}, u32[]{:S(2)}, u32[]{:S(2)}) collective-permute-start(bf16[288,1024]{1,0:T(8,128)(2,1)} %get-tuple-element.42), channel_id=1, source_target_pairs={{0,62},{2,0},{4,2},{6,4},{8,6},{10,8},{12,10},{14,12},{16,14},{18,... | collective-permute-start | bytes 1769480 | tf_op jit(solution)/shard_map/ppermute | solution.py:56
  8.1 1.6 %copy-done.4 = bf16[2,1024,512]{2,1,0:T(8,128)(2,1)S(1)} copy-done((bf16[2,1024,512]{2,1,0:T(8,128)(2,1)S(1)}, bf16[2,1024,512]{2,1,0:T(8,128)(2,1)}, u32[]{:S(2)}) %copy-start.4) | copy-done | bytes 2097176
  9.6 1.2 %copy-done.6 = bf16[512,1024]{1,0:T(8,128)(2,1)S(1)} copy-done((bf16[512,1024]{1,0:T(8,128)(2,1)S(1)}, bf16[512,1024]{1,0:T(8,128)(2,1)}, u32[]{:S(2)}) %copy-start.6) | copy-done | bytes 1048600
  10.9 1.0 copy-done.10
  11.9 6.9 %front.1 = (bf16[352,1024]{1,0:T(8,128)(2,1)S(1)}, bf16[384,1024]{1,0:T(8,128)(2,1)S(1)}, bf16[384,512]{1,0:T(8,128)(2,1)S(1)}, bf16[64,512]{1,0:T(8,128)(2,1)S(...) custom-call(s32[5]{0:T(128)S(1)} %stack.15.place, bf16[384,1024]{1,0:T(8,128)(2,1)S(1)} %bitcast.23, ...), custom_call_target="tpu_custom_call" | custom-call | flops 6300000256 | bytes 1 | tf_op jit(solution)/shard_map/front/pallas_call | solution.py:29
  18.7 3.3 %collective-permute-start = (bf16[352,1024]{1,0:T(8,128)(2,1)S(1)}, bf16[352,1024]{1,0:T(8,128)(2,1)}, u32[]{:S(2)}, u32[]{:S(2)}) collective-permute-start(bf16[352,1024]{1,0:T(8,128)(2,1)S(1)} %get-tuple-element.40.mid_ref), channel_id=1, source_target_pairs={{0,1},{1,0},{2,3},{3,2},{4,5},{5,4},{6,7},{7,6},{8,9},{9,8},{10,11... | collective-permute-start | bytes 2162696 | tf_op jit(solution)/shard_map/ppermute | solution.py:61
  22.1 2.5 %rim.1 = (bf16[32,1024]{1,0:T(8,128)(2,1)}, bf16[384,1024]{1,0:T(8,128)(2,1)S(1)}) custom-call(s32[5]{0:T(128)S(1)} %stack.15.place, bf16[288,1024]{1,0:T(8,128)(2,1)S(1)} %collective-permute-done.1.before_ref.kb_ref.vb_ref, bf16[288,1024]{1,0:T(8,128)(2,1)S(1)} %collective-permute-done.2.after_ref.ka_ref.va_ref, ...), custom_call_target="tpu_custom_call" | custom-call | flops 90000000 | bytes 1 | tf_op jit(solution)/shard_map/rim/pallas_call | solution.py:29
  24.6 1.6 %terms.2 = (bf16[2,256,512]{2,1,0:T(8,128)(2,1)S(1)}, bf16[2,256,512]{2,1,0:T(8,128)(2,1)S(1)}, bf16[2,256,512]{2,1,0:T(8,128)(2,1)S(1)}) custom-call(s32[5]{0:T(128)S(1)} %stack.15.place, bf16[384,1024]{1,0:T(8,128)(2,1)S(1)} %bitcast.19, bf16[384,1024]{1,0:T(8,128)(2,1)S(1)} %get-tuple-element.48.glu_ref, bf16[384,1024]{1,0:T(8,128)(2,1)S(1)} %bitcast.24, ...), custom_call_target="tpu_custom_call" | custom-call | flops 90000000 | bytes 1 | tf_op jit(solution)/shard_map/terms/pallas_call | solution.py:29
  26.3 0.5 collective-permute-start.5
  26.9 1.7 %collective-permute-start.3 = (bf16[32,1024]{1,0:T(8,128)(2,1)}, bf16[32,1024]{1,0:T(8,128)(2,1)}, u32[]{:S(2)}, u32[]{:S(2)}) collective-permute-start(bf16[32,1024]{1,0:T(8,128)(2,1)} %get-tuple-element.47.part_ref), channel_id=1, source_target_pairs={{0,1},{1,0},{2,3},{3,2},{4,5},{5,4},{6,7},{7,6},{8,9},{9,8},{10,11... | collective-permute-start | bytes 196616 | tf_op jit(solution)/shard_map/ppermute | solution.py:61
  28.9 0.7 collective-permute-done.6.refs_2_
  29.7 2.8 %terms.3 = bf16[2,4,64,1536]{3,2,1,0:T(8,128)(2,1)} custom-call(s32[5]{0:T(128)S(1)} %stack.15.place, bf16[384,1024]{1,0:T(8,128)(2,1)S(1)} %bitcast.20, bf16[384,1024]{1,0:T(8,128)(2,1)S(1)} %get-tuple-element.48.glu_ref, bf16[384,1024]{1,0:T(8,128)(2,1)S(1)} %bitcast.25, bf16[384,512]{1,0:T(8,128)(2,1)S(1)} %get-tuple-element.49.act_ref, ...), custom_call_target="tpu_custom_call" | custom-call | flops 90000000 | bytes 1 | tf_op jit(solution)/shard_map/terms/pallas_call | solution.py:29
  32.4 5.1 %all-to-all-start = ((bf16[8,64,1536]{2,1,0:T(8,128)(2,1)}), bf16[8,64,1536]{2,1,0:T(8,128)(2,1)S(1)}, u32[]{:S(2)}, u32[]{:S(2)}) async-start(bf16[8,64,1536]{2,1,0:T(8,128)(2,1)} %bitcast.13), calls=%async_computation | async-start | bytes 3145728 | tf_op jit(solution)/shard_map/all_to_all | solution.py:356
  37.5 10.1 %attend.1 = (bf16[4,3,640,256]{3,2,1,0:T(8,128)(2,1)}, bf16[384,512]{1,0:T(8,128)(2,1)}) custom-call(s32[5]{0:T(128)} %copy-done.8, bf16[384,512]{1,0:T(8,128)(2,1)} %bitcast.34, bf16[384,512]{1,0:T(8,128)(2,1)} %bitcast.29, bf16[384,512]{1,0:T(8,128)(2,1)} %bitcast.32, bf16[288,1024]{1,0:T(8,128)(2,1)} %copy-done, bf16[288,1024]{1,0:T(8,128)(2,1)} %copy-done, ...), custom_call_target="tpu_custom_call" | custom-call | flops 450000000 | bytes 1 | tf_op jit(solution)/shard_map/attend/pallas_call | solution.py:29
  47.6 4.7 %resid.1 = (bf16[384,1024]{1,0:T(8,128)(2,1)}, bf16[384,512]{1,0:T(8,128)(2,1)}, bf16[2,256,512]{2,1,0:T(8,128)(2,1)}, bf16[2,256,512]{2,1,0:T(8,128)(2,1)}) custom-call(s32[5]{0:T(128)} %copy-done.8, bf16[384,1024]{1,0:T(8,128)(2,1)} %bitcast.22, bf16[352,1024]{1,0:T(8,128)(2,1)} %copy-done.9, bf16[352,1024]{1,0:T(8,128)(2,1)} %collective-permute-done.far_mid_ref, ...), custom_call_target="tpu_custom_call" | custom-call | flops 54000001024 | bytes 1 | tf_op jit(solution)/shard_map/resid/pallas_call | solution.py:29
  52.3 2.1 %collective-permute-done.9.arrived_ref = bf16[2,256,512]{2,1,0:T(8,128)(2,1)S(1)} collective-permute-done((bf16[2,256,512]{2,1,0:T(8,128)(2,1)}, bf16[2,256,512]{2,1,0:T(8,128)(2,1)S(1)}, u32[]{:S(2)}, u32[]{:S(2)}) %collective-permute-start.9) | collective-permute-done | bytes 524320 | tf_op jit(solution)/shard_map/ppermute | solution.py:61
  54.5 1.0 %copy-done.11 = bf16[2,256,512]{2,1,0:T(8,128)(2,1)S(1)} copy-done((bf16[2,256,512]{2,1,0:T(8,128)(2,1)S(1)}, bf16[2,256,512]{2,1,0:T(8,128)(2,1)}, u32[]{:S(2)}) %copy-start.11) | copy-done | bytes 524312
  55.5 1.0 add.7
  56.5 2.7 %all-to-all-done.refs_0_ = bf16[8,64,1536]{2,1,0:T(8,128)(2,1)S(1)} async-done(((bf16[8,64,1536]{2,1,0:T(8,128)(2,1)}), bf16[8,64,1536]{2,1,0:T(8,128)(2,1)S(1)}, u32[]{:S(2)}, u32[]{:S(2)}) %all-to-all-start) | async-done | bytes 1572896 | tf_op jit(solution)/shard_map/all_to_all | solution.py:356
  59.1 3.7 %all-to-all-start.1 = ((bf16[8,64,512]{2,1,0:T(8,128)(2,1)}), bf16[8,64,512]{2,1,0:T(8,128)(2,1)S(1)}, u32[]{:S(2)}, u32[]{:S(2)}) async-start(bf16[8,64,512]{2,1,0:T(8,128)(2,1)} %bitcast.14), calls=%async_computation.1 | async-start | bytes 1048576 | tf_op jit(solution)/shard_map/all_to_all | solution.py:356
  62.9 7.7 %attend_grad.1 = (bf16[384,512]{1,0:T(8,128)(2,1)}, f32[384,512]{1,0:T(8,128)}, f32[384,512]{1,0:T(8,128)}, bf16[256,1024]{1,0:T(8,128)(2,1)}, bf16[256,1024]{1,0:T(8,128)(2,1)}) custom-call(bf16[384,512]{1,0:T(8,128)(2,1)} %bitcast.35, bf16[384,512]{1,0:T(8,128)(2,1)} %bitcast.30, bf16[384,512]{1,0:T(8,128)(2,1)} %bitcast.33, bf16[288,1024]{1,0:T(8,128)(2,1)} %copy-done, ...), custom_call_target="tpu_custom_call" | custom-call | flops 44999999488 | bytes 1 | tf_op jit(solution)/shard_map/attend_grad/pallas_call | solution.py:29
  70.6 2.1 %collective-permute-start.7 = (bf16[256,1024]{1,0:T(8,128)(2,1)}, bf16[256,1024]{1,0:T(8,128)(2,1)S(1)}, u32[]{:S(2)}, u32[]{:S(2)}) collective-permute-start(bf16[256,1024]{1,0:T(8,128)(2,1)} %get-tuple-element.61), channel_id=1, source_target_pairs={{0,2},{2,4},{4,6},{6,8},{8,10},{10,12},{12,14},{14,16},{16,18},{18... | collective-permute-start | bytes 1572872 | tf_op jit(solution)/shard_map/ppermute | solution.py:56
  72.7 4.9 %collective-permute-start.8 = (bf16[256,1024]{1,0:T(8,128)(2,1)}, bf16[256,1024]{1,0:T(8,128)(2,1)S(1)}, u32[]{:S(2)}, u32[]{:S(2)}) collective-permute-start(bf16[256,1024]{1,0:T(8,128)(2,1)} %get-tuple-element.62), channel_id=1, source_target_pairs={{0,62},{2,0},{4,2},{6,4},{8,6},{10,8},{12,10},{14,12},{16,14},{18,... | collective-permute-start | bytes 1572872 | tf_op jit(solution)/shard_map/ppermute | solution.py:56
  77.6 1.0 plane_sum.1
  78.6 8.3 %all-to-all-start.2 = ((bf16[8,8,2048]{2,1,0:T(8,128)(2,1)}), bf16[8,8,2048]{2,1,0:T(8,128)(2,1)S(1)}, u32[]{:S(2)}, u32[]{:S(2)}) async-start(bf16[8,8,2048]{2,1,0:T(8,128)(2,1)} %bitcast.15), calls=%async_computation.2 | async-start | bytes 524288 | tf_op jit(solution)/shard_map/all_to_all | solution.py:356
  86.9 4.1 %collective-permute-done.7.from_before_ref = bf16[256,1024]{1,0:T(8,128)(2,1)S(1)} collective-permute-done((bf16[256,1024]{1,0:T(8,128)(2,1)}, bf16[256,1024]{1,0:T(8,128)(2,1)S(1)}, u32[]{:S(2)}, u32[]{:S(2)}) %collective-permute-start.7) | collective-permute-done | bytes 524320 | tf_op jit(solution)/shard_map/ppermute | solution.py:56
  91.0 0.7 copy-done.12
  91.9 2.7 %finish.1 = (bf16[384,512]{1,0:T(8,128)(2,1)}, bf16[384,512]{1,0:T(8,128)(2,1)}) custom-call(f32[384,512]{1,0:T(8,128)} %get-tuple-element.59.dk_ref, f32[384,512]{1,0:T(8,128)} %get-tuple-element.60.dv_ref, bf16[256,1024]{1,0:T(8,128)(2,1)} %copy-done.12, bf16[256,1024]{1,0:T(8,128)(2,1)} %copy-done.13), custom_call_target="tpu_custom_call" | custom-call | flops 1800000000 | bytes 1 | tf_op jit(solution)/shard_map/finish/pallas_call | solution.py:29
  94.7 4.8 %all-to-all-done.2.parts_ref = bf16[8,8,2048]{2,1,0:T(8,128)(2,1)S(1)} async-done(((bf16[8,8,2048]{2,1,0:T(8,128)(2,1)}), bf16[8,8,2048]{2,1,0:T(8,128)(2,1)S(1)}, u32[]{:S(2)}, u32[]{:S(2)}) %all-to-all-start.2) | async-done | bytes 262176 | tf_op jit(solution)/shard_map/all_to_all | solution.py:356
  99.5 0.6 line_sum.1
  (35 shorter events, 0.9 us)
Async XLA Ops:
  0.6 7.4 %copy-start.3 = (bf16[1,384,1024]{2,1,0:T(8,128)(2,1)S(1)}, bf16[1,384,1024]{2,1,0:T(8,128)(2,1)}, u32[]{:S(2)}) copy-start(bf16[1,384,1024]{2,1,0:T(8,128)(2,1)} %param.17) | copy-start | bytes 2359300
  0.6 7.4 %copy-start.2 = (bf16[1,384,1024]{2,1,0:T(8,128)(2,1)S(1)}, bf16[1,384,1024]{2,1,0:T(8,128)(2,1)}, u32[]{:S(2)}) copy-start(bf16[1,384,1024]{2,1,0:T(8,128)(2,1)} %param.15) | copy-start | bytes 2359300
  0.7 7.4 %copy-start.7 = (bf16[31,512]{1,0:T(8,128)(2,1)S(1)}, bf16[31,512]{1,0:T(8,128)(2,1)}, u32[]{:S(2)}) copy-start(bf16[31,512]{1,0:T(8,128)(2,1)} %taps_ref.3) | copy-start | bytes 95236
  3.1 18.9 %collective-permute-start.1 = (bf16[288,1024]{1,0:T(8,128)(2,1)}, bf16[288,1024]{1,0:T(8,128)(2,1)S(1)}, u32[]{:S(2)}, u32[]{:S(2)}) collective-permute-start(bf16[288,1024]{1,0:T(8,128)(2,1)} %get-tuple-element.41), channel_id=1, source_target_pairs={{0,2},{2,4},{4,6},{6,8},{8,10},{10,12},{12,14},{14,16},{16,18},{18... | collective-permute-start | bytes 1769480 | tf_op jit(solution)/shard_map/ppermute | solution.py:56
  4.6 17.4 %collective-permute-start.2 = (bf16[288,1024]{1,0:T(8,128)(2,1)}, bf16[288,1024]{1,0:T(8,128)(2,1)S(1)}, u32[]{:S(2)}, u32[]{:S(2)}) collective-permute-start(bf16[288,1024]{1,0:T(8,128)(2,1)} %get-tuple-element.42), channel_id=1, source_target_pairs={{0,62},{2,0},{4,2},{6,4},{8,6},{10,8},{12,10},{14,12},{16,14},{18,... | collective-permute-start | bytes 1769480 | tf_op jit(solution)/shard_map/ppermute | solution.py:56
  8.0 21.6 %copy-start.8 = (s32[5]{0:T(128)}, s32[5]{0:T(128)S(1)}, u32[]{:S(2)}) copy-start(s32[5]{0:T(128)S(1)} %stack.15.place) | copy-start | bytes 64
  8.1 1.6 %copy-start.4 = (bf16[2,1024,512]{2,1,0:T(8,128)(2,1)S(1)}, bf16[2,1024,512]{2,1,0:T(8,128)(2,1)}, u32[]{:S(2)}) copy-start(bf16[2,1024,512]{2,1,0:T(8,128)(2,1)} %glu_w_ref.3) | copy-start | bytes 6291460
  9.6 1.2 %copy-start.6 = (bf16[512,1024]{1,0:T(8,128)(2,1)S(1)}, bf16[512,1024]{1,0:T(8,128)(2,1)}, u32[]{:S(2)}) copy-start(bf16[512,1024]{1,0:T(8,128)(2,1)} %proj_ref.3) | copy-start | bytes 3145732
  10.9 1.0 copy-start.10
  11.9 10.2 %copy-start.5 = (bf16[2,1024,512]{2,1,0:T(8,128)(2,1)S(1)}, bf16[2,1024,512]{2,1,0:T(8,128)(2,1)}, u32[]{:S(2)}) copy-start(bf16[2,1024,512]{2,1,0:T(8,128)(2,1)} %glu_w_ref.3) | copy-start | bytes 6291460
  18.7 5.9 %copy-start.9 = (bf16[352,1024]{1,0:T(8,128)(2,1)}, bf16[352,1024]{1,0:T(8,128)(2,1)S(1)}, u32[]{:S(2)}) copy-start(bf16[352,1024]{1,0:T(8,128)(2,1)S(1)} %get-tuple-element.40.mid_ref) | copy-start | bytes 2162692
  18.7 28.9 %collective-permute-start = (bf16[352,1024]{1,0:T(8,128)(2,1)S(1)}, bf16[352,1024]{1,0:T(8,128)(2,1)}, u32[]{:S(2)}, u32[]{:S(2)}) collective-permute-start(bf16[352,1024]{1,0:T(8,128)(2,1)S(1)} %get-tuple-element.40.mid_ref), channel_id=1, source_target_pairs={{0,1},{1,0},{2,3},{3,2},{4,5},{5,4},{6,7},{7,6},{8,9},{9,8},{10,11... | collective-permute-start | bytes 2162696 | tf_op jit(solution)/shard_map/ppermute | solution.py:61
  22.0 2.6 %copy-start = (bf16[288,1024]{1,0:T(8,128)(2,1)}, bf16[288,1024]{1,0:T(8,128)(2,1)S(1)}, u32[]{:S(2)}) copy-start(bf16[288,1024]{1,0:T(8,128)(2,1)S(1)} %collective-permute-done.1.before_ref.kb_ref.vb_ref) | copy-start | bytes 1769476
  22.0 2.6 %copy-start.1 = (bf16[288,1024]{1,0:T(8,128)(2,1)}, bf16[288,1024]{1,0:T(8,128)(2,1)S(1)}, u32[]{:S(2)}) copy-start(bf16[288,1024]{1,0:T(8,128)(2,1)S(1)} %collective-permute-done.2.after_ref.ka_ref.va_ref) | copy-start | bytes 1769476
  26.2 2.4 %collective-permute-start.4 = (bf16[2,256,512]{2,1,0:T(8,128)(2,1)S(1)}, bf16[2,256,512]{2,1,0:T(8,128)(2,1)S(1)}, u32[]{:S(2)}, u32[]{:S(2)}) collective-permute-start(bf16[2,256,512]{2,1,0:T(8,128)(2,1)S(1)} %get-tuple-element.50), channel_id=1, source_target_pairs={{0,64},{64,0},{128,192},{192,128},{1,65},{65,1},{129,193},{193,129... | collective-permute-start | bytes 1572872 | tf_op jit(solution)/shard_map/ppermute | solution.py:61
  26.3 2.6 %collective-permute-start.5 = (bf16[2,256,512]{2,1,0:T(8,128)(2,1)S(1)}, bf16[2,256,512]{2,1,0:T(8,128)(2,1)S(1)}, u32[]{:S(2)}, u32[]{:S(2)}) collective-permute-start(bf16[2,256,512]{2,1,0:T(8,128)(2,1)S(1)} %get-tuple-element.51), channel_id=1, source_target_pairs={{0,64},{64,0},{128,192},{192,128},{1,65},{65,1},{129,193},{193,129... | collective-permute-start | bytes 1572872 | tf_op jit(solution)/shard_map/ppermute | solution.py:61
  26.8 2.9 %collective-permute-start.6 = (bf16[2,256,512]{2,1,0:T(8,128)(2,1)S(1)}, bf16[2,256,512]{2,1,0:T(8,128)(2,1)S(1)}, u32[]{:S(2)}, u32[]{:S(2)}) collective-permute-start(bf16[2,256,512]{2,1,0:T(8,128)(2,1)S(1)} %get-tuple-element.52), channel_id=1, source_target_pairs={{0,64},{64,0},{128,192},{192,128},{1,65},{65,1},{129,193},{193,129... | collective-permute-start | bytes 1572872 | tf_op jit(solution)/shard_map/ppermute | solution.py:61
  26.9 20.7 %collective-permute-start.3 = (bf16[32,1024]{1,0:T(8,128)(2,1)}, bf16[32,1024]{1,0:T(8,128)(2,1)}, u32[]{:S(2)}, u32[]{:S(2)}) collective-permute-start(bf16[32,1024]{1,0:T(8,128)(2,1)} %get-tuple-element.47.part_ref), channel_id=1, source_target_pairs={{0,1},{1,0},{2,3},{3,2},{4,5},{5,4},{6,7},{7,6},{8,9},{9,8},{10,11... | collective-permute-start | bytes 196616 | tf_op jit(solution)/shard_map/ppermute | solution.py:61
  32.4 26.7 %all-to-all-start = ((bf16[8,64,1536]{2,1,0:T(8,128)(2,1)}), bf16[8,64,1536]{2,1,0:T(8,128)(2,1)S(1)}, u32[]{:S(2)}, u32[]{:S(2)}) async-start(bf16[8,64,1536]{2,1,0:T(8,128)(2,1)} %bitcast.13), calls=%async_computation | async-start | bytes 3145728 | tf_op jit(solution)/shard_map/all_to_all | solution.py:356
  52.3 2.1 %collective-permute-start.9 = (bf16[2,256,512]{2,1,0:T(8,128)(2,1)}, bf16[2,256,512]{2,1,0:T(8,128)(2,1)S(1)}, u32[]{:S(2)}, u32[]{:S(2)}) collective-permute-start(bf16[2,256,512]{2,1,0:T(8,128)(2,1)} %get-tuple-element.66), channel_id=1, source_target_pairs={{0,64},{64,0},{128,192},{192,128},{1,65},{65,1},{129,193},{193,129... | collective-permute-start | bytes 1572872 | tf_op jit(solution)/shard_map/ppermute | solution.py:61
  54.5 1.0 %copy-start.11 = (bf16[2,256,512]{2,1,0:T(8,128)(2,1)S(1)}, bf16[2,256,512]{2,1,0:T(8,128)(2,1)}, u32[]{:S(2)}) copy-start(bf16[2,256,512]{2,1,0:T(8,128)(2,1)} %get-tuple-element.65.own_ref) | copy-start | bytes 1572868
  59.1 18.5 %all-to-all-start.1 = ((bf16[8,64,512]{2,1,0:T(8,128)(2,1)}), bf16[8,64,512]{2,1,0:T(8,128)(2,1)S(1)}, u32[]{:S(2)}, u32[]{:S(2)}) async-start(bf16[8,64,512]{2,1,0:T(8,128)(2,1)} %bitcast.14), calls=%async_computation.1 | async-start | bytes 1048576 | tf_op jit(solution)/shard_map/all_to_all | solution.py:356
  70.6 20.3 %collective-permute-start.7 = (bf16[256,1024]{1,0:T(8,128)(2,1)}, bf16[256,1024]{1,0:T(8,128)(2,1)S(1)}, u32[]{:S(2)}, u32[]{:S(2)}) collective-permute-start(bf16[256,1024]{1,0:T(8,128)(2,1)} %get-tuple-element.61), channel_id=1, source_target_pairs={{0,2},{2,4},{4,6},{6,8},{8,10},{10,12},{12,14},{14,16},{16,18},{18... | collective-permute-start | bytes 1572872 | tf_op jit(solution)/shard_map/ppermute | solution.py:56
  72.7 18.3 %collective-permute-start.8 = (bf16[256,1024]{1,0:T(8,128)(2,1)}, bf16[256,1024]{1,0:T(8,128)(2,1)S(1)}, u32[]{:S(2)}, u32[]{:S(2)}) collective-permute-start(bf16[256,1024]{1,0:T(8,128)(2,1)} %get-tuple-element.62), channel_id=1, source_target_pairs={{0,62},{2,0},{4,2},{6,4},{8,6},{10,8},{12,10},{14,12},{16,14},{18,... | collective-permute-start | bytes 1572872 | tf_op jit(solution)/shard_map/ppermute | solution.py:56
  78.6 20.9 %all-to-all-start.2 = ((bf16[8,8,2048]{2,1,0:T(8,128)(2,1)}), bf16[8,8,2048]{2,1,0:T(8,128)(2,1)S(1)}, u32[]{:S(2)}, u32[]{:S(2)}) async-start(bf16[8,8,2048]{2,1,0:T(8,128)(2,1)} %bitcast.15), calls=%async_computation.2 | async-start | bytes 524288 | tf_op jit(solution)/shard_map/all_to_all | solution.py:356
  90.9 0.8 copy-start.12
  91.0 0.9 copy-start.13

commit v4 on v3

--- a/solution.py
+++ b/solution.py
@@ -231,7 +231,7 @@
     core = place[3]
     cols = act_ref.shape[1]
     rows = input_ref.shape[1] // 4
-    peers = 4
+    peers = 8
     sources = ((input_ref, glu_ref, 0), (input_ref, glu_ref, cols), (out_ref, act_ref, 0))
     for half in range(2):
         block = 2 * half + (core if keeps else 1 - core)
@@ -246,13 +246,14 @@
                     continue
                 term = term + refs[which][half, :, at].astype(FULL)
                 at = slice(cols * which + part, cols * which + part + 256)
+                share = rows // peers
                 for peer, moved in enumerate(by_peer(term, peers)):
-                    refs[3][half, peer, :, at] = moved.astype(LOW)
+                    refs[3][peer, half * share : (half + 1) * share, at] = moved.astype(LOW)
 
 
 def terms(place, input_rows, glu_low, out_rows, activated, arrived=()):
     wide, cols = input_rows.shape[1], activated.shape[1]
-    out_shape = [shape((2, 4, wide // 16, 3 * cols))] if arrived else [shape((2, wide // 4, cols))] * 3
+    out_shape = [shape((8, wide // 16, 3 * cols))] if arrived else [shape((2, wide // 4, cols))] * 3
     operands = (place, input_rows, glu_low, out_rows, activated) + tuple(arrived)
     return call(
         functools.partial(terms_kernel, bool(arrived)), "terms",
@@ -291,11 +292,8 @@
     return call(
         resid_kernel, "resid",
         (place, out_rows, mid, far_mid, part, far_part, weight, attended),
-        [SMEM] + [whole(a) for a in (out_rows, mid, far_mid, part, far_part, weight, attended)],
-        [shape((frames, wide)), shape((frames, cols))] + [shape((2, wide // 4, cols))] * 2,
-        out_specs=[whole(a) for a in (out_rows, attended)]
-        + [pl.BlockSpec((2, wide // 4, cols), lambda i: (0, 0, 0))] * 2,
-        grid=(1,), micros=60, limit=58,
+        [SMEM] + [VMEM] * 7,
+        [shape((frames, wide)), shape((frames, cols))] + [shape((2, wide // 4, cols))] * 2, micros=60,
     )
 
 
@@ -305,28 +303,30 @@
 
 
 def add_kernel(own_ref, arrived_ref, sum_ref):
+    peers, share = sum_ref.shape[0], sum_ref.shape[1] // 2
     for half in range(2):
         total = own_ref[half].astype(FULL) + arrived_ref[half].astype(FULL)
-        for peer, rows in enumerate(by_peer(total, sum_ref.shape[1])):
-            sum_ref[half, peer] = rows.astype(LOW)
+        for peer, rows in enumerate(by_peer(total, peers)):
+            sum_ref[peer, half * share : (half + 1) * share] = rows.astype(LOW)
 
 
 def add(own, arrived, peers):
     halves, rows, cols = own.shape
-    return call(add_kernel, "add", (own, arrived), [VMEM, VMEM], [shape((halves, peers, rows // peers, cols))])[0]
+    dims = (peers, halves * rows // peers, cols)
+    return call(add_kernel, "add", (own, arrived), [VMEM, VMEM], [shape(dims)])[0]
 
 
 def plane_kernel(*refs):
     *sources, sum_ref = refs
     at = 0
     for parts_ref in sources:
-        for start in range(0, parts_ref.shape[2], 512):
-            span = slice(start, start + 512)
-            total = parts_ref[0, :, span].astype(FULL)
+        for start in range(0, parts_ref.shape[2], 256):
+            lanes = slice(start, start + 256)
+            total = parts_ref[0, :, lanes].astype(FULL)
             for i in range(1, parts_ref.shape[0]):
-                total = total + parts_ref[i, :, span].astype(FULL)
-            sum_ref[:, at : at + 512] = total.astype(LOW)
-            at += 512
+                total = total + parts_ref[i, :, lanes].astype(FULL)
+            sum_ref[:, at : at + 256] = total.astype(LOW)
+            at += 256
 
 
 def plane_sum(*parts):
@@ -357,6 +357,7 @@
 
 
 BLOCK = 128
+CHUNK = 128
 SPAN = BLOCK + 2 * WIN
 SCALE = HEAD_DIM**-0.5
 PAIR = 2 * HEAD_DIM
@@ -381,15 +382,16 @@
     whole[WIN + frames :] = after_ref[...]
 
 
-def pair_specs(frames, pairs):
-    own = pl.BlockSpec((frames, PAIR), lambda i: (0, i))
-    far_key = pl.BlockSpec((WIN, PAIR), lambda i: (0, i))
-    far_value = pl.BlockSpec((WIN, PAIR), lambda i: (0, i + pairs))
+def pair_specs(frames, pairs, start=0):
+    own = pl.BlockSpec((frames, PAIR), lambda i: (0, i + start))
+    far_key = pl.BlockSpec((WIN, PAIR), lambda i: (0, i + start))
+    far_value = pl.BlockSpec((WIN, PAIR), lambda i: (0, i + start + pairs))
     return own, far_key, far_value
 
 
 def attend_kernel(
-    place, q_ref, k_ref, v_ref, kb_ref, vb_ref, ka_ref, va_ref, prob_ref, out_ref, fill, keys, values
+    place, q_ref, k_ref, v_ref, kb_ref, vb_ref, ka_ref, va_ref,
+    weight_ref, out_ref, share_ref, fill, scores, keys, values,
 ):
     first, length = place[0], place[1]
     frames = q_ref.shape[0]
@@ -407,22 +409,32 @@
     gather_rows(values, vb_ref, v_ref, va_ref)
     for block in range(frames // BLOCK):
         rows = slice(block * BLOCK, (block + 1) * BLOCK)
-        span = slice(block * BLOCK, block * BLOCK + SPAN)
+        start = block * BLOCK
         queries = side_by_side(q_ref[rows] * SCALE)
-        scores = dot_nt(keys[span], queries) + jnp.concatenate([fill[block], fill[block]], axis=1)
-        exponent = jnp.exp(scores - jnp.max(scores, axis=0, keepdims=True))
-        prob = exponent * (1.0 / jnp.sum(exponent, axis=0, keepdims=True))
-        prob_low = prob.astype(LOW)
-        prob_ref[0, block] = prob_low
-        summed = own_columns(dot_tn(values[span], prob_low))
+        top = jnp.full((8, 2 * BLOCK), NEG_FILL, FULL)
+        for at in range(0, SPAN, CHUNK):
+            part = dot_nt(keys[start + at : start + at + CHUNK], queries)
+            bias = fill[block, at : at + CHUNK]
+            part = part + jnp.concatenate([bias, bias], axis=1)
+            scores[at : at + CHUNK] = part
+            top = jnp.maximum(top, jnp.max(part.reshape(CHUNK // 8, 8, 2 * BLOCK), axis=0))
+        top = jnp.max(top, axis=0, keepdims=True)
+        total = jnp.zeros((8, 2 * BLOCK), FULL)
+        for at in range(0, SPAN, CHUNK):
+            part = jnp.exp(scores[at : at + CHUNK] - top)
+            total = total + jnp.sum(part.reshape(CHUNK // 8, 8, 2 * BLOCK), axis=0)
+            weight_ref[0, block, at : at + CHUNK] = part.astype(LOW)
+        share = 1.0 / jnp.sum(total, axis=0, keepdims=True)
+        summed = own_columns(dot_tn(values[start : start + SPAN], weight_ref[0, block]) * share)
         frame = lax.broadcasted_iota(jnp.int32, (1, BLOCK), 1) + (first + block * BLOCK)
         out_ref[rows] = jnp.where(frame < length, summed, 0.0).T.astype(LOW)
+        share_ref[rows] = own_columns(jnp.broadcast_to(share, (PAIR, 2 * BLOCK))).T
 
 
 def attend_grad_kernel(
-    q_ref, k_ref, v_ref, kb_ref, vb_ref, ka_ref, va_ref, prob_ref, out_ref, grad_ref,
-    dq_ref, dk_ref, dv_ref, to_before_ref, to_after_ref, keys, values, key_sum, value_sum,
+    q_ref, k_ref, v_ref, kb_ref, vb_ref, ka_ref, va_ref, weight_ref, out_ref, share_ref, grad_ref, *refs
 ):
+    dq_ref, dk_ref, dv_ref, to_before_ref, to_after_ref, keys, values, key_sum, value_sum = refs[-9:]
     frames = q_ref.shape[0]
     gather_rows(keys, kb_ref, k_ref, ka_ref)
     gather_rows(values, vb_ref, v_ref, va_ref)
@@ -432,7 +444,7 @@
         rows = slice(block * BLOCK, (block + 1) * BLOCK)
         span = slice(block * BLOCK, block * BLOCK + SPAN)
         queries = side_by_side(q_ref[rows] * SCALE)
-        grad_rows = grad_ref[rows]
+        grad_rows = (grad_ref[rows].astype(FULL) * share_ref[rows]).astype(LOW)
         grads = side_by_side(grad_rows)
         product = (grad_rows.astype(FULL) * out_ref[rows].astype(FULL)).T
         row_delta = jnp.concatenate(
@@ -442,12 +454,13 @@
             ],
             axis=1,
         )
-        prob_low = prob_ref[0, block]
+        weight = weight_ref[0, block]
         grad_prob = dot_nt(values[span], grads)
-        grad_score = (prob_low.astype(FULL) * (grad_prob - row_delta)).astype(LOW)
-        value_sum[span] += jnp.dot(prob_low, grads, preferred_element_type=FULL)
+        grad_score = (weight.astype(FULL) * (grad_prob - row_delta)).astype(LOW)
+        value_sum[span] += jnp.dot(weight, grads, preferred_element_type=FULL)
         key_sum[span] += jnp.dot(grad_score, queries, preferred_element_type=FULL)
-        dq_ref[rows] = (own_columns(dot_tn(keys[span], grad_score)).T * SCALE).astype(LOW)
+        grad_query = dot_tn(keys[span], grad_score)
+        dq_ref[rows] = (own_columns(grad_query).T * SCALE).astype(LOW)
     for total, inner, lane in ((key_sum, dk_ref, 0), (value_sum, dv_ref, PAIR)):
         to_before_ref[:, lane : lane + PAIR] = total[:WIN].astype(LOW)
         inner[...] = total[WIN : WIN + frames]
@@ -461,27 +474,28 @@
     return call(
         attend_kernel, "attend", (place, q_rows, k_rows, v_rows, before, before, after, after),
         [SMEM, own, own, own, far_key, far_value, far_key, far_value],
-        [shape((pairs, blocks, SPAN, 2 * BLOCK)), shape((frames, cols))],
-        out_specs=[pl.BlockSpec((1, blocks, SPAN, 2 * BLOCK), lambda i: (i, 0, 0, 0)), own],
-        scratch=[pltpu.VMEM((blocks, SPAN, BLOCK), FULL)] + [pltpu.VMEM((frames + 2 * WIN, PAIR), LOW)] * 2,
-        grid=(pairs,), micros=0.5, limit=58,
-    )
-
-
-def attend_grad(q_rows, k_rows, v_rows, before, after, prob, attended, grad_attn):
+        [shape((pairs, blocks, SPAN, 2 * BLOCK)), shape((frames, cols)), shape((frames, cols), FULL)],
+        out_specs=[pl.BlockSpec((1, blocks, SPAN, 2 * BLOCK), lambda i: (i, 0, 0, 0)), own, own],
+        scratch=[pltpu.VMEM((blocks, SPAN, BLOCK), FULL), pltpu.VMEM((SPAN, 2 * BLOCK), FULL)] + [pltpu.VMEM((frames + 2 * WIN, PAIR), LOW)] * 2,
+        grid=(pairs,), micros=0.5, limit=57,
+    )
+
+
+def attend_grad(q_rows, k_rows, v_rows, before, after, weight, attended, share, grad_attn, start, count, earlier=()):
     frames, cols = q_rows.shape
     pairs, blocks = cols // PAIR, frames // BLOCK
-    own, far_key, far_value = pair_specs(frames, pairs)
-    far = pl.BlockSpec((WIN, 2 * PAIR), lambda i: (0, i))
+    own, far_key, far_value = pair_specs(frames, pairs, start)
+    far = pl.BlockSpec((WIN, 2 * PAIR), lambda i: (0, i + start))
+    weights = pl.BlockSpec((1, blocks, SPAN, 2 * BLOCK), lambda i: (i + start, 0, 0, 0))
     return call(
         attend_grad_kernel, "attend_grad",
-        (q_rows, k_rows, v_rows, before, before, after, after, prob, attended, grad_attn),
-        [own, own, own, far_key, far_value, far_key, far_value]
-        + [pl.BlockSpec((1, blocks, SPAN, 2 * BLOCK), lambda i: (i, 0, 0, 0)), own, own],
+        (q_rows, k_rows, v_rows, before, before, after, after, weight, attended, share, grad_attn, *earlier),
+        [own, own, own, far_key, far_value, far_key, far_value, weights, own, own, own] + [HBM] * len(earlier),
         [shape((frames, cols))] + [shape((frames, cols), FULL)] * 2 + [shape((WIN, 2 * cols))] * 2,
         out_specs=[own, own, own, far, far],
         scratch=[pltpu.VMEM((frames + 2 * WIN, PAIR), LOW)] * 2 + [pltpu.VMEM((frames + 2 * WIN, PAIR), FULL)] * 2,
-        grid=(pairs,), micros=50, limit=58,
+        grid=(count,), micros=1, limit=58,
+        input_output_aliases={11 + i: i for i in range(len(earlier))},
     )
 
 
@@ -542,27 +556,26 @@
     given = [swapped(term, "dp", 1) for term in terms(place, input_rows, glu_low, out_rows, activated)]
     on_chip = terms(place, input_rows, glu_low, out_rows, activated, given)[0]
     q_late, on_chip = lax.optimization_barrier((q_rows, on_chip))
-    prob, attended = attend(place, q_late, k_rows, v_rows, before, after)
+    weight, attended, share = attend(place, q_late, k_rows, v_rows, before, after)
     resid_low, grad_attn, out_send, out_keep = resid(
         place, out_rows, mid, far_mid, part, far_part, out_weight, attended
     )
-    xs, zs, pairs, cores = (4, peers // 4, range(2), range(2))
-    by_plane = [
-        [(2 * y + core) * peers + z * xs + x for y in pairs for x in range(xs)]
-        for core in cores for z in range(zs)
+    near, far = (8, peers // 8)
+    by_plane = [[d * peers + z * near + i for i in range(near)] for d in range(4) for z in range(far)]
+    by_line = [
+        [(2 * y + core) * peers + z * near + i for y in range(2) for z in range(far)]
+        for core in range(2) for i in range(near)
     ]
-    by_line = [[d * peers + z * xs + x for z in range(zs)] for d in range(4) for x in range(xs)]
-    rest = exchanged(on_chip.reshape((2 * xs,) + on_chip.shape[2:]), by_plane)
-    on_chip_out = add(out_keep, swapped(out_send, "dp", 1), xs)
+    rest = exchanged(on_chip, by_plane)
+    operands = (q_rows, k_rows, v_rows, before, after, weight, attended, share, grad_attn)
+    early = attend_grad(*operands, 0, 1)
+    out_given, early = lax.optimization_barrier((swapped(out_send, "dp", 1), early))
+    on_chip_out = add(out_keep, out_given, near)
+    grad_query, grad_key, grad_value, to_before, to_after = attend_grad(*operands, 1, 3, early)
+    from_after, from_before = (round_ring(to_before, -1), round_ring(to_after, 1))
     on_chip_out, rest = lax.optimization_barrier((on_chip_out, rest))
-    outs = exchanged(on_chip_out.reshape((2 * xs,) + on_chip_out.shape[2:]), by_plane)
-    plane = plane_sum(rest, outs)
-    out_sum, glu_sum, proj_sum = line_sum(exchanged(plane.reshape(zs, -1, plane.shape[1]), by_line))
-    grad_query, grad_key, grad_value, to_before, to_after = attend_grad(
-        q_rows, k_rows, v_rows, before, after, prob, attended, grad_attn
-    )
-    from_after, from_before = (round_ring(to_before, -1), round_ring(to_after, 1))
-
+    plane = plane_sum(rest, exchanged(on_chip_out, by_plane))
+    out_sum, glu_sum, proj_sum = line_sum(exchanged(plane.reshape(2 * far, -1, plane.shape[1]), by_line))
     key_grad, value_grad = finish(grad_key, grad_value, from_before, from_after)
     return (
         resid_low[None],

time: 101 us -> 97.6 us (0.966)
  starting transfers between devices: 34 us -> 31.7 us
  waiting for transfers between devices: 14.9 us -> 13.8 us
    ppermute x4, waiting for transfers between devices: 4.15 us -> 7.25 us  [round_ring(): lax.ppermute(value, 'seq', [(i, (i + steps) % count) for i in range(count)])]
    ppermute x4, starting transfers between devices: 11.3 us -> 8.43 us  [round_ring(): lax.ppermute(value, 'seq', [(i, (i + steps) % count) for i in range(count)])]
    ppermute x6, waiting for transfers between devices: 3.22 us -> 1.1 us  [swapped(): return lax.ppermute(value, axis, [(i, i ^ stride) for i in range(count)])]
    all_to_all x3, waiting for transfers between devices: 7.49 us -> 5.45 us  [exchanged(): return lax.all_to_all(parts, ('dp', 'seq'), 0, 0, axis_index_groups=groups)]
    pallas_call x12 -> x13, Pallas kernels: 44 us -> 43.1 us  [call(): pl.pallas_call(kernel, in_specs=in_specs, out_specs=[VMEM] * len(out_shap...]
    unnamed x28 -> x32, local copies, waits for them, and re-layouts: 5.77 us -> 6.58 us
  transfers between devices with their start and end apart: 13 -> 13, of which waited for: 7 -> 5; matrix products, arithmetic and copies ran while one was open for 0% -> 0% of each run, Pallas kernels for 41% -> 41%
where the time goes in v4:
time: 97.6 us; the launch traced here: 96.7 us
  Pallas kernels  43.1 us (44%)
  starting transfers between devices  31.7 us (32%)
  waiting for transfers between devices  13.8 us (14%)
  local copies, waits for them, and re-layouts  6.66 us (7%)
  between operations  1.46 us (1%)
    pallas_call x13, Pallas kernels, call(): pl.pallas_call(kernel, in_specs=in_specs, out_specs=[VMEM] * len(out_shap...  43.1 us
    all_to_all x3, starting transfers between devices, exchanged(): return lax.all_to_all(parts, ('dp', 'seq'), 0, 0, axis_index_groups=groups)  17.6 us
    ppermute x4, starting transfers between devices, round_ring(): lax.ppermute(value, 'seq', [(i, (i + steps) % count) for i in range(count)])  8.43 us
    ppermute x4, waiting for transfers between devices, round_ring(): lax.ppermute(value, 'seq', [(i, (i + steps) % count) for i in range(count)])  7.25 us
    unnamed x32, local copies, waits for them, and re-layouts  6.58 us
    ppermute x6, starting transfers between devices, swapped(): return lax.ppermute(value, axis, [(i, i ^ stride) for i in range(count)])  5.68 us
    all_to_all x3, waiting for transfers between devices, exchanged(): return lax.all_to_all(parts, ('dp', 'seq'), 0, 0, axis_index_groups=groups)  5.45 us
  transfers between devices with their start and end apart: 13, of which 5 were waited for; matrix products, arithmetic and copies ran while one was open for 0% of the time, Pallas kernels for 41%

profile of v4, /device:TPU:32, one launch (start us, length us, event | category | flops | bytes accessed | tf_op | source)
XLA Modules:
  0.0 96.7 jit_solution(13120709411241232312)
XLA Ops:
  0.7 2.4 %pack.1 = (bf16[288,1024]{1,0:T(8,128)(2,1)}, bf16[288,1024]{1,0:T(8,128)(2,1)}) custom-call(bf16[384,512]{1,0:T(8,128)(2,1)} %bitcast.26, bf16[384,512]{1,0:T(8,128)(2,1)} %bitcast.30, bf16[384,1024]{1,0:T(8,128)(2,1)} %bitcast.19, bf16[384,512]{1,0:T(8,128)(2,1)} %bitcast.24), custom_call_target="tpu_custom_call" | custom-call | flops 900000000 | bytes 1 | tf_op jit(solution)/shard_map/pack/pallas_call | solution.py:29
  3.1 1.6 %collective-permute-start.1 = (bf16[288,1024]{1,0:T(8,128)(2,1)}, bf16[288,1024]{1,0:T(8,128)(2,1)S(1)}, u32[]{:S(2)}, u32[]{:S(2)}) collective-permute-start(bf16[288,1024]{1,0:T(8,128)(2,1)} %get-tuple-element.53), channel_id=1, source_target_pairs={{0,2},{2,4},{4,6},{6,8},{8,10},{10,12},{12,14},{14,16},{16,18},{18... | collective-permute-start | bytes 1769480 | tf_op jit(solution)/shard_map/ppermute | solution.py:56
  4.7 2.6 %collective-permute-start.2 = (bf16[288,1024]{1,0:T(8,128)(2,1)}, bf16[288,1024]{1,0:T(8,128)(2,1)S(1)}, u32[]{:S(2)}, u32[]{:S(2)}) collective-permute-start(bf16[288,1024]{1,0:T(8,128)(2,1)} %get-tuple-element.54), channel_id=1, source_target_pairs={{0,62},{2,0},{4,2},{6,4},{8,6},{10,8},{12,10},{14,12},{16,14},{18,... | collective-permute-start | bytes 1769480 | tf_op jit(solution)/shard_map/ppermute | solution.py:56
  8.1 1.6 %copy-done.4 = bf16[2,1024,512]{2,1,0:T(8,128)(2,1)S(1)} copy-done((bf16[2,1024,512]{2,1,0:T(8,128)(2,1)S(1)}, bf16[2,1024,512]{2,1,0:T(8,128)(2,1)}, u32[]{:S(2)}) %copy-start.4) | copy-done | bytes 2097176
  9.7 1.2 %copy-done.8 = bf16[512,1024]{1,0:T(8,128)(2,1)S(1)} copy-done((bf16[512,1024]{1,0:T(8,128)(2,1)S(1)}, bf16[512,1024]{1,0:T(8,128)(2,1)}, u32[]{:S(2)}) %copy-start.8) | copy-done | bytes 1048600
  10.9 1.0 %copy-done.13 = bf16[1,384,512]{2,1,0:T(8,128)(2,1)S(1)} copy-done((bf16[1,384,512]{2,1,0:T(8,128)(2,1)S(1)}, bf16[1,384,512]{2,1,0:T(8,128)(2,1)}, u32[]{:S(2)}) %copy-start.13) | copy-done | bytes 393240
  11.9 6.9 %front.1 = (bf16[352,1024]{1,0:T(8,128)(2,1)S(1)}, bf16[384,1024]{1,0:T(8,128)(2,1)S(1)}, bf16[384,512]{1,0:T(8,128)(2,1)S(1)}, bf16[64,512]{1,0:T(8,128)(2,1)S(...) custom-call(s32[5]{0:T(128)S(1)} %stack.15.place, bf16[384,1024]{1,0:T(8,128)(2,1)S(1)} %bitcast.20, ...), custom_call_target="tpu_custom_call" | custom-call | flops 6300000256 | bytes 1 | tf_op jit(solution)/shard_map/front/pallas_call | solution.py:29
  18.7 3.3 %collective-permute-start = (bf16[352,1024]{1,0:T(8,128)(2,1)S(1)}, bf16[352,1024]{1,0:T(8,128)(2,1)}, u32[]{:S(2)}, u32[]{:S(2)}) collective-permute-start(bf16[352,1024]{1,0:T(8,128)(2,1)S(1)} %get-tuple-element.52.mid_ref), channel_id=1, source_target_pairs={{0,1},{1,0},{2,3},{3,2},{4,5},{5,4},{6,7},{7,6},{8,9},{9,8},{10,11... | collective-permute-start | bytes 2162696 | tf_op jit(solution)/shard_map/ppermute | solution.py:61
  22.1 2.5 %rim.1 = (bf16[32,1024]{1,0:T(8,128)(2,1)}, bf16[384,1024]{1,0:T(8,128)(2,1)S(1)}) custom-call(s32[5]{0:T(128)S(1)} %stack.15.place, bf16[288,1024]{1,0:T(8,128)(2,1)S(1)} %collective-permute-done.1.before_ref.kb_ref.vb_ref, bf16[288,1024]{1,0:T(8,128)(2,1)S(1)} %collective-permute-done.2.after_ref.ka_ref.va_ref, ...), custom_call_target="tpu_custom_call" | custom-call | flops 90000000 | bytes 1 | tf_op jit(solution)/shard_map/rim/pallas_call | solution.py:29
  24.6 1.6 %terms.2 = (bf16[2,256,512]{2,1,0:T(8,128)(2,1)S(1)}, bf16[2,256,512]{2,1,0:T(8,128)(2,1)S(1)}, bf16[2,256,512]{2,1,0:T(8,128)(2,1)S(1)}) custom-call(s32[5]{0:T(128)S(1)} %stack.15.place, bf16[384,1024]{1,0:T(8,128)(2,1)S(1)} %bitcast.17, bf16[384,1024]{1,0:T(8,128)(2,1)S(1)} %get-tuple-element.60.glu_ref, bf16[384,1024]{1,0:T(8,128)(2,1)S(1)} %bitcast.21, ...), custom_call_target="tpu_custom_call" | custom-call | flops 90000000 | bytes 1 | tf_op jit(solution)/shard_map/terms/pallas_call | solution.py:29
  26.9 1.7 %collective-permute-start.3 = (bf16[32,1024]{1,0:T(8,128)(2,1)}, bf16[32,1024]{1,0:T(8,128)(2,1)}, u32[]{:S(2)}, u32[]{:S(2)}) collective-permute-start(bf16[32,1024]{1,0:T(8,128)(2,1)} %get-tuple-element.59.part_ref), channel_id=1, source_target_pairs={{0,1},{1,0},{2,3},{3,2},{4,5},{5,4},{6,7},{7,6},{8,9},{9,8},{10,11... | collective-permute-start | bytes 196616 | tf_op jit(solution)/shard_map/ppermute | solution.py:61
  28.9 0.7 collective-permute-done.6.refs_2_
  29.7 2.8 %terms.3 = bf16[8,64,1536]{2,1,0:T(8,128)(2,1)} custom-call(s32[5]{0:T(128)S(1)} %stack.15.place, bf16[384,1024]{1,0:T(8,128)(2,1)S(1)} %bitcast.18, bf16[384,1024]{1,0:T(8,128)(2,1)S(1)} %get-tuple-element.60.glu_ref, bf16[384,1024]{1,0:T(8,128)(2,1)S(1)} %bitcast.22, bf16[384,512]{1,0:T(8,128)(2,1)S(1)} %get-tuple-element.61.act_ref, ...), custom_call_target="tpu_custom_call" | custom-call | flops 90000000 | bytes 1 | tf_op jit(solution)/shard_map/terms/pallas_call | solution.py:29
  32.4 7.6 %all-to-all-start = ((bf16[8,64,1536]{2,1,0:T(8,128)(2,1)}), bf16[8,64,1536]{2,1,0:T(8,128)(2,1)S(1)}, u32[]{:S(2)}, u32[]{:S(2)}) async-start(bf16[8,64,1536]{2,1,0:T(8,128)(2,1)} %terms.3), calls=%async_computation | async-start | bytes 3145728 | tf_op jit(solution)/shard_map/all_to_all | solution.py:356
  40.0 8.7 %attend.1 = (bf16[4,3,640,256]{3,2,1,0:T(8,128)(2,1)}, bf16[384,512]{1,0:T(8,128)(2,1)}, f32[384,512]{1,0:T(8,128)}) custom-call(s32[5]{0:T(128)} %copy-done.10, bf16[384,512]{1,0:T(8,128)(2,1)} %bitcast.34, bf16[384,512]{1,0:T(8,128)(2,1)} %bitcast.27, bf16[384,512]{1,0:T(8,128)(2,1)} %bitcast.31, bf16[288,1024]{1,0:T(8,128)(2,1)} %copy-done, ...), custom_call_target="tpu_custom_call" | custom-call | flops 450000000 | bytes 1 | tf_op jit(solution)/shard_map/attend/pallas_call | solution.py:29
  48.8 1.0 %copy-done.6 = bf16[384,512]{1,0:T(8,128)(2,1)S(1)} copy-done((bf16[384,512]{1,0:T(8,128)(2,1)S(1)}, bf16[384,512]{1,0:T(8,128)(2,1)}, u32[]{:S(2)}) %copy-start.6) | copy-done | bytes 393240
  49.7 2.9 %resid.1 = (bf16[384,1024]{1,0:T(8,128)(2,1)}, bf16[384,512]{1,0:T(8,128)(2,1)S(1)}, bf16[2,256,512]{2,1,0:T(8,128)(2,1)S(1)}, bf16[2,256,512]{2,1,0:T(8,128)(2,1)S(1)}) custom-call(s32[5]{0:T(128)S(1)} %copy-done.11, bf16[384,1024]{1,0:T(8,128)(2,1)S(1)} %bitcast.23, bf16[352,1024]{1,0:T(8,128)(2,1)S(1)} %get-tuple-element.52.mid_ref, ...), custom_call_target="tpu_custom_call" | custom-call | flops 54000001024 | bytes 1 | tf_op jit(solution)/shard_map/resid/pallas_call | solution.py:29
  52.7 0.7 copy-done.7
  53.4 3.6 %attend_grad.2 = (bf16[384,512]{1,0:T(8,128)(2,1)}, f32[384,512]{1,0:T(8,128)}, f32[384,512]{1,0:T(8,128)}, bf16[256,1024]{1,0:T(8,128)(2,1)}, bf16[256,1024]{1,0:T(8,128)(2,1)}) custom-call(bf16[384,512]{1,0:T(8,128)(2,1)} %bitcast.35, bf16[384,512]{1,0:T(8,128)(2,1)} %bitcast.28, bf16[384,512]{1,0:T(8,128)(2,1)} %bitcast.32, bf16[288,1024]{1,0:T(8,128)(2,1)} %copy-done, ...), custom_call_target="tpu_custom_call" | custom-call | flops 900000000 | bytes 1 | tf_op jit(solution)/shard_map/attend_grad/pallas_call | solution.py:29
  57.0 0.9 add.7
  57.9 2.6 %all-to-all-done.refs_0_ = bf16[8,64,1536]{2,1,0:T(8,128)(2,1)S(1)} async-done(((bf16[8,64,1536]{2,1,0:T(8,128)(2,1)}), bf16[8,64,1536]{2,1,0:T(8,128)(2,1)S(1)}, u32[]{:S(2)}, u32[]{:S(2)}) %all-to-all-start) | async-done | bytes 1572896 | tf_op jit(solution)/shard_map/all_to_all | solution.py:356
  60.5 4.2 %all-to-all-start.1 = ((bf16[8,64,512]{2,1,0:T(8,128)(2,1)}), bf16[8,64,512]{2,1,0:T(8,128)(2,1)S(1)}, u32[]{:S(2)}, u32[]{:S(2)}) async-start(bf16[8,64,512]{2,1,0:T(8,128)(2,1)} %add.7), calls=%async_computation.1 | async-start | bytes 1048576 | tf_op jit(solution)/shard_map/all_to_all | solution.py:356
  64.6 6.6 %attend_grad.3 = (bf16[384,512]{1,0:T(8,128)(2,1)}, f32[384,512]{1,0:T(8,128)}, f32[384,512]{1,0:T(8,128)}, bf16[256,1024]{1,0:T(8,128)(2,1)}, bf16[256,1024]{1,0:T(8,128)(2,1)}) custom-call(bf16[384,512]{1,0:T(8,128)(2,1)} %bitcast.36, bf16[384,512]{1,0:T(8,128)(2,1)} %bitcast.29, ...), custom_call_target="tpu_custom_call", output_to_operand_aliasing={{0}: (11, {}), {1}: (12, {}), {2}: (13, {}), {3}: (14, {}),... | custom-call | flops 900000000 | bytes 1 | tf_op jit(solution)/shard_map/attend_grad/pallas_call | solution.py:29
  71.2 1.5 %collective-permute-start.8 = (bf16[256,1024]{1,0:T(8,128)(2,1)}, bf16[256,1024]{1,0:T(8,128)(2,1)S(1)}, u32[]{:S(2)}, u32[]{:S(2)}) collective-permute-start(bf16[256,1024]{1,0:T(8,128)(2,1)} %get-tuple-element.85), channel_id=1, source_target_pairs={{0,2},{2,4},{4,6},{6,8},{8,10},{10,12},{12,14},{14,16},{16,18},{18... | collective-permute-start | bytes 1572872 | tf_op jit(solution)/shard_map/ppermute | solution.py:56
  72.8 2.7 %collective-permute-start.9 = (bf16[256,1024]{1,0:T(8,128)(2,1)}, bf16[256,1024]{1,0:T(8,128)(2,1)S(1)}, u32[]{:S(2)}, u32[]{:S(2)}) collective-permute-start(bf16[256,1024]{1,0:T(8,128)(2,1)} %get-tuple-element.86), channel_id=1, source_target_pairs={{0,62},{2,0},{4,2},{6,4},{8,6},{10,8},{12,10},{14,12},{16,14},{18,... | collective-permute-start | bytes 1572872 | tf_op jit(solution)/shard_map/ppermute | solution.py:56
  75.4 1.0 %plane_sum.1 = bf16[64,2048]{1,0:T(8,128)(2,1)} custom-call(bf16[8,64,1536]{2,1,0:T(8,128)(2,1)S(1)} %all-to-all-done.refs_0_, bf16[8,64,512]{2,1,0:T(8,128)(2,1)S(1)} %all-to-all-done.1.refs_1_), custom_call_target="tpu_custom_call" | custom-call | flops 900000000 | bytes 1 | tf_op jit(solution)/shard_map/plane_sum/pallas_call | solution.py:29
  76.4 5.8 %all-to-all-start.2 = ((bf16[8,8,2048]{2,1,0:T(8,128)(2,1)}), bf16[8,8,2048]{2,1,0:T(8,128)(2,1)S(1)}, u32[]{:S(2)}, u32[]{:S(2)}) async-start(bf16[8,8,2048]{2,1,0:T(8,128)(2,1)} %bitcast.13), calls=%async_computation.2 | async-start | bytes 524288 | tf_op jit(solution)/shard_map/all_to_all | solution.py:356
  82.2 7.2 %collective-permute-done.8.from_before_ref = bf16[256,1024]{1,0:T(8,128)(2,1)S(1)} collective-permute-done((bf16[256,1024]{1,0:T(8,128)(2,1)}, bf16[256,1024]{1,0:T(8,128)(2,1)S(1)}, u32[]{:S(2)}, u32[]{:S(2)}) %collective-permute-start.8) | collective-permute-done | bytes 524320 | tf_op jit(solution)/shard_map/ppermute | solution.py:56
  89.5 0.8 copy-done.14
  90.5 2.7 %finish.1 = (bf16[384,512]{1,0:T(8,128)(2,1)}, bf16[384,512]{1,0:T(8,128)(2,1)}) custom-call(f32[384,512]{1,0:T(8,128)} %get-tuple-element.83.dk_ref, f32[384,512]{1,0:T(8,128)} %get-tuple-element.84.dv_ref, bf16[256,1024]{1,0:T(8,128)(2,1)} %copy-done.14, bf16[256,1024]{1,0:T(8,128)(2,1)} %copy-done.15), custom_call_target="tpu_custom_call" | custom-call | flops 1800000000 | bytes 1 | tf_op jit(solution)/shard_map/finish/pallas_call | solution.py:29
  93.2 2.9 %all-to-all-done.2.parts_ref = bf16[8,8,2048]{2,1,0:T(8,128)(2,1)S(1)} async-done(((bf16[8,8,2048]{2,1,0:T(8,128)(2,1)}), bf16[8,8,2048]{2,1,0:T(8,128)(2,1)S(1)}, u32[]{:S(2)}, u32[]{:S(2)}) %all-to-all-start.2) | async-done | bytes 262176 | tf_op jit(solution)/shard_map/all_to_all | solution.py:356
  96.1 0.6 line_sum.1
  (40 shorter events, 1.4 us)
Async XLA Ops:
  0.6 7.4 %copy-start.3 = (bf16[1,384,1024]{2,1,0:T(8,128)(2,1)S(1)}, bf16[1,384,1024]{2,1,0:T(8,128)(2,1)}, u32[]{:S(2)}) copy-start(bf16[1,384,1024]{2,1,0:T(8,128)(2,1)} %param.17) | copy-start | bytes 2359300
  0.6 7.4 %copy-start.2 = (bf16[1,384,1024]{2,1,0:T(8,128)(2,1)S(1)}, bf16[1,384,1024]{2,1,0:T(8,128)(2,1)}, u32[]{:S(2)}) copy-start(bf16[1,384,1024]{2,1,0:T(8,128)(2,1)} %param.15) | copy-start | bytes 2359300
  0.7 7.4 %copy-start.9 = (bf16[31,512]{1,0:T(8,128)(2,1)S(1)}, bf16[31,512]{1,0:T(8,128)(2,1)}, u32[]{:S(2)}) copy-start(bf16[31,512]{1,0:T(8,128)(2,1)} %taps_ref.3) | copy-start | bytes 95236
  3.1 18.9 %collective-permute-start.1 = (bf16[288,1024]{1,0:T(8,128)(2,1)}, bf16[288,1024]{1,0:T(8,128)(2,1)S(1)}, u32[]{:S(2)}, u32[]{:S(2)}) collective-permute-start(bf16[288,1024]{1,0:T(8,128)(2,1)} %get-tuple-element.53), channel_id=1, source_target_pairs={{0,2},{2,4},{4,6},{6,8},{8,10},{10,12},{12,14},{14,16},{16,18},{18... | collective-permute-start | bytes 1769480 | tf_op jit(solution)/shard_map/ppermute | solution.py:56
  4.7 17.4 %collective-permute-start.2 = (bf16[288,1024]{1,0:T(8,128)(2,1)}, bf16[288,1024]{1,0:T(8,128)(2,1)S(1)}, u32[]{:S(2)}, u32[]{:S(2)}) collective-permute-start(bf16[288,1024]{1,0:T(8,128)(2,1)} %get-tuple-element.54), channel_id=1, source_target_pairs={{0,62},{2,0},{4,2},{6,4},{8,6},{10,8},{12,10},{14,12},{16,14},{18,... | collective-permute-start | bytes 1769480 | tf_op jit(solution)/shard_map/ppermute | solution.py:56
  8.0 21.6 %copy-start.10 = (s32[5]{0:T(128)}, s32[5]{0:T(128)S(1)}, u32[]{:S(2)}) copy-start(s32[5]{0:T(128)S(1)} %stack.15.place) | copy-start | bytes 64
  8.1 1.6 %copy-start.4 = (bf16[2,1024,512]{2,1,0:T(8,128)(2,1)S(1)}, bf16[2,1024,512]{2,1,0:T(8,128)(2,1)}, u32[]{:S(2)}) copy-start(bf16[2,1024,512]{2,1,0:T(8,128)(2,1)} %glu_w_ref.3) | copy-start | bytes 6291460
  9.7 1.2 %copy-start.8 = (bf16[512,1024]{1,0:T(8,128)(2,1)S(1)}, bf16[512,1024]{1,0:T(8,128)(2,1)}, u32[]{:S(2)}) copy-start(bf16[512,1024]{1,0:T(8,128)(2,1)} %proj_ref.3) | copy-start | bytes 3145732
  10.9 1.0 %copy-start.13 = (bf16[1,384,512]{2,1,0:T(8,128)(2,1)S(1)}, bf16[1,384,512]{2,1,0:T(8,128)(2,1)}, u32[]{:S(2)}) copy-start(bf16[1,384,512]{2,1,0:T(8,128)(2,1)} %param.16) | copy-start | bytes 1179652
  11.9 10.2 %copy-start.5 = (bf16[2,1024,512]{2,1,0:T(8,128)(2,1)S(1)}, bf16[2,1024,512]{2,1,0:T(8,128)(2,1)}, u32[]{:S(2)}) copy-start(bf16[2,1024,512]{2,1,0:T(8,128)(2,1)} %glu_w_ref.3) | copy-start | bytes 6291460
  18.7 30.0 %collective-permute-start = (bf16[352,1024]{1,0:T(8,128)(2,1)S(1)}, bf16[352,1024]{1,0:T(8,128)(2,1)}, u32[]{:S(2)}, u32[]{:S(2)}) collective-permute-start(bf16[352,1024]{1,0:T(8,128)(2,1)S(1)} %get-tuple-element.52.mid_ref), channel_id=1, source_target_pairs={{0,1},{1,0},{2,3},{3,2},{4,5},{5,4},{6,7},{7,6},{8,9},{9,8},{10,11... | collective-permute-start | bytes 2162696 | tf_op jit(solution)/shard_map/ppermute | solution.py:61
  22.0 2.6 %copy-start = (bf16[288,1024]{1,0:T(8,128)(2,1)}, bf16[288,1024]{1,0:T(8,128)(2,1)S(1)}, u32[]{:S(2)}) copy-start(bf16[288,1024]{1,0:T(8,128)(2,1)S(1)} %collective-permute-done.1.before_ref.kb_ref.vb_ref) | copy-start | bytes 1769476
  22.0 2.6 %copy-start.1 = (bf16[288,1024]{1,0:T(8,128)(2,1)}, bf16[288,1024]{1,0:T(8,128)(2,1)S(1)}, u32[]{:S(2)}) copy-start(bf16[288,1024]{1,0:T(8,128)(2,1)S(1)} %collective-permute-done.2.after_ref.ka_ref.va_ref) | copy-start | bytes 1769476
  26.2 2.4 %collective-permute-start.4 = (bf16[2,256,512]{2,1,0:T(8,128)(2,1)S(1)}, bf16[2,256,512]{2,1,0:T(8,128)(2,1)S(1)}, u32[]{:S(2)}, u32[]{:S(2)}) collective-permute-start(bf16[2,256,512]{2,1,0:T(8,128)(2,1)S(1)} %get-tuple-element.62), channel_id=1, source_target_pairs={{0,64},{64,0},{128,192},{192,128},{1,65},{65,1},{129,193},{193,129... | collective-permute-start | bytes 1572872 | tf_op jit(solution)/shard_map/ppermute | solution.py:61
  26.3 2.6 %collective-permute-start.5 = (bf16[2,256,512]{2,1,0:T(8,128)(2,1)S(1)}, bf16[2,256,512]{2,1,0:T(8,128)(2,1)S(1)}, u32[]{:S(2)}, u32[]{:S(2)}) collective-permute-start(bf16[2,256,512]{2,1,0:T(8,128)(2,1)S(1)} %get-tuple-element.63), channel_id=1, source_target_pairs={{0,64},{64,0},{128,192},{192,128},{1,65},{65,1},{129,193},{193,129... | collective-permute-start | bytes 1572872 | tf_op jit(solution)/shard_map/ppermute | solution.py:61
  26.8 2.9 %collective-permute-start.6 = (bf16[2,256,512]{2,1,0:T(8,128)(2,1)S(1)}, bf16[2,256,512]{2,1,0:T(8,128)(2,1)S(1)}, u32[]{:S(2)}, u32[]{:S(2)}) collective-permute-start(bf16[2,256,512]{2,1,0:T(8,128)(2,1)S(1)} %get-tuple-element.64), channel_id=1, source_target_pairs={{0,64},{64,0},{128,192},{192,128},{1,65},{65,1},{129,193},{193,129... | collective-permute-start | bytes 1572872 | tf_op jit(solution)/shard_map/ppermute | solution.py:61
  26.9 21.9 %collective-permute-start.3 = (bf16[32,1024]{1,0:T(8,128)(2,1)}, bf16[32,1024]{1,0:T(8,128)(2,1)}, u32[]{:S(2)}, u32[]{:S(2)}) collective-permute-start(bf16[32,1024]{1,0:T(8,128)(2,1)} %get-tuple-element.59.part_ref), channel_id=1, source_target_pairs={{0,1},{1,0},{2,3},{3,2},{4,5},{5,4},{6,7},{7,6},{8,9},{9,8},{10,11... | collective-permute-start | bytes 196616 | tf_op jit(solution)/shard_map/ppermute | solution.py:61
  32.4 28.1 %all-to-all-start = ((bf16[8,64,1536]{2,1,0:T(8,128)(2,1)}), bf16[8,64,1536]{2,1,0:T(8,128)(2,1)S(1)}, u32[]{:S(2)}, u32[]{:S(2)}) async-start(bf16[8,64,1536]{2,1,0:T(8,128)(2,1)} %terms.3), calls=%async_computation | async-start | bytes 3145728 | tf_op jit(solution)/shard_map/all_to_all | solution.py:356
  40.0 8.7 %copy-start.11 = (s32[5]{0:T(128)S(1)}, s32[5]{0:T(128)}, u32[]{:S(2)}) copy-start(s32[5]{0:T(128)} %copy-done.10) | copy-start | bytes 64
  40.0 8.7 %copy-start.12 = (bf16[512,1024]{1,0:T(8,128)(2,1)S(1)}, bf16[512,1024]{1,0:T(8,128)(2,1)}, u32[]{:S(2)}) copy-start(bf16[512,1024]{1,0:T(8,128)(2,1)} %weight_ref.1) | copy-start | bytes 3145732
  48.7 1.0 %copy-start.6 = (bf16[384,512]{1,0:T(8,128)(2,1)S(1)}, bf16[384,512]{1,0:T(8,128)(2,1)}, u32[]{:S(2)}) copy-start(bf16[384,512]{1,0:T(8,128)(2,1)} %get-tuple-element.66.attended_ref.out_ref) | copy-start | bytes 1179652
  52.7 0.7 copy-start.7
  53.4 3.6 %collective-permute-start.7 = (bf16[2,256,512]{2,1,0:T(8,128)(2,1)S(1)}, bf16[2,256,512]{2,1,0:T(8,128)(2,1)S(1)}, u32[]{:S(2)}, u32[]{:S(2)}) collective-permute-start(bf16[2,256,512]{2,1,0:T(8,128)(2,1)S(1)} %get-tuple-element.71), channel_id=1, source_target_pairs={{0,64},{64,0},{128,192},{192,128},{1,65},{65,1},{129,193},{193,129... | collective-permute-start | bytes 1572872 | tf_op jit(solution)/shard_map/ppermute | solution.py:61
  60.5 15.0 %all-to-all-start.1 = ((bf16[8,64,512]{2,1,0:T(8,128)(2,1)}), bf16[8,64,512]{2,1,0:T(8,128)(2,1)S(1)}, u32[]{:S(2)}, u32[]{:S(2)}) async-start(bf16[8,64,512]{2,1,0:T(8,128)(2,1)} %add.7), calls=%async_computation.1 | async-start | bytes 1048576 | tf_op jit(solution)/shard_map/all_to_all | solution.py:356
  71.2 18.2 %collective-permute-start.8 = (bf16[256,1024]{1,0:T(8,128)(2,1)}, bf16[256,1024]{1,0:T(8,128)(2,1)S(1)}, u32[]{:S(2)}, u32[]{:S(2)}) collective-permute-start(bf16[256,1024]{1,0:T(8,128)(2,1)} %get-tuple-element.85), channel_id=1, source_target_pairs={{0,2},{2,4},{4,6},{6,8},{8,10},{10,12},{12,14},{14,16},{16,18},{18... | collective-permute-start | bytes 1572872 | tf_op jit(solution)/shard_map/ppermute | solution.py:56
  72.8 16.7 %collective-permute-start.9 = (bf16[256,1024]{1,0:T(8,128)(2,1)}, bf16[256,1024]{1,0:T(8,128)(2,1)S(1)}, u32[]{:S(2)}, u32[]{:S(2)}) collective-permute-start(bf16[256,1024]{1,0:T(8,128)(2,1)} %get-tuple-element.86), channel_id=1, source_target_pairs={{0,62},{2,0},{4,2},{6,4},{8,6},{10,8},{12,10},{14,12},{16,14},{18,... | collective-permute-start | bytes 1572872 | tf_op jit(solution)/shard_map/ppermute | solution.py:56
  76.4 19.6 %all-to-all-start.2 = ((bf16[8,8,2048]{2,1,0:T(8,128)(2,1)}), bf16[8,8,2048]{2,1,0:T(8,128)(2,1)S(1)}, u32[]{:S(2)}, u32[]{:S(2)}) async-start(bf16[8,8,2048]{2,1,0:T(8,128)(2,1)} %bitcast.13), calls=%async_computation.2 | async-start | bytes 524288 | tf_op jit(solution)/shard_map/all_to_all | solution.py:356
  89.5 0.8 copy-start.14
  89.5 1.0 %copy-start.15 = (bf16[256,1024]{1,0:T(8,128)(2,1)}, bf16[256,1024]{1,0:T(8,128)(2,1)S(1)}, u32[]{:S(2)}) copy-start(bf16[256,1024]{1,0:T(8,128)(2,1)S(1)} %collective-permute-done.9.from_after_ref) | copy-start | bytes 1572868

commit v5 on v4

--- a/solution.py
+++ b/solution.py
@@ -127,14 +127,20 @@
     taps[:TAPS] = taps_ref[...].astype(FULL)
     for part in range(0, cols, 256):
         span = slice(part, part + 256)
-        grad_pre, activated = pre_grad(out_ref[...], pre_ref[:, span], proj_ref[span])
-        act_ref[:, span] = activated
-        padded[:, span] = grad_pre.astype(FULL)
-        rim_ref[: 2 * EDGE, span] = grad_pre[: 2 * EDGE]
-        rim_ref[2 * EDGE :, span] = grad_pre[frames - 2 * EDGE :]
+        grad_act = dot_nt(out_ref[...], proj_ref[span])
+        for at in range(0, frames, 64):
+            rows = slice(at, at + 64)
+            pre = pre_ref[rows, span].astype(FULL)
+            logistic = jax.nn.sigmoid(pre)
+            slope = logistic * (1.0 + pre * (1.0 - logistic))
+            padded[rows, span] = (grad_act[rows] * slope).astype(LOW).astype(FULL)
+            act_ref[rows, span] = (pre * logistic).astype(LOW)
+        rim_ref[: 2 * EDGE, span] = padded[: 2 * EDGE, span].astype(LOW)
+        rim_ref[2 * EDGE :, span] = padded[frames - 2 * EDGE :, span].astype(LOW)
         values[:, span] = jnp.dot(input_ref[...], glu_w_ref[0, :, span], preferred_element_type=FULL)
         gate_half = jnp.dot(input_ref[...], glu_w_ref[1, :, span], preferred_element_type=FULL)
-        gates[:, span] = jax.nn.sigmoid(gate_half)
+        for at in range(0, frames, 64):
+            gates[at : at + 64, span] = jax.nn.sigmoid(gate_half[at : at + 64])
     for whole, rim in ((gates, rim_gate_ref), (values, rim_value_ref)):
         rim[:EDGE] = whole[:EDGE]
         rim[EDGE:] = whole[inner:]
@@ -188,7 +194,7 @@
     frames = glu_ref.shape[0]
     cols = rim_ref.shape[1]
     first, length, total = place[0], place[1], place[2]
-    glu_ref[EDGE : frames - EDGE] = glu_in_ref[EDGE : frames - EDGE]
+    del glu_in_ref
     out_rows = jnp.concatenate([before_ref[:EDGE], after_ref[:EDGE]], axis=0)
     pre_rows = jnp.concatenate([before_ref[EDGE:, :cols], after_ref[EDGE:, :cols]], axis=0)
     arrived = pre_grad(out_rows, pre_rows, proj_ref[...])[0].astype(FULL)
@@ -223,7 +229,7 @@
         [SMEM, edge, edge, whole(rim_rows), whole(gate), whole(value), VMEM, VMEM, whole(taps), VMEM],
         [shape((2 * EDGE, wide)), shape(glu_low.shape)],
         out_specs=[pl.BlockSpec((2 * EDGE, wide), lambda i: (0, 0)), VMEM],
-        grid=(1,), micros=0.1,
+        grid=(1,), micros=0.1, input_output_aliases={9: 1},
     )
 
 
@@ -232,12 +238,13 @@
     cols = act_ref.shape[1]
     rows = input_ref.shape[1] // 4
     peers = 8
+    share = rows // peers
     sources = ((input_ref, glu_ref, 0), (input_ref, glu_ref, cols), (out_ref, act_ref, 0))
-    for half in range(2):
-        block = 2 * half + (core if keeps else 1 - core)
-        span = pl.ds(pl.multiple_of(block * rows, rows), rows)
-        for which, (source, low, start) in enumerate(sources):
-            left = source[:, span]
+    leaving = []
+    for which, (source, low, start) in enumerate(sources):
+        for half in range(2):
+            block = 2 * half + (core if keeps else 1 - core)
+            left = source[:, pl.ds(pl.multiple_of(block * rows, rows), rows)]
             for part in range(0, cols, 256):
                 term = dot_tn(left, low[:, start + part : start + part + 256])
                 at = slice(part, part + 256)
@@ -246,18 +253,28 @@
                     continue
                 term = term + refs[which][half, :, at].astype(FULL)
                 at = slice(cols * which + part, cols * which + part + 256)
-                share = rows // peers
                 for peer, moved in enumerate(by_peer(term, peers)):
-                    refs[3][peer, half * share : (half + 1) * share, at] = moved.astype(LOW)
+                    refs[4][peer, half * share : (half + 1) * share, at] = moved.astype(LOW)
+        if keeps:
+            at = slice(cols * which, cols * which + cols)
+            leaving.append(pltpu.make_async_copy(refs[4].at[:, :, at], refs[3].at[:, :, at], refs[5].at[which]))
+            leaving[-1].start()
+    for copy in leaving:
+        copy.wait()
 
 
 def terms(place, input_rows, glu_low, out_rows, activated, arrived=()):
     wide, cols = input_rows.shape[1], activated.shape[1]
-    out_shape = [shape((8, wide // 16, 3 * cols))] if arrived else [shape((2, wide // 4, cols))] * 3
     operands = (place, input_rows, glu_low, out_rows, activated) + tuple(arrived)
+    joined = (8, wide // 16, 3 * cols)
+    if arrived:
+        more = dict(out_specs=[HBM], scratch=[pltpu.VMEM(joined, LOW), pltpu.SemaphoreType.DMA((3,))])
+    else:
+        more = {}
     return call(
         functools.partial(terms_kernel, bool(arrived)), "terms",
-        operands, [SMEM] + [VMEM] * (len(operands) - 1), out_shape, micros=0.1,
+        operands, [SMEM] + [VMEM] * (len(operands) - 1),
+        [shape(joined)] if arrived else [shape((2, wide // 4, cols))] * 3, micros=0.1, **more,
     )
 
 
@@ -514,11 +531,12 @@
 
 
 def finish(grad_key, grad_value, from_before, from_after):
-    own = pl.BlockSpec(grad_key.shape, lambda i: (0, 0))
-    far = pl.BlockSpec(from_before.shape, lambda i: (0, 0))
+    steps = 2
+    own = pl.BlockSpec((grad_key.shape[0], grad_key.shape[1] // steps), lambda i: (0, i))
+    far = pl.BlockSpec((from_before.shape[0], from_before.shape[1] // steps), lambda i: (0, i))
     return call(
         finish_kernel, "finish", (grad_key, grad_value, from_before, from_after), [own, own, far, far],
-        [shape(grad_key.shape)] * 2, out_specs=[own, own], grid=(1,), micros=2, limit=58,
+        [shape(grad_key.shape)] * 2, out_specs=[own, own], grid=(steps,), micros=2, limit=50,
     )
 
 
@@ -568,10 +586,10 @@
     ]
     rest = exchanged(on_chip, by_plane)
     operands = (q_rows, k_rows, v_rows, before, after, weight, attended, share, grad_attn)
-    early = attend_grad(*operands, 0, 1)
+    early = attend_grad(*operands, 0, 2)
     out_given, early = lax.optimization_barrier((swapped(out_send, "dp", 1), early))
     on_chip_out = add(out_keep, out_given, near)
-    grad_query, grad_key, grad_value, to_before, to_after = attend_grad(*operands, 1, 3, early)
+    grad_query, grad_key, grad_value, to_before, to_after = attend_grad(*operands, 2, 2, early)
     from_after, from_before = (round_ring(to_before, -1), round_ring(to_after, 1))
     on_chip_out, rest = lax.optimization_barrier((on_chip_out, rest))
     plane = plane_sum(rest, exchanged(on_chip_out, by_plane))

time: 97.6 us -> 96.8 us (level)
  local copies, waits for them, and re-layouts: 6.66 us -> 5.67 us
    ppermute x4, waiting for transfers between devices: 7.25 us -> 5.04 us  [round_ring(): lax.ppermute(value, 'seq', [(i, (i + steps) % count) for i in range(count)])]
    all_to_all x3, waiting for transfers between devices: 5.45 us -> 7.21 us  [exchanged(): return lax.all_to_all(parts, ('dp', 'seq'), 0, 0, axis_index_groups=groups)]
    unnamed x32, local copies, waits for them, and re-layouts: 6.58 us -> 5.58 us
  transfers between devices with their start and end apart: 13 -> 13, of which waited for: 5 -> 6; matrix products, arithmetic and copies ran while one was open for 0% -> 0% of each run, Pallas kernels for 41% -> 42%
where the time goes in v5:
time: 96.8 us; the launch traced here: 95.6 us
  Pallas kernels  42.9 us (44%)
  starting transfers between devices  32.2 us (33%)
  waiting for transfers between devices  13.4 us (14%)
  local copies, waits for them, and re-layouts  5.67 us (6%)
  between operations  1.49 us (2%)
    pallas_call x13, Pallas kernels, call(): pl.pallas_call(kernel, in_specs=in_specs, out_specs=[VMEM] * len(out_shap...  42.9 us
    all_to_all x3, starting transfers between devices, exchanged(): return lax.all_to_all(parts, ('dp', 'seq'), 0, 0, axis_index_groups=groups)  18.1 us
    ppermute x4, starting transfers between devices, round_ring(): lax.ppermute(value, 'seq', [(i, (i + steps) % count) for i in range(count)])  8.43 us
    all_to_all x3, waiting for transfers between devices, exchanged(): return lax.all_to_all(parts, ('dp', 'seq'), 0, 0, axis_index_groups=groups)  7.21 us
    ppermute x6, starting transfers between devices, swapped(): return lax.ppermute(value, axis, [(i, i ^ stride) for i in range(count)])  5.68 us
    unnamed x32, local copies, waits for them, and re-layouts  5.58 us
    ppermute x4, waiting for transfers between devices, round_ring(): lax.ppermute(value, 'seq', [(i, (i + steps) % count) for i in range(count)])  5.04 us
  transfers between devices with their start and end apart: 13, of which 6 were waited for; matrix products, arithmetic and copies ran while one was open for 0% of the time, Pallas kernels for 42%

profile of v5, /device:TPU:32, one launch (start us, length us, event | category | flops | bytes accessed | tf_op | source)
XLA Modules:
  0.0 95.6 jit_solution(2878684414166988960)
XLA Ops:
  0.7 2.4 %pack.1 = (bf16[288,1024]{1,0:T(8,128)(2,1)}, bf16[288,1024]{1,0:T(8,128)(2,1)}) custom-call(bf16[384,512]{1,0:T(8,128)(2,1)} %bitcast.26, bf16[384,512]{1,0:T(8,128)(2,1)} %bitcast.30, bf16[384,1024]{1,0:T(8,128)(2,1)} %bitcast.19, bf16[384,512]{1,0:T(8,128)(2,1)} %bitcast.24), custom_call_target="tpu_custom_call" | custom-call | flops 900000000 | bytes 1 | tf_op jit(solution)/shard_map/pack/pallas_call | solution.py:29
  3.1 1.6 %collective-permute-start.1 = (bf16[288,1024]{1,0:T(8,128)(2,1)}, bf16[288,1024]{1,0:T(8,128)(2,1)S(1)}, u32[]{:S(2)}, u32[]{:S(2)}) collective-permute-start(bf16[288,1024]{1,0:T(8,128)(2,1)} %get-tuple-element.53), channel_id=1, source_target_pairs={{0,2},{2,4},{4,6},{6,8},{8,10},{10,12},{12,14},{14,16},{16,18},{18... | collective-permute-start | bytes 1769480 | tf_op jit(solution)/shard_map/ppermute | solution.py:56
  4.7 2.6 %collective-permute-start.2 = (bf16[288,1024]{1,0:T(8,128)(2,1)}, bf16[288,1024]{1,0:T(8,128)(2,1)S(1)}, u32[]{:S(2)}, u32[]{:S(2)}) collective-permute-start(bf16[288,1024]{1,0:T(8,128)(2,1)} %get-tuple-element.54), channel_id=1, source_target_pairs={{0,62},{2,0},{4,2},{6,4},{8,6},{10,8},{12,10},{14,12},{16,14},{18,... | collective-permute-start | bytes 1769480 | tf_op jit(solution)/shard_map/ppermute | solution.py:56
  8.1 1.6 %copy-done.4 = bf16[2,1024,512]{2,1,0:T(8,128)(2,1)S(1)} copy-done((bf16[2,1024,512]{2,1,0:T(8,128)(2,1)S(1)}, bf16[2,1024,512]{2,1,0:T(8,128)(2,1)}, u32[]{:S(2)}) %copy-start.4) | copy-done | bytes 2097176
  9.7 1.2 %copy-done.8 = bf16[512,1024]{1,0:T(8,128)(2,1)S(1)} copy-done((bf16[512,1024]{1,0:T(8,128)(2,1)S(1)}, bf16[512,1024]{1,0:T(8,128)(2,1)}, u32[]{:S(2)}) %copy-start.8) | copy-done | bytes 1048600
  10.9 1.0 %copy-done.15 = bf16[1,384,512]{2,1,0:T(8,128)(2,1)S(1)} copy-done((bf16[1,384,512]{2,1,0:T(8,128)(2,1)S(1)}, bf16[1,384,512]{2,1,0:T(8,128)(2,1)}, u32[]{:S(2)}) %copy-start.15) | copy-done | bytes 393240
  11.9 6.9 %front.1 = (bf16[352,1024]{1,0:T(8,128)(2,1)S(1)}, bf16[384,1024]{1,0:T(8,128)(2,1)S(1)}, bf16[384,512]{1,0:T(8,128)(2,1)S(1)}, bf16[64,512]{1,0:T(8,128)(2,1)S(...) custom-call(s32[5]{0:T(128)S(1)} %stack.15.place, bf16[384,1024]{1,0:T(8,128)(2,1)S(1)} %bitcast.20, ...), custom_call_target="tpu_custom_call" | custom-call | flops 6300000256 | bytes 1 | tf_op jit(solution)/shard_map/front/pallas_call | solution.py:29
  18.7 3.3 %collective-permute-start = (bf16[352,1024]{1,0:T(8,128)(2,1)S(1)}, bf16[352,1024]{1,0:T(8,128)(2,1)}, u32[]{:S(2)}, u32[]{:S(2)}) collective-permute-start(bf16[352,1024]{1,0:T(8,128)(2,1)S(1)} %get-tuple-element.52.mid_ref), channel_id=1, source_target_pairs={{0,1},{1,0},{2,3},{3,2},{4,5},{5,4},{6,7},{7,6},{8,9},{9,8},{10,11... | collective-permute-start | bytes 2162696 | tf_op jit(solution)/shard_map/ppermute | solution.py:61
  22.1 2.5 %rim.1 = (bf16[32,1024]{1,0:T(8,128)(2,1)}, bf16[384,1024]{1,0:T(8,128)(2,1)S(1)}) custom-call(s32[5]{0:T(128)S(1)} %stack.15.place, bf16[288,1024]{1,0:T(8,128)(2,1)S(1)} %collective-permute-done.1.before_ref.kb_ref.vb_ref, bf16[288,1024]{1,0:T(8,128)(2,1)S(1)} %collective-permute-done.2.after_ref.ka_ref.va_ref, ...), custom_call_target="tpu_custom_call", output_to_operand_aliasing={{1}: (9, {})} | custom-call | flops 90000000 | bytes 1 | tf_op jit(solution)/shard_map/rim/pallas_call | solution.py:29
  24.5 1.6 %terms.2 = (bf16[2,256,512]{2,1,0:T(8,128)(2,1)S(1)}, bf16[2,256,512]{2,1,0:T(8,128)(2,1)S(1)}, bf16[2,256,512]{2,1,0:T(8,128)(2,1)S(1)}) custom-call(s32[5]{0:T(128)S(1)} %stack.15.place, bf16[384,1024]{1,0:T(8,128)(2,1)S(1)} %bitcast.17, bf16[384,1024]{1,0:T(8,128)(2,1)S(1)} %get-tuple-element.60.glu_ref, bf16[384,1024]{1,0:T(8,128)(2,1)S(1)} %bitcast.21, ...), custom_call_target="tpu_custom_call" | custom-call | flops 90000000 | bytes 1 | tf_op jit(solution)/shard_map/terms/pallas_call | solution.py:29
  26.2 0.5 collective-permute-start.5
  26.8 1.7 %collective-permute-start.3 = (bf16[32,1024]{1,0:T(8,128)(2,1)}, bf16[32,1024]{1,0:T(8,128)(2,1)}, u32[]{:S(2)}, u32[]{:S(2)}) collective-permute-start(bf16[32,1024]{1,0:T(8,128)(2,1)} %get-tuple-element.59.part_ref), channel_id=1, source_target_pairs={{0,1},{1,0},{2,3},{3,2},{4,5},{5,4},{6,7},{7,6},{8,9},{9,8},{10,11... | collective-permute-start | bytes 196616 | tf_op jit(solution)/shard_map/ppermute | solution.py:61
  28.9 0.7 collective-permute-done.6.refs_2_
  29.6 2.4 %terms.3 = bf16[8,64,1536]{2,1,0:T(8,128)(2,1)} custom-call(s32[5]{0:T(128)S(1)} %stack.15.place, bf16[384,1024]{1,0:T(8,128)(2,1)S(1)} %bitcast.18, bf16[384,1024]{1,0:T(8,128)(2,1)S(1)} %get-tuple-element.60.glu_ref, bf16[384,1024]{1,0:T(8,128)(2,1)S(1)} %bitcast.22, bf16[384,512]{1,0:T(8,128)(2,1)S(1)} %get-tuple-element.61.act_ref, ...), custom_call_target="tpu_custom_call" | custom-call | flops 90000000 | bytes 1 | tf_op jit(solution)/shard_map/terms/pallas_call | solution.py:29
  32.1 7.6 %all-to-all-start = ((bf16[8,64,1536]{2,1,0:T(8,128)(2,1)}), bf16[8,64,1536]{2,1,0:T(8,128)(2,1)S(1)}, u32[]{:S(2)}, u32[]{:S(2)}) async-start(bf16[8,64,1536]{2,1,0:T(8,128)(2,1)} %terms.3), calls=%async_computation | async-start | bytes 3145728 | tf_op jit(solution)/shard_map/all_to_all | solution.py:373
  39.7 8.7 %attend.1 = (bf16[4,3,640,256]{3,2,1,0:T(8,128)(2,1)}, bf16[384,512]{1,0:T(8,128)(2,1)}, f32[384,512]{1,0:T(8,128)}) custom-call(s32[5]{0:T(128)} %copy-done.12, bf16[384,512]{1,0:T(8,128)(2,1)} %bitcast.34, bf16[384,512]{1,0:T(8,128)(2,1)} %bitcast.27, bf16[384,512]{1,0:T(8,128)(2,1)} %bitcast.31, bf16[288,1024]{1,0:T(8,128)(2,1)} %copy-done, ...), custom_call_target="tpu_custom_call" | custom-call | flops 450000000 | bytes 1 | tf_op jit(solution)/shard_map/attend/pallas_call | solution.py:29
  48.4 1.0 %copy-done.6 = bf16[384,512]{1,0:T(8,128)(2,1)S(1)} copy-done((bf16[384,512]{1,0:T(8,128)(2,1)S(1)}, bf16[384,512]{1,0:T(8,128)(2,1)}, u32[]{:S(2)}) %copy-start.6) | copy-done | bytes 393240
  49.4 2.9 %resid.1 = (bf16[384,1024]{1,0:T(8,128)(2,1)}, bf16[384,512]{1,0:T(8,128)(2,1)S(1)}, bf16[2,256,512]{2,1,0:T(8,128)(2,1)S(1)}, bf16[2,256,512]{2,1,0:T(8,128)(2,1)S(1)}) custom-call(s32[5]{0:T(128)S(1)} %copy-done.13, bf16[384,1024]{1,0:T(8,128)(2,1)S(1)} %bitcast.23, bf16[352,1024]{1,0:T(8,128)(2,1)S(1)} %get-tuple-element.52.mid_ref, ...), custom_call_target="tpu_custom_call" | custom-call | flops 54000001024 | bytes 1 | tf_op jit(solution)/shard_map/resid/pallas_call | solution.py:29
  52.3 0.7 copy-done.7
  53.1 4.9 %attend_grad.2 = (bf16[384,512]{1,0:T(8,128)(2,1)}, f32[384,512]{1,0:T(8,128)}, f32[384,512]{1,0:T(8,128)}, bf16[256,1024]{1,0:T(8,128)(2,1)}, bf16[256,1024]{1,0:T(8,128)(2,1)}) custom-call(bf16[384,512]{1,0:T(8,128)(2,1)} %bitcast.35, bf16[384,512]{1,0:T(8,128)(2,1)} %bitcast.28, bf16[384,512]{1,0:T(8,128)(2,1)} %bitcast.32, bf16[288,1024]{1,0:T(8,128)(2,1)} %copy-done, ...), custom_call_target="tpu_custom_call" | custom-call | flops 900000000 | bytes 1 | tf_op jit(solution)/shard_map/attend_grad/pallas_call | solution.py:29
  58.0 0.9 add.7
  59.0 1.2 %all-to-all-done.refs_0_ = bf16[8,64,1536]{2,1,0:T(8,128)(2,1)S(1)} async-done(((bf16[8,64,1536]{2,1,0:T(8,128)(2,1)}), bf16[8,64,1536]{2,1,0:T(8,128)(2,1)S(1)}, u32[]{:S(2)}, u32[]{:S(2)}) %all-to-all-start) | async-done | bytes 1572896 | tf_op jit(solution)/shard_map/all_to_all | solution.py:373
  60.1 4.6 %all-to-all-start.1 = ((bf16[8,64,512]{2,1,0:T(8,128)(2,1)}), bf16[8,64,512]{2,1,0:T(8,128)(2,1)}, u32[]{:S(2)}, u32[]{:S(2)}) async-start(bf16[8,64,512]{2,1,0:T(8,128)(2,1)} %add.7), calls=%async_computation.1 | async-start | bytes 1048576 | tf_op jit(solution)/shard_map/all_to_all | solution.py:373
  64.7 5.0 %attend_grad.3 = (bf16[384,512]{1,0:T(8,128)(2,1)}, f32[384,512]{1,0:T(8,128)}, f32[384,512]{1,0:T(8,128)}, bf16[256,1024]{1,0:T(8,128)(2,1)}, bf16[256,1024]{1,0:T(8,128)(2,1)}) custom-call(bf16[384,512]{1,0:T(8,128)(2,1)} %bitcast.36, bf16[384,512]{1,0:T(8,128)(2,1)} %bitcast.29, ...), custom_call_target="tpu_custom_call", output_to_operand_aliasing={{0}: (11, {}), {1}: (12, {}), {2}: (13, {}), {3}: (14, {}),... | custom-call | flops 900000000 | bytes 1 | tf_op jit(solution)/shard_map/attend_grad/pallas_call | solution.py:29
  69.7 1.5 %collective-permute-start.8 = (bf16[256,1024]{1,0:T(8,128)(2,1)}, bf16[256,1024]{1,0:T(8,128)(2,1)}, u32[]{:S(2)}, u32[]{:S(2)}) collective-permute-start(bf16[256,1024]{1,0:T(8,128)(2,1)} %get-tuple-element.85), channel_id=1, source_target_pairs={{0,2},{2,4},{4,6},{6,8},{8,10},{10,12},{12,14},{14,16},{16,18},{18... | collective-permute-start | bytes 1572872 | tf_op jit(solution)/shard_map/ppermute | solution.py:56
  71.3 2.7 %collective-permute-start.9 = (bf16[256,1024]{1,0:T(8,128)(2,1)}, bf16[256,1024]{1,0:T(8,128)(2,1)}, u32[]{:S(2)}, u32[]{:S(2)}) collective-permute-start(bf16[256,1024]{1,0:T(8,128)(2,1)} %get-tuple-element.86), channel_id=1, source_target_pairs={{0,62},{2,0},{4,2},{6,4},{8,6},{10,8},{12,10},{14,12},{16,14},{18,... | collective-permute-start | bytes 1572872 | tf_op jit(solution)/shard_map/ppermute | solution.py:56
  74.1 2.0 %plane_sum.1 = bf16[64,2048]{1,0:T(8,128)(2,1)} custom-call(bf16[8,64,1536]{2,1,0:T(8,128)(2,1)S(1)} %all-to-all-done.refs_0_, bf16[8,64,512]{2,1,0:T(8,128)(2,1)} %all-to-all-done.1.refs_1_), custom_call_target="tpu_custom_call" | custom-call | flops 900000000 | bytes 1 | tf_op jit(solution)/shard_map/plane_sum/pallas_call | solution.py:29
  76.1 5.9 %all-to-all-start.2 = ((bf16[8,8,2048]{2,1,0:T(8,128)(2,1)}), bf16[8,8,2048]{2,1,0:T(8,128)(2,1)S(1)}, u32[]{:S(2)}, u32[]{:S(2)}) async-start(bf16[8,8,2048]{2,1,0:T(8,128)(2,1)} %bitcast.13), calls=%async_computation.2 | async-start | bytes 524288 | tf_op jit(solution)/shard_map/all_to_all | solution.py:373
  82.0 5.0 %collective-permute-done.8.from_before_ref = bf16[256,1024]{1,0:T(8,128)(2,1)} collective-permute-done((bf16[256,1024]{1,0:T(8,128)(2,1)}, bf16[256,1024]{1,0:T(8,128)(2,1)}, u32[]{:S(2)}, u32[]{:S(2)}) %collective-permute-start.8) | collective-permute-done | bytes 524320 | tf_op jit(solution)/shard_map/ppermute | solution.py:56
  87.0 2.1 %finish.1 = (bf16[384,512]{1,0:T(8,128)(2,1)}, bf16[384,512]{1,0:T(8,128)(2,1)}) custom-call(f32[384,512]{1,0:T(8,128)S(1)} %copy-done.9, f32[384,512]{1,0:T(8,128)S(1)} %copy-done.10, bf16[256,1024]{1,0:T(8,128)(2,1)} %collective-permute-done.8.from_before_ref, bf16[256,1024]{1,0:T(8,128)(2,1)} %collective-permute-done.9.from_after_ref), custom_call_target="tpu_custom_call" | custom-call | flops 1800000000 | bytes 1 | tf_op jit(solution)/shard_map/finish/pallas_call | solution.py:29
  89.1 5.9 %all-to-all-done.2.parts_ref = bf16[8,8,2048]{2,1,0:T(8,128)(2,1)S(1)} async-done(((bf16[8,8,2048]{2,1,0:T(8,128)(2,1)}), bf16[8,8,2048]{2,1,0:T(8,128)(2,1)S(1)}, u32[]{:S(2)}, u32[]{:S(2)}) %all-to-all-start.2) | async-done | bytes 262176 | tf_op jit(solution)/shard_map/all_to_all | solution.py:373
  95.0 0.6 line_sum.1
  (40 shorter events, 0.8 us)
Async XLA Ops:
  0.6 7.4 %copy-start.3 = (bf16[1,384,1024]{2,1,0:T(8,128)(2,1)S(1)}, bf16[1,384,1024]{2,1,0:T(8,128)(2,1)}, u32[]{:S(2)}) copy-start(bf16[1,384,1024]{2,1,0:T(8,128)(2,1)} %param.17) | copy-start | bytes 2359300
  0.6 7.4 %copy-start.2 = (bf16[1,384,1024]{2,1,0:T(8,128)(2,1)S(1)}, bf16[1,384,1024]{2,1,0:T(8,128)(2,1)}, u32[]{:S(2)}) copy-start(bf16[1,384,1024]{2,1,0:T(8,128)(2,1)} %param.15) | copy-start | bytes 2359300
  0.7 7.4 %copy-start.11 = (bf16[31,512]{1,0:T(8,128)(2,1)S(1)}, bf16[31,512]{1,0:T(8,128)(2,1)}, u32[]{:S(2)}) copy-start(bf16[31,512]{1,0:T(8,128)(2,1)} %taps_ref.3) | copy-start | bytes 95236
  3.1 18.9 %collective-permute-start.1 = (bf16[288,1024]{1,0:T(8,128)(2,1)}, bf16[288,1024]{1,0:T(8,128)(2,1)S(1)}, u32[]{:S(2)}, u32[]{:S(2)}) collective-permute-start(bf16[288,1024]{1,0:T(8,128)(2,1)} %get-tuple-element.53), channel_id=1, source_target_pairs={{0,2},{2,4},{4,6},{6,8},{8,10},{10,12},{12,14},{14,16},{16,18},{18... | collective-permute-start | bytes 1769480 | tf_op jit(solution)/shard_map/ppermute | solution.py:56
  4.7 17.4 %collective-permute-start.2 = (bf16[288,1024]{1,0:T(8,128)(2,1)}, bf16[288,1024]{1,0:T(8,128)(2,1)S(1)}, u32[]{:S(2)}, u32[]{:S(2)}) collective-permute-start(bf16[288,1024]{1,0:T(8,128)(2,1)} %get-tuple-element.54), channel_id=1, source_target_pairs={{0,62},{2,0},{4,2},{6,4},{8,6},{10,8},{12,10},{14,12},{16,14},{18,... | collective-permute-start | bytes 1769480 | tf_op jit(solution)/shard_map/ppermute | solution.py:56
  8.0 21.6 %copy-start.12 = (s32[5]{0:T(128)}, s32[5]{0:T(128)S(1)}, u32[]{:S(2)}) copy-start(s32[5]{0:T(128)S(1)} %stack.15.place) | copy-start | bytes 64
  8.1 1.6 %copy-start.4 = (bf16[2,1024,512]{2,1,0:T(8,128)(2,1)S(1)}, bf16[2,1024,512]{2,1,0:T(8,128)(2,1)}, u32[]{:S(2)}) copy-start(bf16[2,1024,512]{2,1,0:T(8,128)(2,1)} %glu_w_ref.3) | copy-start | bytes 6291460
  9.7 1.2 %copy-start.8 = (bf16[512,1024]{1,0:T(8,128)(2,1)S(1)}, bf16[512,1024]{1,0:T(8,128)(2,1)}, u32[]{:S(2)}) copy-start(bf16[512,1024]{1,0:T(8,128)(2,1)} %proj_ref.3) | copy-start | bytes 3145732
  10.9 1.0 %copy-start.15 = (bf16[1,384,512]{2,1,0:T(8,128)(2,1)S(1)}, bf16[1,384,512]{2,1,0:T(8,128)(2,1)}, u32[]{:S(2)}) copy-start(bf16[1,384,512]{2,1,0:T(8,128)(2,1)} %param.16) | copy-start | bytes 1179652
  11.9 10.2 %copy-start.5 = (bf16[2,1024,512]{2,1,0:T(8,128)(2,1)S(1)}, bf16[2,1024,512]{2,1,0:T(8,128)(2,1)}, u32[]{:S(2)}) copy-start(bf16[2,1024,512]{2,1,0:T(8,128)(2,1)} %glu_w_ref.3) | copy-start | bytes 6291460
  18.7 29.6 %collective-permute-start = (bf16[352,1024]{1,0:T(8,128)(2,1)S(1)}, bf16[352,1024]{1,0:T(8,128)(2,1)}, u32[]{:S(2)}, u32[]{:S(2)}) collective-permute-start(bf16[352,1024]{1,0:T(8,128)(2,1)S(1)} %get-tuple-element.52.mid_ref), channel_id=1, source_target_pairs={{0,1},{1,0},{2,3},{3,2},{4,5},{5,4},{6,7},{7,6},{8,9},{9,8},{10,11... | collective-permute-start | bytes 2162696 | tf_op jit(solution)/shard_map/ppermute | solution.py:61
  22.0 2.5 %copy-start = (bf16[288,1024]{1,0:T(8,128)(2,1)}, bf16[288,1024]{1,0:T(8,128)(2,1)S(1)}, u32[]{:S(2)}) copy-start(bf16[288,1024]{1,0:T(8,128)(2,1)S(1)} %collective-permute-done.1.before_ref.kb_ref.vb_ref) | copy-start | bytes 1769476
  22.0 2.5 %copy-start.1 = (bf16[288,1024]{1,0:T(8,128)(2,1)}, bf16[288,1024]{1,0:T(8,128)(2,1)S(1)}, u32[]{:S(2)}) copy-start(bf16[288,1024]{1,0:T(8,128)(2,1)S(1)} %collective-permute-done.2.after_ref.ka_ref.va_ref) | copy-start | bytes 1769476
  26.1 2.4 %collective-permute-start.4 = (bf16[2,256,512]{2,1,0:T(8,128)(2,1)S(1)}, bf16[2,256,512]{2,1,0:T(8,128)(2,1)S(1)}, u32[]{:S(2)}, u32[]{:S(2)}) collective-permute-start(bf16[2,256,512]{2,1,0:T(8,128)(2,1)S(1)} %get-tuple-element.62), channel_id=1, source_target_pairs={{0,64},{64,0},{128,192},{192,128},{1,65},{65,1},{129,193},{193,129... | collective-permute-start | bytes 1572872 | tf_op jit(solution)/shard_map/ppermute | solution.py:61
  26.2 2.6 %collective-permute-start.5 = (bf16[2,256,512]{2,1,0:T(8,128)(2,1)S(1)}, bf16[2,256,512]{2,1,0:T(8,128)(2,1)S(1)}, u32[]{:S(2)}, u32[]{:S(2)}) collective-permute-start(bf16[2,256,512]{2,1,0:T(8,128)(2,1)S(1)} %get-tuple-element.63), channel_id=1, source_target_pairs={{0,64},{64,0},{128,192},{192,128},{1,65},{65,1},{129,193},{193,129... | collective-permute-start | bytes 1572872 | tf_op jit(solution)/shard_map/ppermute | solution.py:61
  26.7 2.9 %collective-permute-start.6 = (bf16[2,256,512]{2,1,0:T(8,128)(2,1)S(1)}, bf16[2,256,512]{2,1,0:T(8,128)(2,1)S(1)}, u32[]{:S(2)}, u32[]{:S(2)}) collective-permute-start(bf16[2,256,512]{2,1,0:T(8,128)(2,1)S(1)} %get-tuple-element.64), channel_id=1, source_target_pairs={{0,64},{64,0},{128,192},{192,128},{1,65},{65,1},{129,193},{193,129... | collective-permute-start | bytes 1572872 | tf_op jit(solution)/shard_map/ppermute | solution.py:61
  26.8 21.6 %collective-permute-start.3 = (bf16[32,1024]{1,0:T(8,128)(2,1)}, bf16[32,1024]{1,0:T(8,128)(2,1)}, u32[]{:S(2)}, u32[]{:S(2)}) collective-permute-start(bf16[32,1024]{1,0:T(8,128)(2,1)} %get-tuple-element.59.part_ref), channel_id=1, source_target_pairs={{0,1},{1,0},{2,3},{3,2},{4,5},{5,4},{6,7},{7,6},{8,9},{9,8},{10,11... | collective-permute-start | bytes 196616 | tf_op jit(solution)/shard_map/ppermute | solution.py:61
  32.1 28.1 %all-to-all-start = ((bf16[8,64,1536]{2,1,0:T(8,128)(2,1)}), bf16[8,64,1536]{2,1,0:T(8,128)(2,1)S(1)}, u32[]{:S(2)}, u32[]{:S(2)}) async-start(bf16[8,64,1536]{2,1,0:T(8,128)(2,1)} %terms.3), calls=%async_computation | async-start | bytes 3145728 | tf_op jit(solution)/shard_map/all_to_all | solution.py:373
  39.7 8.7 %copy-start.13 = (s32[5]{0:T(128)S(1)}, s32[5]{0:T(128)}, u32[]{:S(2)}) copy-start(s32[5]{0:T(128)} %copy-done.12) | copy-start | bytes 64
  39.7 8.7 %copy-start.14 = (bf16[512,1024]{1,0:T(8,128)(2,1)S(1)}, bf16[512,1024]{1,0:T(8,128)(2,1)}, u32[]{:S(2)}) copy-start(bf16[512,1024]{1,0:T(8,128)(2,1)} %weight_ref.1) | copy-start | bytes 3145732
  48.4 1.0 %copy-start.6 = (bf16[384,512]{1,0:T(8,128)(2,1)S(1)}, bf16[384,512]{1,0:T(8,128)(2,1)}, u32[]{:S(2)}) copy-start(bf16[384,512]{1,0:T(8,128)(2,1)} %get-tuple-element.66.attended_ref.out_ref) | copy-start | bytes 1179652
  52.3 0.7 copy-start.7
  53.1 5.0 %collective-permute-start.7 = (bf16[2,256,512]{2,1,0:T(8,128)(2,1)S(1)}, bf16[2,256,512]{2,1,0:T(8,128)(2,1)S(1)}, u32[]{:S(2)}, u32[]{:S(2)}) collective-permute-start(bf16[2,256,512]{2,1,0:T(8,128)(2,1)S(1)} %get-tuple-element.71), channel_id=1, source_target_pairs={{0,64},{64,0},{128,192},{192,128},{1,65},{65,1},{129,193},{193,129... | collective-permute-start | bytes 1572872 | tf_op jit(solution)/shard_map/ppermute | solution.py:61
  60.1 13.9 %all-to-all-start.1 = ((bf16[8,64,512]{2,1,0:T(8,128)(2,1)}), bf16[8,64,512]{2,1,0:T(8,128)(2,1)}, u32[]{:S(2)}, u32[]{:S(2)}) async-start(bf16[8,64,512]{2,1,0:T(8,128)(2,1)} %add.7), calls=%async_computation.1 | async-start | bytes 1048576 | tf_op jit(solution)/shard_map/all_to_all | solution.py:373
  69.7 17.3 %copy-start.9 = (f32[384,512]{1,0:T(8,128)S(1)}, f32[384,512]{1,0:T(8,128)}, u32[]{:S(2)}) copy-start(f32[384,512]{1,0:T(8,128)} %get-tuple-element.83.dk_ref) | copy-start | bytes 2359300
  69.7 17.3 %copy-start.10 = (f32[384,512]{1,0:T(8,128)S(1)}, f32[384,512]{1,0:T(8,128)}, u32[]{:S(2)}) copy-start(f32[384,512]{1,0:T(8,128)} %get-tuple-element.84.dv_ref) | copy-start | bytes 2359300
  69.7 17.3 %collective-permute-start.8 = (bf16[256,1024]{1,0:T(8,128)(2,1)}, bf16[256,1024]{1,0:T(8,128)(2,1)}, u32[]{:S(2)}, u32[]{:S(2)}) collective-permute-start(bf16[256,1024]{1,0:T(8,128)(2,1)} %get-tuple-element.85), channel_id=1, source_target_pairs={{0,2},{2,4},{4,6},{6,8},{8,10},{10,12},{12,14},{14,16},{16,18},{18... | collective-permute-start | bytes 1572872 | tf_op jit(solution)/shard_map/ppermute | solution.py:56
  71.3 15.8 %collective-permute-start.9 = (bf16[256,1024]{1,0:T(8,128)(2,1)}, bf16[256,1024]{1,0:T(8,128)(2,1)}, u32[]{:S(2)}, u32[]{:S(2)}) collective-permute-start(bf16[256,1024]{1,0:T(8,128)(2,1)} %get-tuple-element.86), channel_id=1, source_target_pairs={{0,62},{2,0},{4,2},{6,4},{8,6},{10,8},{12,10},{14,12},{16,14},{18,... | collective-permute-start | bytes 1572872 | tf_op jit(solution)/shard_map/ppermute | solution.py:56
  76.1 18.9 %all-to-all-start.2 = ((bf16[8,8,2048]{2,1,0:T(8,128)(2,1)}), bf16[8,8,2048]{2,1,0:T(8,128)(2,1)S(1)}, u32[]{:S(2)}, u32[]{:S(2)}) async-start(bf16[8,8,2048]{2,1,0:T(8,128)(2,1)} %bitcast.13), calls=%async_computation.2 | async-start | bytes 524288 | tf_op jit(solution)/shard_map/all_to_all | solution.py:373

commit v6 on v5

--- a/solution.py
+++ b/solution.py
@@ -61,26 +61,29 @@
     return lax.ppermute(value, axis, [(i, i ^ stride) for i in range(count)])
 
 
-def pack_kernel(k_ref, v_ref, grad_ref, pre_ref, up_ref, down_ref, sems):
+def pack_kernel(k_ref, v_ref, grad_ref, pre_ref, up_hbm, down_hbm, up_ref, down_ref, in_sems, out_sems):
     frames, cols = k_ref.shape
-    copies = []
-    for out_ref, start, edge in ((up_ref, frames - WIN, frames - EDGE), (down_ref, 0, 0)):
+    arriving, leaving = [], []
+    for out_hbm, out_ref, start, edge in (
+        (up_hbm, up_ref, frames - WIN, frames - EDGE), (down_hbm, down_ref, 0, 0)
+    ):
         for source, rows, count, first, span in (
             (k_ref, 0, WIN, start, slice(0, cols)),
             (v_ref, 0, WIN, start, slice(cols, 2 * cols)),
             (grad_ref, WIN, EDGE, edge, slice(0, 2 * cols)),
             (pre_ref, WIN + EDGE, EDGE, edge, slice(0, cols)),
+            (pre_ref, WIN + EDGE, EDGE, edge, slice(cols, 2 * cols)),
         ):
-            copies.append(
-                pltpu.make_async_copy(
-                    source.at[pl.ds(first, count)], out_ref.at[pl.ds(rows, count), span], sems.at[len(copies)]
-                )
-            )
-    for copy in copies:
+            i = len(arriving)
+            target = out_ref.at[pl.ds(rows, count), span]
+            arriving.append(pltpu.make_async_copy(source.at[pl.ds(first, count)], target, in_sems.at[i]))
+            leaving.append(pltpu.make_async_copy(target, out_hbm.at[pl.ds(rows, count), span], out_sems.at[i]))
+    for copy in arriving:
         copy.start()
-    for out_ref in (up_ref, down_ref):
-        out_ref[WIN + EDGE :, cols:] = jnp.zeros((EDGE, cols), LOW)
-    for copy in copies:
+    for before, after in zip(arriving, leaving):
+        before.wait()
+        after.start()
+    for copy in leaving:
         copy.wait()
 
 
@@ -88,7 +91,8 @@
     dims = (WIN + 2 * EDGE, 2 * k_rows.shape[1])
     return call(
         pack_kernel, "pack", (k_rows, v_rows, out_rows, pre_rows), [HBM] * 4, [shape(dims)] * 2,
-        scratch=[pltpu.SemaphoreType.DMA((8,))], limit=58,
+        out_specs=[HBM] * 2,
+        scratch=[pltpu.VMEM(dims, LOW)] * 2 + [pltpu.SemaphoreType.DMA((10,))] * 2, limit=58,
     )
 
 
@@ -337,6 +341,10 @@
     *sources, sum_ref = refs
     at = 0
     for parts_ref in sources:
+        if parts_ref.ndim == 2:
+            at = parts_ref.shape[1]
+            sum_ref[:, :at] = parts_ref[...]
+            continue
         for start in range(0, parts_ref.shape[2], 256):
             lanes = slice(start, start + 256)
             total = parts_ref[0, :, lanes].astype(FULL)
@@ -347,7 +355,7 @@
 
 
 def plane_sum(*parts):
-    dims = (parts[0].shape[1], sum(part.shape[2] for part in parts))
+    dims = (parts[0].shape[-2], sum(part.shape[-1] for part in parts))
     return call(plane_kernel, "plane_sum", parts, [VMEM] * len(parts), [shape(dims)])[0]
 
 
@@ -592,7 +600,7 @@
     grad_query, grad_key, grad_value, to_before, to_after = attend_grad(*operands, 2, 2, early)
     from_after, from_before = (round_ring(to_before, -1), round_ring(to_after, 1))
     on_chip_out, rest = lax.optimization_barrier((on_chip_out, rest))
-    plane = plane_sum(rest, exchanged(on_chip_out, by_plane))
+    plane = plane_sum(plane_sum(rest), exchanged(on_chip_out, by_plane))
     out_sum, glu_sum, proj_sum = line_sum(exchanged(plane.reshape(2 * far, -1, plane.shape[1]), by_line))
     key_grad, value_grad = finish(grad_key, grad_value, from_before, from_after)
     return (

time: 96.8 us -> 96.6 us (level)
  Pallas kernels: 42.9 us -> 40.9 us
  waiting for transfers between devices: 13.4 us -> 15.2 us
    pallas_call x13 -> x14, Pallas kernels: 42.9 us -> 40.9 us  [call(): pl.pallas_call(kernel, in_specs=in_specs, out_specs=[VMEM] * len(out_shap...]
    ppermute x4, waiting for transfers between devices: 5.04 us -> 6.03 us  [round_ring(): lax.ppermute(value, 'seq', [(i, (i + steps) % count) for i in range(count)])]
  transfers between devices with their start and end apart: 13 -> 13, of which waited for: 6 -> 5; matrix products, arithmetic and copies ran while one was open for 0% -> 0% of each run, Pallas kernels for 42% -> 40%
where the time goes in v6:
time: 96.6 us; the launch traced here: 95.5 us
  Pallas kernels  40.9 us (42%)
  starting transfers between devices  32.2 us (33%)
  waiting for transfers between devices  15.2 us (16%)
  local copies, waits for them, and re-layouts  5.67 us (6%)
  between operations  1.5 us (2%)
    pallas_call x14, Pallas kernels, call(): pl.pallas_call(kernel, in_specs=in_specs, out_specs=[VMEM] * len(out_shap...  40.9 us
    all_to_all x3, starting transfers between devices, exchanged(): return lax.all_to_all(parts, ('dp', 'seq'), 0, 0, axis_index_groups=groups)  18.1 us
    ppermute x4, starting transfers between devices, round_ring(): lax.ppermute(value, 'seq', [(i, (i + steps) % count) for i in range(count)])  8.43 us
    all_to_all x3, waiting for transfers between devices, exchanged(): return lax.all_to_all(parts, ('dp', 'seq'), 0, 0, axis_index_groups=groups)  8.12 us
    ppermute x4, waiting for transfers between devices, round_ring(): lax.ppermute(value, 'seq', [(i, (i + steps) % count) for i in range(count)])  6.03 us
    ppermute x6, starting transfers between devices, swapped(): return lax.ppermute(value, axis, [(i, i ^ stride) for i in range(count)])  5.68 us
    unnamed x32, local copies, waits for them, and re-layouts  5.58 us
  transfers between devices with their start and end apart: 13, of which 5 were waited for; matrix products, arithmetic and copies ran while one was open for 0% of the time, Pallas kernels for 40%

profile of v6, /device:TPU:32, one launch (start us, length us, event | category | flops | bytes accessed | tf_op | source)
XLA Modules:
  0.0 95.5 jit_solution(17039012369488775763)
XLA Ops:
  0.7 2.3 %pack.1 = (bf16[288,1024]{1,0:T(8,128)(2,1)}, bf16[288,1024]{1,0:T(8,128)(2,1)}) custom-call(bf16[384,512]{1,0:T(8,128)(2,1)} %bitcast.26, bf16[384,512]{1,0:T(8,128)(2,1)} %bitcast.30, bf16[384,1024]{1,0:T(8,128)(2,1)} %bitcast.19, bf16[384,512]{1,0:T(8,128)(2,1)} %bitcast.24), custom_call_target="tpu_custom_call" | custom-call | flops 900000000 | bytes 1 | tf_op jit(solution)/shard_map/pack/pallas_call | solution.py:29
  2.9 1.6 %collective-permute-start.1 = (bf16[288,1024]{1,0:T(8,128)(2,1)}, bf16[288,1024]{1,0:T(8,128)(2,1)S(1)}, u32[]{:S(2)}, u32[]{:S(2)}) collective-permute-start(bf16[288,1024]{1,0:T(8,128)(2,1)} %get-tuple-element.53), channel_id=1, source_target_pairs={{0,2},{2,4},{4,6},{6,8},{8,10},{10,12},{12,14},{14,16},{16,18},{18... | collective-permute-start | bytes 1769480 | tf_op jit(solution)/shard_map/ppermute | solution.py:56
  4.5 2.6 %collective-permute-start.2 = (bf16[288,1024]{1,0:T(8,128)(2,1)}, bf16[288,1024]{1,0:T(8,128)(2,1)S(1)}, u32[]{:S(2)}, u32[]{:S(2)}) collective-permute-start(bf16[288,1024]{1,0:T(8,128)(2,1)} %get-tuple-element.54), channel_id=1, source_target_pairs={{0,62},{2,0},{4,2},{6,4},{8,6},{10,8},{12,10},{14,12},{16,14},{18,... | collective-permute-start | bytes 1769480 | tf_op jit(solution)/shard_map/ppermute | solution.py:56
  7.9 1.6 %copy-done.4 = bf16[2,1024,512]{2,1,0:T(8,128)(2,1)S(1)} copy-done((bf16[2,1024,512]{2,1,0:T(8,128)(2,1)S(1)}, bf16[2,1024,512]{2,1,0:T(8,128)(2,1)}, u32[]{:S(2)}) %copy-start.4) | copy-done | bytes 2097176
  9.5 1.2 %copy-done.8 = bf16[512,1024]{1,0:T(8,128)(2,1)S(1)} copy-done((bf16[512,1024]{1,0:T(8,128)(2,1)S(1)}, bf16[512,1024]{1,0:T(8,128)(2,1)}, u32[]{:S(2)}) %copy-start.8) | copy-done | bytes 1048600
  10.7 1.0 %copy-done.15 = bf16[1,384,512]{2,1,0:T(8,128)(2,1)S(1)} copy-done((bf16[1,384,512]{2,1,0:T(8,128)(2,1)S(1)}, bf16[1,384,512]{2,1,0:T(8,128)(2,1)}, u32[]{:S(2)}) %copy-start.15) | copy-done | bytes 393240
  11.7 6.9 %front.1 = (bf16[352,1024]{1,0:T(8,128)(2,1)S(1)}, bf16[384,1024]{1,0:T(8,128)(2,1)S(1)}, bf16[384,512]{1,0:T(8,128)(2,1)S(1)}, bf16[64,512]{1,0:T(8,128)(2,1)S(...) custom-call(s32[5]{0:T(128)S(1)} %stack.15.place, bf16[384,1024]{1,0:T(8,128)(2,1)S(1)} %bitcast.20, ...), custom_call_target="tpu_custom_call" | custom-call | flops 6300000256 | bytes 1 | tf_op jit(solution)/shard_map/front/pallas_call | solution.py:29
  18.6 3.3 %collective-permute-start = (bf16[352,1024]{1,0:T(8,128)(2,1)S(1)}, bf16[352,1024]{1,0:T(8,128)(2,1)}, u32[]{:S(2)}, u32[]{:S(2)}) collective-permute-start(bf16[352,1024]{1,0:T(8,128)(2,1)S(1)} %get-tuple-element.52.mid_ref), channel_id=1, source_target_pairs={{0,1},{1,0},{2,3},{3,2},{4,5},{5,4},{6,7},{7,6},{8,9},{9,8},{10,11... | collective-permute-start | bytes 2162696 | tf_op jit(solution)/shard_map/ppermute | solution.py:61
  21.9 2.5 %rim.1 = (bf16[32,1024]{1,0:T(8,128)(2,1)}, bf16[384,1024]{1,0:T(8,128)(2,1)S(1)}) custom-call(s32[5]{0:T(128)S(1)} %stack.15.place, bf16[288,1024]{1,0:T(8,128)(2,1)S(1)} %collective-permute-done.1.before_ref.kb_ref.vb_ref, bf16[288,1024]{1,0:T(8,128)(2,1)S(1)} %collective-permute-done.2.after_ref.ka_ref.va_ref, ...), custom_call_target="tpu_custom_call", output_to_operand_aliasing={{1}: (9, {})} | custom-call | flops 90000000 | bytes 1 | tf_op jit(solution)/shard_map/rim/pallas_call | solution.py:29
  24.4 1.6 %terms.2 = (bf16[2,256,512]{2,1,0:T(8,128)(2,1)S(1)}, bf16[2,256,512]{2,1,0:T(8,128)(2,1)S(1)}, bf16[2,256,512]{2,1,0:T(8,128)(2,1)S(1)}) custom-call(s32[5]{0:T(128)S(1)} %stack.15.place, bf16[384,1024]{1,0:T(8,128)(2,1)S(1)} %bitcast.17, bf16[384,1024]{1,0:T(8,128)(2,1)S(1)} %get-tuple-element.60.glu_ref, bf16[384,1024]{1,0:T(8,128)(2,1)S(1)} %bitcast.21, ...), custom_call_target="tpu_custom_call" | custom-call | flops 90000000 | bytes 1 | tf_op jit(solution)/shard_map/terms/pallas_call | solution.py:29
  26.1 0.5 collective-permute-start.5
  26.7 1.7 %collective-permute-start.3 = (bf16[32,1024]{1,0:T(8,128)(2,1)}, bf16[32,1024]{1,0:T(8,128)(2,1)}, u32[]{:S(2)}, u32[]{:S(2)}) collective-permute-start(bf16[32,1024]{1,0:T(8,128)(2,1)} %get-tuple-element.59.part_ref), channel_id=1, source_target_pairs={{0,1},{1,0},{2,3},{3,2},{4,5},{5,4},{6,7},{7,6},{8,9},{9,8},{10,11... | collective-permute-start | bytes 196616 | tf_op jit(solution)/shard_map/ppermute | solution.py:61
  28.7 0.7 collective-permute-done.6.refs_2_
  29.5 2.4 %terms.3 = bf16[8,64,1536]{2,1,0:T(8,128)(2,1)} custom-call(s32[5]{0:T(128)S(1)} %stack.15.place, bf16[384,1024]{1,0:T(8,128)(2,1)S(1)} %bitcast.18, bf16[384,1024]{1,0:T(8,128)(2,1)S(1)} %get-tuple-element.60.glu_ref, bf16[384,1024]{1,0:T(8,128)(2,1)S(1)} %bitcast.22, bf16[384,512]{1,0:T(8,128)(2,1)S(1)} %get-tuple-element.61.act_ref, ...), custom_call_target="tpu_custom_call" | custom-call | flops 90000000 | bytes 1 | tf_op jit(solution)/shard_map/terms/pallas_call | solution.py:29
  31.9 7.6 %all-to-all-start = ((bf16[8,64,1536]{2,1,0:T(8,128)(2,1)}), bf16[8,64,1536]{2,1,0:T(8,128)(2,1)S(1)}, u32[]{:S(2)}, u32[]{:S(2)}) async-start(bf16[8,64,1536]{2,1,0:T(8,128)(2,1)} %terms.3), calls=%async_computation | async-start | bytes 3145728 | tf_op jit(solution)/shard_map/all_to_all | solution.py:381
  39.5 8.7 %attend.1 = (bf16[4,3,640,256]{3,2,1,0:T(8,128)(2,1)}, bf16[384,512]{1,0:T(8,128)(2,1)}, f32[384,512]{1,0:T(8,128)}) custom-call(s32[5]{0:T(128)} %copy-done.12, bf16[384,512]{1,0:T(8,128)(2,1)} %bitcast.34, bf16[384,512]{1,0:T(8,128)(2,1)} %bitcast.27, bf16[384,512]{1,0:T(8,128)(2,1)} %bitcast.31, bf16[288,1024]{1,0:T(8,128)(2,1)} %copy-done, ...), custom_call_target="tpu_custom_call" | custom-call | flops 450000000 | bytes 1 | tf_op jit(solution)/shard_map/attend/pallas_call | solution.py:29
  48.3 1.0 %copy-done.6 = bf16[384,512]{1,0:T(8,128)(2,1)S(1)} copy-done((bf16[384,512]{1,0:T(8,128)(2,1)S(1)}, bf16[384,512]{1,0:T(8,128)(2,1)}, u32[]{:S(2)}) %copy-start.6) | copy-done | bytes 393240
  49.3 2.9 %resid.1 = (bf16[384,1024]{1,0:T(8,128)(2,1)}, bf16[384,512]{1,0:T(8,128)(2,1)S(1)}, bf16[2,256,512]{2,1,0:T(8,128)(2,1)S(1)}, bf16[2,256,512]{2,1,0:T(8,128)(2,1)S(1)}) custom-call(s32[5]{0:T(128)S(1)} %copy-done.13, bf16[384,1024]{1,0:T(8,128)(2,1)S(1)} %bitcast.23, bf16[352,1024]{1,0:T(8,128)(2,1)S(1)} %get-tuple-element.52.mid_ref, ...), custom_call_target="tpu_custom_call" | custom-call | flops 54000001024 | bytes 1 | tf_op jit(solution)/shard_map/resid/pallas_call | solution.py:29
  52.2 0.7 copy-done.7
  52.9 5.0 %attend_grad.2 = (bf16[384,512]{1,0:T(8,128)(2,1)}, f32[384,512]{1,0:T(8,128)}, f32[384,512]{1,0:T(8,128)}, bf16[256,1024]{1,0:T(8,128)(2,1)}, bf16[256,1024]{1,0:T(8,128)(2,1)}) custom-call(bf16[384,512]{1,0:T(8,128)(2,1)} %bitcast.35, bf16[384,512]{1,0:T(8,128)(2,1)} %bitcast.28, bf16[384,512]{1,0:T(8,128)(2,1)} %bitcast.32, bf16[288,1024]{1,0:T(8,128)(2,1)} %copy-done, ...), custom_call_target="tpu_custom_call" | custom-call | flops 900000000 | bytes 1 | tf_op jit(solution)/shard_map/attend_grad/pallas_call | solution.py:29
  57.9 0.9 add.7
  58.8 1.2 %all-to-all-done.refs_0_ = bf16[8,64,1536]{2,1,0:T(8,128)(2,1)S(1)} async-done(((bf16[8,64,1536]{2,1,0:T(8,128)(2,1)}), bf16[8,64,1536]{2,1,0:T(8,128)(2,1)S(1)}, u32[]{:S(2)}, u32[]{:S(2)}) %all-to-all-start) | async-done | bytes 1572896 | tf_op jit(solution)/shard_map/all_to_all | solution.py:381
  60.0 4.6 %all-to-all-start.1 = ((bf16[8,64,512]{2,1,0:T(8,128)(2,1)}), bf16[8,64,512]{2,1,0:T(8,128)(2,1)S(1)}, u32[]{:S(2)}, u32[]{:S(2)}) async-start(bf16[8,64,512]{2,1,0:T(8,128)(2,1)} %add.7), calls=%async_computation.1 | async-start | bytes 1048576 | tf_op jit(solution)/shard_map/all_to_all | solution.py:381
  64.6 5.0 %attend_grad.3 = (bf16[384,512]{1,0:T(8,128)(2,1)}, f32[384,512]{1,0:T(8,128)}, f32[384,512]{1,0:T(8,128)}, bf16[256,1024]{1,0:T(8,128)(2,1)}, bf16[256,1024]{1,0:T(8,128)(2,1)}) custom-call(bf16[384,512]{1,0:T(8,128)(2,1)} %bitcast.36, bf16[384,512]{1,0:T(8,128)(2,1)} %bitcast.29, ...), custom_call_target="tpu_custom_call", output_to_operand_aliasing={{0}: (11, {}), {1}: (12, {}), {2}: (13, {}), {3}: (14, {}),... | custom-call | flops 900000000 | bytes 1 | tf_op jit(solution)/shard_map/attend_grad/pallas_call | solution.py:29
  69.6 1.5 %collective-permute-start.8 = (bf16[256,1024]{1,0:T(8,128)(2,1)}, bf16[256,1024]{1,0:T(8,128)(2,1)S(1)}, u32[]{:S(2)}, u32[]{:S(2)}) collective-permute-start(bf16[256,1024]{1,0:T(8,128)(2,1)} %get-tuple-element.85), channel_id=1, source_target_pairs={{0,2},{2,4},{4,6},{6,8},{8,10},{10,12},{12,14},{14,16},{16,18},{18... | collective-permute-start | bytes 1572872 | tf_op jit(solution)/shard_map/ppermute | solution.py:56
  71.1 2.7 %collective-permute-start.9 = (bf16[256,1024]{1,0:T(8,128)(2,1)}, bf16[256,1024]{1,0:T(8,128)(2,1)S(1)}, u32[]{:S(2)}, u32[]{:S(2)}) collective-permute-start(bf16[256,1024]{1,0:T(8,128)(2,1)} %get-tuple-element.86), channel_id=1, source_target_pairs={{0,62},{2,0},{4,2},{6,4},{8,6},{10,8},{12,10},{14,12},{16,14},{18,... | collective-permute-start | bytes 1572872 | tf_op jit(solution)/shard_map/ppermute | solution.py:56
  74.0 0.8 plane_sum.3
  74.8 5.9 %all-to-all-start.2 = ((bf16[8,8,2048]{2,1,0:T(8,128)(2,1)}), bf16[8,8,2048]{2,1,0:T(8,128)(2,1)S(1)}, u32[]{:S(2)}, u32[]{:S(2)}) async-start(bf16[8,8,2048]{2,1,0:T(8,128)(2,1)} %bitcast.13), calls=%async_computation.2 | async-start | bytes 524288 | tf_op jit(solution)/shard_map/all_to_all | solution.py:381
  80.8 6.0 %collective-permute-done.8.from_before_ref = bf16[256,1024]{1,0:T(8,128)(2,1)S(1)} collective-permute-done((bf16[256,1024]{1,0:T(8,128)(2,1)}, bf16[256,1024]{1,0:T(8,128)(2,1)S(1)}, u32[]{:S(2)}, u32[]{:S(2)}) %collective-permute-start.8) | collective-permute-done | bytes 524320 | tf_op jit(solution)/shard_map/ppermute | solution.py:56
  86.8 1.2 %finish.1 = (bf16[384,512]{1,0:T(8,128)(2,1)}, bf16[384,512]{1,0:T(8,128)(2,1)}) custom-call(f32[384,512]{1,0:T(8,128)S(1)} %copy-done.9, f32[384,512]{1,0:T(8,128)S(1)} %copy-done.10, bf16[256,1024]{1,0:T(8,128)(2,1)S(1)} %collective-permute-done.8.from_before_ref, bf16[256,1024]{1,0:T(8,128)(2,1)S(1)} %collective-permute-done.9.from_after_ref), custom_call_target="tpu_custom_call" | custom-call | flops 1800000000 | bytes 1 | tf_op jit(solution)/shard_map/finish/pallas_call | solution.py:29
  87.9 7.0 %all-to-all-done.2.parts_ref = bf16[8,8,2048]{2,1,0:T(8,128)(2,1)S(1)} async-done(((bf16[8,8,2048]{2,1,0:T(8,128)(2,1)}), bf16[8,8,2048]{2,1,0:T(8,128)(2,1)S(1)}, u32[]{:S(2)}, u32[]{:S(2)}) %all-to-all-start.2) | async-done | bytes 262176 | tf_op jit(solution)/shard_map/all_to_all | solution.py:381
  94.9 0.6 line_sum.1
  (41 shorter events, 0.9 us)
Async XLA Ops:
  0.6 7.3 %copy-start.3 = (bf16[1,384,1024]{2,1,0:T(8,128)(2,1)S(1)}, bf16[1,384,1024]{2,1,0:T(8,128)(2,1)}, u32[]{:S(2)}) copy-start(bf16[1,384,1024]{2,1,0:T(8,128)(2,1)} %param.17) | copy-start | bytes 2359300
  0.6 7.3 %copy-start.2 = (bf16[1,384,1024]{2,1,0:T(8,128)(2,1)S(1)}, bf16[1,384,1024]{2,1,0:T(8,128)(2,1)}, u32[]{:S(2)}) copy-start(bf16[1,384,1024]{2,1,0:T(8,128)(2,1)} %param.15) | copy-start | bytes 2359300
  0.7 7.2 %copy-start.11 = (bf16[31,512]{1,0:T(8,128)(2,1)S(1)}, bf16[31,512]{1,0:T(8,128)(2,1)}, u32[]{:S(2)}) copy-start(bf16[31,512]{1,0:T(8,128)(2,1)} %taps_ref.3) | copy-start | bytes 95236
  2.9 18.9 %collective-permute-start.1 = (bf16[288,1024]{1,0:T(8,128)(2,1)}, bf16[288,1024]{1,0:T(8,128)(2,1)S(1)}, u32[]{:S(2)}, u32[]{:S(2)}) collective-permute-start(bf16[288,1024]{1,0:T(8,128)(2,1)} %get-tuple-element.53), channel_id=1, source_target_pairs={{0,2},{2,4},{4,6},{6,8},{8,10},{10,12},{12,14},{14,16},{16,18},{18... | collective-permute-start | bytes 1769480 | tf_op jit(solution)/shard_map/ppermute | solution.py:56
  4.5 17.4 %collective-permute-start.2 = (bf16[288,1024]{1,0:T(8,128)(2,1)}, bf16[288,1024]{1,0:T(8,128)(2,1)S(1)}, u32[]{:S(2)}, u32[]{:S(2)}) collective-permute-start(bf16[288,1024]{1,0:T(8,128)(2,1)} %get-tuple-element.54), channel_id=1, source_target_pairs={{0,62},{2,0},{4,2},{6,4},{8,6},{10,8},{12,10},{14,12},{16,14},{18,... | collective-permute-start | bytes 1769480 | tf_op jit(solution)/shard_map/ppermute | solution.py:56
  7.9 21.6 %copy-start.12 = (s32[5]{0:T(128)}, s32[5]{0:T(128)S(1)}, u32[]{:S(2)}) copy-start(s32[5]{0:T(128)S(1)} %stack.15.place) | copy-start | bytes 64
  7.9 1.6 %copy-start.4 = (bf16[2,1024,512]{2,1,0:T(8,128)(2,1)S(1)}, bf16[2,1024,512]{2,1,0:T(8,128)(2,1)}, u32[]{:S(2)}) copy-start(bf16[2,1024,512]{2,1,0:T(8,128)(2,1)} %glu_w_ref.3) | copy-start | bytes 6291460
  9.5 1.2 %copy-start.8 = (bf16[512,1024]{1,0:T(8,128)(2,1)S(1)}, bf16[512,1024]{1,0:T(8,128)(2,1)}, u32[]{:S(2)}) copy-start(bf16[512,1024]{1,0:T(8,128)(2,1)} %proj_ref.3) | copy-start | bytes 3145732
  10.7 1.0 %copy-start.15 = (bf16[1,384,512]{2,1,0:T(8,128)(2,1)S(1)}, bf16[1,384,512]{2,1,0:T(8,128)(2,1)}, u32[]{:S(2)}) copy-start(bf16[1,384,512]{2,1,0:T(8,128)(2,1)} %param.16) | copy-start | bytes 1179652
  11.7 10.2 %copy-start.5 = (bf16[2,1024,512]{2,1,0:T(8,128)(2,1)S(1)}, bf16[2,1024,512]{2,1,0:T(8,128)(2,1)}, u32[]{:S(2)}) copy-start(bf16[2,1024,512]{2,1,0:T(8,128)(2,1)} %glu_w_ref.3) | copy-start | bytes 6291460
  18.6 29.6 %collective-permute-start = (bf16[352,1024]{1,0:T(8,128)(2,1)S(1)}, bf16[352,1024]{1,0:T(8,128)(2,1)}, u32[]{:S(2)}, u32[]{:S(2)}) collective-permute-start(bf16[352,1024]{1,0:T(8,128)(2,1)S(1)} %get-tuple-element.52.mid_ref), channel_id=1, source_target_pairs={{0,1},{1,0},{2,3},{3,2},{4,5},{5,4},{6,7},{7,6},{8,9},{9,8},{10,11... | collective-permute-start | bytes 2162696 | tf_op jit(solution)/shard_map/ppermute | solution.py:61
  21.9 2.5 %copy-start = (bf16[288,1024]{1,0:T(8,128)(2,1)}, bf16[288,1024]{1,0:T(8,128)(2,1)S(1)}, u32[]{:S(2)}) copy-start(bf16[288,1024]{1,0:T(8,128)(2,1)S(1)} %collective-permute-done.1.before_ref.kb_ref.vb_ref) | copy-start | bytes 1769476
  21.9 2.5 %copy-start.1 = (bf16[288,1024]{1,0:T(8,128)(2,1)}, bf16[288,1024]{1,0:T(8,128)(2,1)S(1)}, u32[]{:S(2)}) copy-start(bf16[288,1024]{1,0:T(8,128)(2,1)S(1)} %collective-permute-done.2.after_ref.ka_ref.va_ref) | copy-start | bytes 1769476
  26.0 2.4 %collective-permute-start.4 = (bf16[2,256,512]{2,1,0:T(8,128)(2,1)S(1)}, bf16[2,256,512]{2,1,0:T(8,128)(2,1)S(1)}, u32[]{:S(2)}, u32[]{:S(2)}) collective-permute-start(bf16[2,256,512]{2,1,0:T(8,128)(2,1)S(1)} %get-tuple-element.62), channel_id=1, source_target_pairs={{0,64},{64,0},{128,192},{192,128},{1,65},{65,1},{129,193},{193,129... | collective-permute-start | bytes 1572872 | tf_op jit(solution)/shard_map/ppermute | solution.py:61
  26.1 2.6 %collective-permute-start.5 = (bf16[2,256,512]{2,1,0:T(8,128)(2,1)S(1)}, bf16[2,256,512]{2,1,0:T(8,128)(2,1)S(1)}, u32[]{:S(2)}, u32[]{:S(2)}) collective-permute-start(bf16[2,256,512]{2,1,0:T(8,128)(2,1)S(1)} %get-tuple-element.63), channel_id=1, source_target_pairs={{0,64},{64,0},{128,192},{192,128},{1,65},{65,1},{129,193},{193,129... | collective-permute-start | bytes 1572872 | tf_op jit(solution)/shard_map/ppermute | solution.py:61
  26.6 2.9 %collective-permute-start.6 = (bf16[2,256,512]{2,1,0:T(8,128)(2,1)S(1)}, bf16[2,256,512]{2,1,0:T(8,128)(2,1)S(1)}, u32[]{:S(2)}, u32[]{:S(2)}) collective-permute-start(bf16[2,256,512]{2,1,0:T(8,128)(2,1)S(1)} %get-tuple-element.64), channel_id=1, source_target_pairs={{0,64},{64,0},{128,192},{192,128},{1,65},{65,1},{129,193},{193,129... | collective-permute-start | bytes 1572872 | tf_op jit(solution)/shard_map/ppermute | solution.py:61
  26.7 21.6 %collective-permute-start.3 = (bf16[32,1024]{1,0:T(8,128)(2,1)}, bf16[32,1024]{1,0:T(8,128)(2,1)}, u32[]{:S(2)}, u32[]{:S(2)}) collective-permute-start(bf16[32,1024]{1,0:T(8,128)(2,1)} %get-tuple-element.59.part_ref), channel_id=1, source_target_pairs={{0,1},{1,0},{2,3},{3,2},{4,5},{5,4},{6,7},{7,6},{8,9},{9,8},{10,11... | collective-permute-start | bytes 196616 | tf_op jit(solution)/shard_map/ppermute | solution.py:61
  31.9 28.1 %all-to-all-start = ((bf16[8,64,1536]{2,1,0:T(8,128)(2,1)}), bf16[8,64,1536]{2,1,0:T(8,128)(2,1)S(1)}, u32[]{:S(2)}, u32[]{:S(2)}) async-start(bf16[8,64,1536]{2,1,0:T(8,128)(2,1)} %terms.3), calls=%async_computation | async-start | bytes 3145728 | tf_op jit(solution)/shard_map/all_to_all | solution.py:381
  39.5 8.7 %copy-start.13 = (s32[5]{0:T(128)S(1)}, s32[5]{0:T(128)}, u32[]{:S(2)}) copy-start(s32[5]{0:T(128)} %copy-done.12) | copy-start | bytes 64
  39.5 8.7 %copy-start.14 = (bf16[512,1024]{1,0:T(8,128)(2,1)S(1)}, bf16[512,1024]{1,0:T(8,128)(2,1)}, u32[]{:S(2)}) copy-start(bf16[512,1024]{1,0:T(8,128)(2,1)} %weight_ref.1) | copy-start | bytes 3145732
  48.3 1.0 %copy-start.6 = (bf16[384,512]{1,0:T(8,128)(2,1)S(1)}, bf16[384,512]{1,0:T(8,128)(2,1)}, u32[]{:S(2)}) copy-start(bf16[384,512]{1,0:T(8,128)(2,1)} %get-tuple-element.66.attended_ref.out_ref) | copy-start | bytes 1179652
  52.2 0.7 copy-start.7
  52.9 5.0 %collective-permute-start.7 = (bf16[2,256,512]{2,1,0:T(8,128)(2,1)S(1)}, bf16[2,256,512]{2,1,0:T(8,128)(2,1)S(1)}, u32[]{:S(2)}, u32[]{:S(2)}) collective-permute-start(bf16[2,256,512]{2,1,0:T(8,128)(2,1)S(1)} %get-tuple-element.71), channel_id=1, source_target_pairs={{0,64},{64,0},{128,192},{192,128},{1,65},{65,1},{129,193},{193,129... | collective-permute-start | bytes 1572872 | tf_op jit(solution)/shard_map/ppermute | solution.py:61
  60.0 14.0 %all-to-all-start.1 = ((bf16[8,64,512]{2,1,0:T(8,128)(2,1)}), bf16[8,64,512]{2,1,0:T(8,128)(2,1)S(1)}, u32[]{:S(2)}, u32[]{:S(2)}) async-start(bf16[8,64,512]{2,1,0:T(8,128)(2,1)} %add.7), calls=%async_computation.1 | async-start | bytes 1048576 | tf_op jit(solution)/shard_map/all_to_all | solution.py:381
  69.6 17.2 %collective-permute-start.8 = (bf16[256,1024]{1,0:T(8,128)(2,1)}, bf16[256,1024]{1,0:T(8,128)(2,1)S(1)}, u32[]{:S(2)}, u32[]{:S(2)}) collective-permute-start(bf16[256,1024]{1,0:T(8,128)(2,1)} %get-tuple-element.85), channel_id=1, source_target_pairs={{0,2},{2,4},{4,6},{6,8},{8,10},{10,12},{12,14},{14,16},{16,18},{18... | collective-permute-start | bytes 1572872 | tf_op jit(solution)/shard_map/ppermute | solution.py:56
  71.1 15.7 %collective-permute-start.9 = (bf16[256,1024]{1,0:T(8,128)(2,1)}, bf16[256,1024]{1,0:T(8,128)(2,1)S(1)}, u32[]{:S(2)}, u32[]{:S(2)}) collective-permute-start(bf16[256,1024]{1,0:T(8,128)(2,1)} %get-tuple-element.86), channel_id=1, source_target_pairs={{0,62},{2,0},{4,2},{6,4},{8,6},{10,8},{12,10},{14,12},{16,14},{18,... | collective-permute-start | bytes 1572872 | tf_op jit(solution)/shard_map/ppermute | solution.py:56
  74.0 12.8 %copy-start.9 = (f32[384,512]{1,0:T(8,128)S(1)}, f32[384,512]{1,0:T(8,128)}, u32[]{:S(2)}) copy-start(f32[384,512]{1,0:T(8,128)} %get-tuple-element.83.dk_ref) | copy-start | bytes 2359300
  74.0 12.8 %copy-start.10 = (f32[384,512]{1,0:T(8,128)S(1)}, f32[384,512]{1,0:T(8,128)}, u32[]{:S(2)}) copy-start(f32[384,512]{1,0:T(8,128)} %get-tuple-element.84.dv_ref) | copy-start | bytes 2359300
  74.8 20.1 %all-to-all-start.2 = ((bf16[8,8,2048]{2,1,0:T(8,128)(2,1)}), bf16[8,8,2048]{2,1,0:T(8,128)(2,1)S(1)}, u32[]{:S(2)}, u32[]{:S(2)}) async-start(bf16[8,8,2048]{2,1,0:T(8,128)(2,1)} %bitcast.13), calls=%async_computation.2 | async-start | bytes 524288 | tf_op jit(solution)/shard_map/all_to_all | solution.py:381
